TPU v7x, 32 devices: a whole 2x2x4 slice. The times are simulated.
32 devices in a mesh: dp: 2 (over x), space: 16 (over z, y, core).
Axes of the slice: x: 2, y: 2, z: 4, core: 2. Of those that a mesh axis runs over, the one named last changes fastest.
Arguments:
- images: bfloat16 [2, 16, 96, 64, 128], P('dp', 'space'), may hold values from -60 to 60
- first_weight: bfloat16 [3, 3, 128, 256], replicated, may hold values from -0.1875 to 0.1875
- norm_gain: float32 [256], replicated, may hold values from 0.5 to 2
- norm_bias: float32 [256], replicated, may hold values from -2 to 2
- second_weight: bfloat16 [3, 3, 256, 256], replicated, may hold values from -0.125 to 0.125
- upstream: bfloat16 [2, 16, 48, 32, 256], P('dp', 'space'), may hold values from -45 to 45
Outputs:
- input_grad: bfloat16 [2, 16, 96, 64, 128], P('dp', 'space')
- first_grad: float32 [3, 3, 128, 256], replicated
- second_grad: float32 [3, 3, 256, 256], replicated
- gain_grad: float32 [256], replicated
- bias_grad: float32 [256], replicated
All inputs are finite; a program needn't handle non-finite values.
Results may differ from a plain program's by a relative error of at most 0.0049.
Values may be sent and summed in bfloat16 or wider, within the bound.
No kernel may reach another device: no remote copies, remote signals or barrier semaphores. Data moves between devices by JAX's collectives and lax.ppermute only.
A program may use at most 64 MiB of HBM per device.

v0:
```python
import functools

import jax
import jax.numpy as jnp
from jax import lax
from jax.experimental import pallas as pl
from jax.experimental.pallas import tpu as pltpu
from jax.sharding import PartitionSpec as P

GROUPS = 32
TCOLS = 4
F32 = jnp.float32
BF16 = jnp.bfloat16
MIB = 1024 * 1024
CHUNK = 256


def call(kernel, outs, args, scratch=(), flops=0, aliases=None, limit=40, smem=0):
    specs = [pl.BlockSpec(memory_space=pltpu.SMEM)] * smem
    specs += [pl.BlockSpec(memory_space=pltpu.VMEM)] * (len(args) - smem)
    moved = sum(a.size * a.dtype.itemsize for a in list(args) + list(outs))
    return pl.pallas_call(
        kernel,
        out_shape=list(outs),
        in_specs=specs,
        out_specs=[pl.BlockSpec(memory_space=pltpu.VMEM)] * len(outs),
        scratch_shapes=list(scratch),
        input_output_aliases=aliases or {},
        compiler_params=pltpu.CompilerParams(vmem_limit_bytes=limit * MIB),
        cost_estimate=pl.CostEstimate(flops=flops, bytes_accessed=moved, transcendentals=0),
    )(*args)


def shape(dims, dtype):
    return jax.ShapeDtypeStruct(tuple(dims), dtype)


def dot(a, b):
    return lax.dot_general(a, b, (((1,), (0,)), ((), ())), preferred_element_type=F32)


def tree_sum(values):
    while len(values) > 1:
        values = [
            values[i] + values[i + 1] if i + 1 < len(values) else values[i]
            for i in range(0, len(values), 2)
        ]
    return values[0]


def planes_kernel(rows, cols, x_ref, w_ref, planes_ref, z_ref, wide):
    cin = x_ref.shape[2]
    planes_ref[0:cols, :] = jnp.zeros((cols, 6 * cin), BF16)
    step = CHUNK // cols
    wide[:, 0:8, :] = jnp.zeros((2 * step, 8, cin), F32)

    def deinterleave(i, carry):
        base = pl.multiple_of(i * 2 * step, 2 * step)
        wide[:, 8 : 8 + 2 * cols, :] = x_ref[pl.ds(base, 2 * step)].astype(F32)
        row = pl.multiple_of((i * step + 1) * cols, cols)
        for parity in range(2):
            for slot, first in enumerate((7, 8, 9)):
                part = wide[pl.ds(parity, step, stride=2), pl.ds(first, cols, stride=2), :]
                lane = (parity * 3 + slot) * cin
                planes_ref[pl.ds(row, CHUNK), lane : lane + cin] = part.reshape(CHUNK, cin).astype(BF16)
        return carry

    lax.fori_loop(0, rows // step, deinterleave, 0)

    def convolve(i, carry):
        row = pl.multiple_of(i * CHUNK, CHUNK)
        above = planes_ref[pl.ds(row, CHUNK), 3 * cin :]
        here = planes_ref[pl.ds(pl.multiple_of(row + cols, cols), CHUNK), :]
        z_ref[pl.ds(row, CHUNK), :] = dot(above, w_ref[0 : 3 * cin]) + dot(here, w_ref[3 * cin :])
        return carry

    lax.fori_loop(0, rows * cols // CHUNK, convolve, 0)


def edge_parts(cols, xcol_ref, xrow_ref, corner_ref, col_pad, row_pad):
    rows = xcol_ref.shape[0] // 2
    col_pad[0:8, :] = jnp.broadcast_to(corner_ref[0:1, :].astype(F32), (8, corner_ref.shape[1]))
    col_pad[8 : 8 + 2 * rows, :] = xcol_ref[...].astype(F32)
    row_pad[0:8, :] = jnp.zeros((8, xrow_ref.shape[1]), F32)
    row_pad[8 : 8 + 2 * cols, :] = xrow_ref[...].astype(F32)
    left = [col_pad[pl.ds(first, rows, stride=2), :] for first in (7, 8, 9)]
    over = [row_pad[pl.ds(first, cols, stride=2), :] for first in (7, 8, 9)]
    return left, over


def edges_kernel(rows, cols, z_in, xcol_ref, xrow_ref, corner_ref, w_ref, z_ref, stats_ref, col_pad, row_pad, rim):
    cin = xrow_ref.shape[1]
    left, over = edge_parts(cols, xcol_ref, xrow_ref, corner_ref, col_pad, row_pad)
    z_ref[...] = z_in[...]
    from_above = dot(jnp.concatenate(over, 1).astype(BF16), w_ref[0 : 3 * cin])
    from_left = (
        dot(left[0].astype(BF16), w_ref[0:cin])
        + dot(left[1].astype(BF16), w_ref[3 * cin : 4 * cin])
        + dot(left[2].astype(BF16), w_ref[6 * cin : 7 * cin])
    )
    z_ref[0:cols, :] = z_ref[0:cols, :] + from_above
    rim[...] = from_left
    for p in range(rows):
        z_ref[p * cols : p * cols + 1, :] = z_ref[p * cols : p * cols + 1, :] + rim[p : p + 1, :]
    z = z_ref[...]
    stats_ref[0:1, :] = jnp.sum(z, axis=0, keepdims=True)
    stats_ref[1:2, :] = jnp.sum(z * z, axis=0, keepdims=True)


def windows_kernel(rows, cols, planes_ref, xcol_ref, xrow_ref, corner_ref, t_ref, col_pad, row_pad, wide):
    cin = xrow_ref.shape[1]
    cells = rows * cols
    left, over = edge_parts(cols, xcol_ref, xrow_ref, corner_ref, col_pad, row_pad)
    for half, parts in ((0, left[1]), (3, left[2])):
        wide[...] = planes_ref[cols:, half * cin : (half + 1) * cin].astype(F32)
        wide[pl.ds(0, rows, stride=cols), :] = parts
        window = wide[...].astype(BF16)
        t_ref[(half + 3) * cin : (half + 4) * cin, :] = window.T
    wide[cols:, :] = planes_ref[cols:cells, 3 * cin : 4 * cin].astype(F32)
    wide[0:cols, :] = over[0]
    wide[pl.ds(0, rows, stride=cols), :] = left[0]
    t_ref[0:cin, :] = wide[...].astype(BF16).T
    for slot in (1, 2):
        lane = (3 + slot) * cin
        below = planes_ref[cols:cells, lane : lane + cin]
        window = jnp.concatenate([over[slot].astype(BF16), below], 0)
        t_ref[slot * cin : (slot + 1) * cin, :] = window.T
    for slot in (1, 2, 4, 5):
        lane = slot * cin
        t_ref[lane + 3 * cin : lane + 4 * cin, :] = planes_ref[cols:, lane : lane + cin].T


def upstream_kernel(rows, cols, g_ref, left_ref, right_ref, above_ref, below_ref, w_ref, taps_ref, act_grad_ref, wide, w_t, rims):
    pitch = cols + 16
    depth = g_ref.shape[1]
    for p in range(rows):
        wide[(p + 1) * pitch + 8 : (p + 1) * pitch + 8 + cols, :] = g_ref[p * cols : (p + 1) * cols, :].astype(F32)
    rims[0] = left_ref[...].astype(F32)
    rims[1] = right_ref[...].astype(F32)
    for p in range(rows):
        first = (p + 1) * pitch + 7
        wide[first : first + 1, :] = rims[0, p : p + 1, :]
        wide[first + 1 + cols : first + 2 + cols, :] = rims[1, p : p + 1, :]
    wide[7 : 9 + cols, :] = above_ref[...].astype(F32)
    last = (rows + 1) * pitch
    wide[last + 7 : last + 9 + cols, :] = below_ref[...].astype(F32)
    for r in range(rows + 2):
        for b in range(3):
            first = r * pitch + 9 - b
            taps_ref[b, r * cols : (r + 1) * cols, :] = wide[first : first + cols, :].astype(BF16)
    for tap in range(9):
        w_t[tap * depth : (tap + 1) * depth, :] = w_ref[tap * depth : (tap + 1) * depth, :].T

    def convolve(i, carry):
        row = pl.multiple_of(i * CHUNK, CHUNK)
        parts = []
        for a in range(3):
            for b in range(3):
                parts.append(taps_ref[b, pl.ds(pl.multiple_of(row + (2 - a) * cols, cols), CHUNK), :])
        act_grad_ref[pl.ds(row, CHUNK), :] = dot(jnp.concatenate(parts, 1), w_t[...])
        return carry

    lax.fori_loop(0, rows * cols // CHUNK, convolve, 0)


def group_sum(value, depth):
    size = depth // GROUPS
    one = lax.broadcasted_iota(jnp.int32, (depth, depth), 0) // size
    two = lax.broadcasted_iota(jnp.int32, (depth, depth), 1) // size
    same = jnp.where(one == two, 1.0, 0.0).astype(F32)
    return lax.dot_general(
        value, same, (((1,), (0,)), ((), ())), precision=lax.Precision.HIGHEST, preferred_element_type=F32
    )


def activate_kernel(count, norm_count, *refs):
    stats = refs[:count]
    z_ref, act_grad_ref, gain_ref, bias_ref, act_ref, pre_ref, sums_ref, moments_ref = refs[count:]
    cells, depth = z_ref.shape
    total = group_sum(tree_sum([s[...] for s in stats]), depth) / norm_count
    mean = total[0:1, :]
    inv_std = 1.0 / jnp.sqrt(total[1:2, :] - mean * mean + 1e-05)
    moments_ref[0:1, :] = mean
    moments_ref[1:2, :] = inv_std
    gain = gain_ref[...]
    bias = bias_ref[...]

    def chunk(i, carry):
        row = pl.multiple_of(i * 64, 64)
        normed = (z_ref[pl.ds(row, 64), :] - mean) * inv_std
        shifted = normed * gain + bias
        sig = 1.0 / (1.0 + jnp.exp(-shifted))
        act_ref[pl.ds(row, 64), :] = (shifted * sig).astype(BF16)
        pre = act_grad_ref[pl.ds(row, 64), :] * sig * (1.0 + shifted * (1.0 - sig))
        pre_ref[pl.ds(row, 64), :] = pre
        one = jnp.sum(pre.reshape(8, 8, depth), axis=0)
        two = jnp.sum((pre * normed).reshape(8, 8, depth), axis=0)
        return carry[0] + one, carry[1] + two

    zero = jnp.zeros((8, depth), F32)
    one, two = lax.fori_loop(0, cells // 64, chunk, (zero, zero))
    sums_ref[0:1, :] = jnp.sum(one, axis=0, keepdims=True)
    sums_ref[1:2, :] = jnp.sum(two, axis=0, keepdims=True)


def second_kernel(rows, cols, me_ref, act_ref, taps_ref, out_ref, whole):
    cells = rows * cols
    depth = act_ref.shape[1]
    act_t = act_ref[...].T
    for a in range(3):
        for b in range(3):
            first = (2 - a) * cols
            tap = a * 3 + b
            whole[tap * depth : (tap + 1) * depth, :] = dot(act_t, taps_ref[b, first : first + cells, :])
    spread(me_ref, whole, out_ref)


def spread(me_ref, whole, out_ref):
    size = out_ref.shape[1]
    for slot in range(8):
        first = pl.multiple_of((me_ref[0] ^ slot) * size, 16)
        out_ref[slot] = whole[pl.ds(first, size), :]


def conv_grad_kernel(count, norm_count, rows, cols, me_ref, *refs):
    sums = refs[:count]
    z_ref, pre_ref, moments_ref, gain_ref, t_ref, grad_ref, col_ref, total_ref, out_ref, whole, rims = refs[count:]
    cells, depth = z_ref.shape
    total = tree_sum([s[...] for s in sums])
    total_ref[...] = total
    gain = gain_ref[...]
    means = group_sum(total * gain, depth) / norm_count
    mean = moments_ref[0:1, :]
    inv_std = moments_ref[1:2, :]
    shift = means[0:1, :]
    scale = means[1:2, :]

    def value(z, pre):
        return ((gain * pre - shift - (z - mean) * inv_std * scale) * inv_std).astype(BF16)

    def chunk(i, carry):
        row = pl.multiple_of(i * 64, 64)
        grad_ref[pl.ds(row, 64), :] = value(z_ref[pl.ds(row, 64), :], pre_ref[pl.ds(row, 64), :])
        return carry

    lax.fori_loop(0, cells // 64, chunk, 0)
    for p in range(rows):
        rims[0, p : p + 1, :] = z_ref[p * cols : p * cols + 1, :]
        rims[1, p : p + 1, :] = pre_ref[p * cols : p * cols + 1, :]
    col_ref[...] = value(rims[0], rims[1])

    def product(i, carry):
        row = pl.multiple_of(i * 128, 128)
        whole[pl.ds(row, 128), :] = dot(t_ref[pl.ds(row, 128), :], grad_ref[...])
        return carry

    lax.fori_loop(0, t_ref.shape[0] // 128, product, 0)
    spread(me_ref, whole, out_ref)


def input_kernel(rows, cols, d_ref, right_ref, below_ref, corner_ref, w_ref, out_ref, moved, w_t, wide, mixed, rim):
    cells = rows * cols
    cin = out_ref.shape[2]
    depth = d_ref.shape[1]
    plain = moved.at[0]
    shifted = moved.at[1]
    plain[0:cells, :] = d_ref[...]
    plain[cells : cells + cols, :] = below_ref[...]
    wide[0:cells, :] = d_ref[...].astype(F32)
    wide[cells : cells + cols, :] = below_ref[...].astype(F32)
    wide[cells + cols :, :] = jnp.zeros((8, depth), F32)
    right = right_ref[...].astype(F32)
    corner = corner_ref[...].astype(F32)
    shifted[...] = wide[1 : 1 + cells + cols, :].astype(BF16)
    for tap in range(9):
        w_t[tap] = w_ref[tap * cin : (tap + 1) * cin, :].T
    wide[0 : cells + cols, :] = shifted[...].astype(F32)
    rim[...] = right
    for p in range(rows):
        last = (p + 1) * cols - 1
        wide[last : last + 1, :] = rim[p : p + 1, :]
    wide[cells + cols - 1 : cells + cols, :] = corner
    shifted[...] = wide[0 : cells + cols, :].astype(BF16)
    step = CHUNK // cols

    def chunk(i, carry):
        row = pl.multiple_of(i * CHUNK, CHUNK)
        under = pl.multiple_of(row + cols, cols)
        d = plain[pl.ds(row, CHUNK), :]
        dc = shifted[pl.ds(row, CHUNK), :]
        dr = plain[pl.ds(under, CHUNK), :]
        drc = shifted[pl.ds(under, CHUNK), :]
        even_even = dot(d, w_t[4])
        even_odd = dot(d, w_t[5]) + dot(dc, w_t[3])
        odd_even = dot(d, w_t[7]) + dot(dr, w_t[1])
        odd_odd = dot(d, w_t[8]) + dot(dc, w_t[6]) + dot(dr, w_t[2]) + dot(drc, w_t[0])
        for parity, pair in enumerate(((even_even, even_odd), (odd_even, odd_odd))):
            for side in range(2):
                mixed[pl.ds(parity, step, stride=2), pl.ds(side, cols, stride=2), :] = pair[side].reshape(
                    step, cols, cin
                )
        out_ref[pl.ds(pl.multiple_of(i * 2 * step, 2 * step), 2 * step)] = mixed[...].astype(BF16)
        return carry

    lax.fori_loop(0, rows // step, chunk, 0)


def gather_kernel(me_ref, *refs):
    me = me_ref[0]
    count = len(refs) // 6
    for g in range(count):
        own = refs[g * 5 : g * 5 + 4]
        other = refs[g * 5 + 4]
        out_ref = refs[count * 5 + g]
        for slot in range(4):
            out_ref[me ^ slot] = own[slot][...].astype(F32)
            out_ref[me ^ slot ^ 4] = other[slot].astype(F32)


def on_device(dp_size, tiles, images, first_weight, norm_gain, norm_bias, second_weight, upstream):
    rows, cols, depth = upstream.shape[2:]
    cin = images.shape[4]
    cells = rows * cols
    group_size = depth // GROUPS
    norm_count = float(cells * tiles * group_size)
    tile_rows = tiles // TCOLS
    axes = ("dp", "space")
    devices = dp_size * tiles

    def flip(value, mask):
        return lax.ppermute(value, axes, [(i, i ^ mask) for i in range(devices)])

    def moved(value, down, right):
        pairs = []
        for t in range(tiles):
            place = (t + TCOLS + 2) % tiles
            r, c = place // TCOLS + down, place % TCOLS + right
            if 0 <= r < tile_rows and 0 <= c < TCOLS:
                pairs.append((t, (r * TCOLS + c - TCOLS - 2) % tiles))
        return lax.ppermute(value, "space", pairs)

    def all_sums(value):
        value = value + flip(value, 1)
        value = value + flip(value, 2)
        return [value] + [flip(value, 4 * k) for k in range(1, tiles // 4)]

    def summed(parts):
        return tree_sum([p.astype(F32) for p in parts])

    masks = [0, 2, tiles, tiles + 2]

    def scattered(slots):
        half = slots[0:4] + flip(slots[4:8], 1)
        sent = half[1:4].astype(BF16)
        shard = summed([half[0]] + [flip(sent[k - 1], masks[k]) for k in (1, 2, 3)]).astype(BF16)
        if dp_size > 2:
            shard = summed([shard] + [flip(shard, 2 * tiles * k) for k in range(1, dp_size // 2)]).astype(BF16)
        return summed([shard] + [flip(shard, 4 * k) for k in range(1, tiles // 4)]).astype(BF16)

    def gathered(shard):
        own = [shard] + [flip(shard, masks[k]) for k in (1, 2, 3)]
        return own + [flip(jnp.stack(own), 1)]

    space = lax.axis_index("space")
    me = (space % 2) * 4 + (lax.axis_index("dp") % 2) * 2 + (space // 2) % 2
    me = me.astype(jnp.int32).reshape(1)
    x = images[0, 0]
    w1 = first_weight.reshape(9 * cin, depth)
    w2 = second_weight.reshape(9 * depth, depth)
    gain = norm_gain.reshape(1, depth)
    bias = norm_bias.reshape(1, depth)
    xcol = moved(x[:, -1, :], 0, 1)
    xrow = moved(x[-1], 1, 0)
    corner = moved(x[-1, -1:], 1, 1)

    g3 = upstream[0, 0]
    gleft = moved(g3[:, -1, :], 0, 1)
    gright = moved(g3[:, 0, :], 0, -1)
    gabove = moved(jnp.concatenate([gleft[-1:], g3[-1], gright[-1:]], 0), 1, 0)
    gbelow = moved(jnp.concatenate([gleft[:1], g3[0], gright[:1]], 0), -1, 0)

    planes, z = call(
        functools.partial(planes_kernel, rows, cols),
        [shape((cells + cols, 6 * cin), BF16), shape((cells, depth), F32)],
        [x, w1],
        [pltpu.VMEM((2 * CHUNK // cols, 2 * cols + 8, cin), F32)],
        flops=2 * cells * 9 * cin * depth,
    )
    pads = [pltpu.VMEM((2 * rows + 8, cin), F32), pltpu.VMEM((2 * cols + 8, cin), F32)]
    z, stats = call(
        functools.partial(edges_kernel, rows, cols),
        [shape((cells, depth), F32), shape((2, depth), F32)],
        [z, xcol, xrow, corner, w1],
        pads + [pltpu.VMEM((rows, depth), F32)],
        flops=2 * 80 * 3 * cin * depth,
    )
    stats = all_sums(stats)
    taps, act_grad = call(
        functools.partial(upstream_kernel, rows, cols),
        [shape((3, cells + 2 * cols, depth), BF16), shape((cells, depth), F32)],
        [g3.reshape(cells, depth), gleft, gright, gabove, gbelow, w2],
        [pltpu.VMEM(((rows + 2) * (cols + 16), depth), F32), pltpu.VMEM((9 * depth, depth), BF16), pltpu.VMEM((2, rows, depth), F32)],
        flops=2 * cells * 9 * depth * depth,
    )
    (windows,) = call(
        functools.partial(windows_kernel, rows, cols),
        [shape((9 * cin, cells), BF16)],
        [planes, xcol, xrow, corner],
        pads + [pltpu.VMEM((cells, cin), F32)],
        flops=2 * cells * 9 * cin * depth,
    )
    activated, pre_grad, sums, moments = call(
        functools.partial(activate_kernel, len(stats), norm_count),
        [shape((cells, depth), BF16), shape((cells, depth), F32), shape((2, depth), F32), shape((2, depth), F32)],
        stats + [z, act_grad, gain, bias],
        flops=cells * depth * 30,
    )
    sums = all_sums(sums)
    (second_slots,) = call(
        functools.partial(second_kernel, rows, cols),
        [shape((8, 9 * depth // 8, depth), F32)],
        [me, activated, taps],
        [pltpu.VMEM((9 * depth, depth), F32)],
        flops=2 * cells * 9 * depth * depth,
        smem=1,
    )
    second_shard = scattered(second_slots)
    conv_grad, dcol, total, first_slots = call(
        functools.partial(conv_grad_kernel, len(sums), norm_count, rows, cols),
        [
            shape((cells, depth), BF16),
            shape((rows, depth), BF16),
            shape((2, depth), F32),
            shape((8, 9 * cin // 8, depth), F32),
        ],
        [me] + sums + [z, pre_grad, moments, gain, windows],
        [pltpu.VMEM((9 * cin, depth), F32), pltpu.VMEM((2, rows, depth), F32)],
        flops=2 * cells * 9 * cin * depth,
        smem=1,
    )
    first_shard = scattered(first_slots)
    dright = moved(dcol, 0, -1)
    dbelow = moved(conv_grad[:cols], -1, 0)
    dcorner = moved(conv_grad[:1], -1, -1)
    (input_grad,) = call(
        functools.partial(input_kernel, rows, cols),
        [shape((2 * rows, 2 * cols, cin), BF16)],
        [conv_grad, dright, dbelow, dcorner, w1],
        [
            pltpu.VMEM((2, cells + cols, depth), BF16),
            pltpu.VMEM((9, depth, cin), BF16),
            pltpu.VMEM((cells + cols + 8, depth), F32),
            pltpu.VMEM((2 * CHUNK // cols, 2 * cols, cin), F32),
            pltpu.VMEM((rows, depth), F32),
        ],
        flops=2 * cells * 9 * cin * depth,
    )
    for k in range(dp_size.bit_length() - 1):
        total = total + flip(total, tiles << k)
    second_grad, first_grad = call(
        gather_kernel,
        [shape((8, 9 * depth // 8, depth), F32), shape((8, 9 * cin // 8, depth), F32)],
        [me] + gathered(second_shard) + gathered(first_shard),
        smem=1,
    )
    return (
        input_grad[None, None],
        first_grad.reshape(first_weight.shape),
        second_grad.reshape(second_weight.shape),
        total[1],
        total[0],
    )


def solution(mesh):
    placed = (
        P("dp", "space", None, None, None),
        P(),
        P(),
        P(),
        P(),
        P("dp", "space", None, None, None),
    )
    return jax.shard_map(
        functools.partial(on_device, mesh.shape["dp"], mesh.shape["space"]),
        mesh=mesh,
        in_specs=placed,
        out_specs=(P("dp", "space", None, None, None), P(), P(), P(), P()),
        check_vma=False,
    )
```

profile of v0, /device:TPU:1, one launch (start us, length us, event | category | flops | bytes accessed | tf_op | source)
XLA Modules:
  0.0 128.8 jit_solution(16713538503597618651)
XLA Ops:
  1.5 4.0 %collective-permute-start.1 = (bf16[64,128]{1,0:T(8,128)(2,1)S(1)}, bf16[64,128]{1,0:T(8,128)(2,1)S(1)}, u32[]{:S(2)}, u32[]{:S(2)}) collective-permute-start(bf16[64,128]{1,0:T(8,128)(2,1)S(1)} %slice_bitcast_fusion.13), channel_id=1, source_target_pairs={{0,4},{1,5},{2,6},{3,7},{4,8},{5,9},{10,14},{11,15},{12,0},{13,1},... | collective-permute-start | bytes 49160 | tf_op jit(solution)/shard_map/ppermute | solution.py:340
  7.1 2.9 %collective-permute-start.9 = (bf16[48,256]{1,0:T(8,128)(2,1)S(1)}, bf16[48,256]{1,0:T(8,128)(2,1)S(1)}, u32[]{:S(2)}, u32[]{:S(2)}) collective-permute-start(bf16[48,256]{1,0:T(8,128)(2,1)S(1)} %get-tuple-element.43), channel_id=1, source_target_pairs={{0,15},{1,0},{3,2},{4,3},{5,4},{7,6},{8,7},{9,8},{11,10},{12,11},{... | collective-permute-start | bytes 73736 | tf_op jit(solution)/shard_map/ppermute | solution.py:340
  15.2 3.2 %collective-permute-start.10 = (bf16[34,256]{1,0:T(8,128)(2,1)S(1)}, bf16[34,256]{1,0:T(8,128)(2,1)S(1)}, u32[]{:S(2)}, u32[]{:S(2)}) collective-permute-start(bf16[34,256]{1,0:T(8,128)(2,1)S(1)} %pad_maximum_fusion.2), channel_id=1, source_target_pairs={{0,4},{1,5},{2,6},{3,7},{4,8},{5,9},{10,14},{11,15},{12,0},{13,1},... | collective-permute-start | bytes 52232 | tf_op jit(solution)/shard_map/ppermute | solution.py:340
  18.4 3.9 %collective-permute-start.11 = (bf16[34,256]{1,0:T(8,128)(2,1)S(1)}, bf16[34,256]{1,0:T(8,128)(2,1)S(1)}, u32[]{:S(2)}, u32[]{:S(2)}) collective-permute-start(bf16[34,256]{1,0:T(8,128)(2,1)S(1)} %pad_maximum_fusion.3), channel_id=1, source_target_pairs={{0,12},{1,13},{2,14},{3,15},{4,0},{5,1},{6,2},{7,3},{8,4},{9,5},{1... | collective-permute-start | bytes 52232 | tf_op jit(solution)/shard_map/ppermute | solution.py:340
  22.3 2.6 %shard_map.101 = (bf16[1568,768]{1,0:T(8,128)(2,1)S(1)}, f32[1536,256]{1,0:T(8,128)S(1)}) custom-call(bf16[96,64,128]{2,1,0:T(8,128)(2,1)S(1)} %bitcast.68, bf16[1152,256]{1,0:T(8,128)(2,1)S(1)} %bitcast.72), custom_call_target="tpu_custom_call" | custom-call | flops 905969664 | bytes 6144000 | tf_op jit(solution)/shard_map/pallas_call | solution.py:22
  26.8 5.9 %collective-permute-start.3 = (f32[2,256]{1,0:T(2,128)S(1)}, f32[2,256]{1,0:T(2,128)S(1)}, u32[]{:S(2)}, u32[]{:S(2)}) collective-permute-start(f32[2,256]{1,0:T(2,128)S(1)} %get-tuple-element.22), channel_id=1, source_target_pairs={{0,1},{1,0},{2,3},{3,2},{4,5},{5,4},{6,7},{7,6},{8,9},{9,8},{10,11... | collective-permute-start | bytes 6152 | tf_op jit(solution)/shard_map/ppermute | solution.py:331
  33.9 2.1 %collective-permute-done.4 = f32[2,256]{1,0:T(2,128)S(1)} collective-permute-done((f32[2,256]{1,0:T(2,128)S(1)}, f32[2,256]{1,0:T(2,128)S(1)}, u32[]{:S(2)}, u32[]{:S(2)}) %collective-permute-start.4) | collective-permute-done | bytes 2080 | tf_op jit(solution)/shard_map/ppermute | solution.py:331
  36.6 2.9 %collective-permute-start.5 = (f32[2,256]{1,0:T(2,128)S(1)}, f32[2,256]{1,0:T(2,128)S(1)}, u32[]{:S(2)}, u32[]{:S(2)}) collective-permute-start(f32[2,256]{1,0:T(2,128)S(1)} %add.80.refs_0_), channel_id=1, source_target_pairs={{0,4},{1,5},{2,6},{3,7},{4,0},{5,1},{6,2},{7,3},{8,12},{9,13},{10,... | collective-permute-start | bytes 6152 | tf_op jit(solution)/shard_map/ppermute | solution.py:331
  40.8 3.8 %shard_map.103 = (bf16[3,1600,256]{2,1,0:T(8,128)(2,1)S(1)}, f32[1536,256]{1,0:T(8,128)S(1)}) custom-call(bf16[1536,256]{1,0:T(8,128)(2,1)S(1)} %bitcast.70, bf16[48,256]{1,0:T(8,128)(2,1)S(1)} %collective-permute-done.8.left_ref, bf16[48,256]{1,0:T(8,128)(2,1)S(1)} %collective-permute-done.9.right_ref, ...), custom_call_target="tpu_custom_call" | custom-call | flops 1811939328 | bytes 6080512 | tf_op jit(solution)/shard_map/pallas_call | solution.py:22
  46.1 2.2 %shard_map.108 = f32[8,288,256]{2,1,0:T(8,128)S(1)} custom-call(s32[1]{0:T(128)} %bitcast.me_ref, bf16[1536,256]{1,0:T(8,128)(2,1)S(1)} %get-tuple-element.31.act_ref, bf16[3,1600,256]{2,1,0:T(8,128)(2,1)S(1)} %get-tuple-element.32.taps_ref), custom_call_target="tpu_custom_call" | custom-call | flops 1811939328 | bytes 5603332 | tf_op jit(solution)/shard_map/pallas_call | solution.py:22
  48.4 2.4 %collective-permute-start.20 = (f32[4,288,256]{2,1,0:T(8,128)S(1)}, f32[4,288,256]{2,1,0:T(8,128)S(1)}, u32[]{:S(2)}, u32[]{:S(2)}) collective-permute-start(f32[4,288,256]{2,1,0:T(8,128)S(1)} %slice.130), channel_id=1, source_target_pairs={{0,1},{1,0},{2,3},{3,2},{4,5},{5,4},{6,7},{7,6},{8,9},{9,8},{10,11... | collective-permute-start | bytes 3538952 | tf_op jit(solution)/shard_map/ppermute | solution.py:331
  50.9 2.4 %collective-permute-done.12 = f32[2,256]{1,0:T(2,128)S(1)} collective-permute-done((f32[2,256]{1,0:T(2,128)S(1)}, f32[2,256]{1,0:T(2,128)S(1)}, u32[]{:S(2)}, u32[]{:S(2)}) %collective-permute-start.12) | collective-permute-done | bytes 2080 | tf_op jit(solution)/shard_map/ppermute | solution.py:331
  53.6 2.1 %collective-permute-done.13 = f32[2,256]{1,0:T(2,128)S(1)} collective-permute-done((f32[2,256]{1,0:T(2,128)S(1)}, f32[2,256]{1,0:T(2,128)S(1)}, u32[]{:S(2)}, u32[]{:S(2)}) %collective-permute-start.13) | collective-permute-done | bytes 2080 | tf_op jit(solution)/shard_map/ppermute | solution.py:331
  56.6 2.6 %collective-permute-start.14 = (f32[2,256]{1,0:T(2,128)S(1)}, f32[2,256]{1,0:T(2,128)S(1)}, u32[]{:S(2)}, u32[]{:S(2)}) collective-permute-start(f32[2,256]{1,0:T(2,128)S(1)} %add.82.refs_0_), channel_id=1, source_target_pairs={{0,4},{1,5},{2,6},{3,7},{4,0},{5,1},{6,2},{7,3},{8,12},{9,13},{10,... | collective-permute-start | bytes 6152 | tf_op jit(solution)/shard_map/ppermute | solution.py:331
  60.4 3.4 %shard_map.106 = (bf16[1536,256]{1,0:T(8,128)(2,1)S(1)}, bf16[48,256]{1,0:T(8,128)(2,1)S(1)}, f32[2,256]{1,0:T(2,128)S(1)}, f32[8,144,256]{2,1,0:T(8,128)S(1)}) custom-call(s32[1]{0:T(128)} %bitcast.me_ref, f32[2,256]{1,0:T(2,128)S(1)} %add.82.refs_0_, f32[2,256]{1,0:T(2,128)S(1)} %collective-permute-done.14.refs_1_, ...), custom_call_target="tpu_custom_call" | custom-call | flops 905969664 | bytes 8688644 | tf_op jit(solution)/shard_map/pallas_call | solution.py:22
  63.9 2.8 %collective-permute-start.31 = (f32[4,144,256]{2,1,0:T(8,128)S(1)}, f32[4,144,256]{2,1,0:T(8,128)S(1)}, u32[]{:S(2)}, u32[]{:S(2)}) collective-permute-start(f32[4,144,256]{2,1,0:T(8,128)S(1)} %slice.114), channel_id=1, source_target_pairs={{0,1},{1,0},{2,3},{3,2},{4,5},{5,4},{6,7},{7,6},{8,9},{9,8},{10,11... | collective-permute-start | bytes 1769480 | tf_op jit(solution)/shard_map/ppermute | solution.py:331
  69.8 5.8 %collective-permute-done.21 = bf16[288,256]{1,0:T(8,128)(2,1)S(1)} collective-permute-done((bf16[288,256]{1,0:T(8,128)(2,1)S(1)}, bf16[288,256]{1,0:T(8,128)(2,1)S(1)}, u32[]{:S(2)}, u32[]{:S(2)}) %collective-permute-start.21) | collective-permute-done | bytes 147488 | tf_op jit(solution)/shard_map/ppermute | solution.py:331
  76.6 2.1 %collective-permute-start.26 = (bf16[288,256]{1,0:T(8,128)(2,1)S(1)}, bf16[288,256]{1,0:T(8,128)(2,1)S(1)}, u32[]{:S(2)}, u32[]{:S(2)}) collective-permute-start(bf16[288,256]{1,0:T(8,128)(2,1)S(1)} %fusion.2), channel_id=1, source_target_pairs={{0,12},{1,13},{2,14},{3,15},{4,8},{5,9},{6,10},{7,11},{8,4},{9,5},... | collective-permute-start | bytes 442376 | tf_op jit(solution)/shard_map/ppermute | solution.py:331
  83.9 9.1 %collective-permute-done.25 = bf16[288,256]{1,0:T(8,128)(2,1)S(1)} collective-permute-done((bf16[288,256]{1,0:T(8,128)(2,1)S(1)}, bf16[288,256]{1,0:T(8,128)(2,1)S(1)}, u32[]{:S(2)}, u32[]{:S(2)}) %collective-permute-start.25) | collective-permute-done | bytes 147488 | tf_op jit(solution)/shard_map/ppermute | solution.py:331
  96.3 2.2 %collective-permute-done.29.refs_3_ = bf16[288,256]{1,0:T(8,128)(2,1)S(1)} collective-permute-done((bf16[288,256]{1,0:T(8,128)(2,1)S(1)}, bf16[288,256]{1,0:T(8,128)(2,1)S(1)}, u32[]{:S(2)}, u32[]{:S(2)}) %collective-permute-start.29) | collective-permute-done | bytes 147488 | tf_op jit(solution)/shard_map/ppermute | solution.py:331
  100.2 2.4 %collective-permute-done.27.refs_1_ = bf16[288,256]{1,0:T(8,128)(2,1)S(1)} collective-permute-done((bf16[288,256]{1,0:T(8,128)(2,1)S(1)}, bf16[288,256]{1,0:T(8,128)(2,1)S(1)}, u32[]{:S(2)}, u32[]{:S(2)}) %collective-permute-start.27) | collective-permute-done | bytes 147488 | tf_op jit(solution)/shard_map/ppermute | solution.py:331
  103.7 2.6 %collective-permute-start.40 = (bf16[144,256]{1,0:T(8,128)(2,1)S(1)}, bf16[144,256]{1,0:T(8,128)(2,1)S(1)}, u32[]{:S(2)}, u32[]{:S(2)}) collective-permute-start(bf16[144,256]{1,0:T(8,128)(2,1)S(1)} %add_convert_fusion.1.refs_5_), channel_id=1, source_target_pairs={{0,18},{1,19},{2,16},{3,17},{4,22},{5,23},{6,20},{7,21},{8,26},{9,... | collective-permute-start | bytes 221192 | tf_op jit(solution)/shard_map/ppermute | solution.py:331
  109.5 6.8 %collective-permute-start.19 = (bf16[1,256]{1,0:T(2,128)(2,1)S(1)}, bf16[1,256]{1,0:T(2,128)(2,1)S(1)}, u32[]{:S(2)}, u32[]{:S(2)}) collective-permute-start(bf16[1,256]{1,0:T(2,128)(2,1)S(1)} %slice.106), channel_id=1, source_target_pairs={{0,11},{1,12},{3,14},{4,15},{5,0},{7,2},{8,3},{9,4},{15,10},{16,27... | collective-permute-start | bytes 1544 | tf_op jit(solution)/shard_map/ppermute | solution.py:340
  121.9 4.9 %shard_map.107 = bf16[96,64,128]{2,1,0:T(8,128)(2,1)} custom-call(bf16[1536,256]{1,0:T(8,128)(2,1)S(1)} %get-tuple-element.29.d_ref, bf16[48,256]{1,0:T(8,128)(2,1)S(1)} %collective-permute-done.17.right_ref, bf16[32,256]{1,0:T(8,128)(2,1)S(1)} %collective-permute-done.18.below_ref, bf16[1,256]{1,0:T(2,128)(2,1)S(1)} %collective-permute-done.19.corner_ref, ...), custom_call_target="tpu_custom_call" | custom-call | flops 905969664 | bytes 2990592 | tf_op jit(solution)/shard_map/pallas_call | solution.py:22
  (118 shorter events, 42.4 us)
Async XLA Ops:
  1.5 24.9 %collective-permute-start.1 = (bf16[64,128]{1,0:T(8,128)(2,1)S(1)}, bf16[64,128]{1,0:T(8,128)(2,1)S(1)}, u32[]{:S(2)}, u32[]{:S(2)}) collective-permute-start(bf16[64,128]{1,0:T(8,128)(2,1)S(1)} %slice_bitcast_fusion.13), channel_id=1, source_target_pairs={{0,4},{1,5},{2,6},{3,7},{4,8},{5,9},{10,14},{11,15},{12,0},{13,1},... | collective-permute-start | bytes 49160 | tf_op jit(solution)/shard_map/ppermute | solution.py:340
  7.1 8.0 %collective-permute-start.9 = (bf16[48,256]{1,0:T(8,128)(2,1)S(1)}, bf16[48,256]{1,0:T(8,128)(2,1)S(1)}, u32[]{:S(2)}, u32[]{:S(2)}) collective-permute-start(bf16[48,256]{1,0:T(8,128)(2,1)S(1)} %get-tuple-element.43), channel_id=1, source_target_pairs={{0,15},{1,0},{3,2},{4,3},{5,4},{7,6},{8,7},{9,8},{11,10},{12,11},{... | collective-permute-start | bytes 73736 | tf_op jit(solution)/shard_map/ppermute | solution.py:340
  12.5 13.9 %collective-permute-start.2 = (bf16[1,128]{1,0:T(2,128)(2,1)S(1)}, bf16[1,128]{1,0:T(2,128)(2,1)S(1)}, u32[]{:S(2)}, u32[]{:S(2)}) collective-permute-start(bf16[1,128]{1,0:T(2,128)(2,1)S(1)} %slice_bitcast_fusion.14), channel_id=1, source_target_pairs={{0,5},{2,7},{3,8},{4,9},{10,15},{11,0},{12,1},{14,3},{15,4},{16,21... | collective-permute-start | bytes 776 | tf_op jit(solution)/shard_map/ppermute | solution.py:340
  13.8 12.6 %collective-permute-start = (bf16[96,128]{1,0:T(8,128)(2,1)S(1)}, bf16[96,128]{1,0:T(8,128)(2,1)S(1)}, u32[]{:S(2)}, u32[]{:S(2)}) collective-permute-start(bf16[96,128]{1,0:T(8,128)(2,1)S(1)} %slice_bitcast_fusion.10), channel_id=1, source_target_pairs={{0,1},{2,3},{3,4},{4,5},{6,7},{7,8},{8,9},{10,11},{11,12},{12,13},... | collective-permute-start | bytes 73736 | tf_op jit(solution)/shard_map/ppermute | solution.py:340
  15.2 24.4 %collective-permute-start.10 = (bf16[34,256]{1,0:T(8,128)(2,1)S(1)}, bf16[34,256]{1,0:T(8,128)(2,1)S(1)}, u32[]{:S(2)}, u32[]{:S(2)}) collective-permute-start(bf16[34,256]{1,0:T(8,128)(2,1)S(1)} %pad_maximum_fusion.2), channel_id=1, source_target_pairs={{0,4},{1,5},{2,6},{3,7},{4,8},{5,9},{10,14},{11,15},{12,0},{13,1},... | collective-permute-start | bytes 52232 | tf_op jit(solution)/shard_map/ppermute | solution.py:340
  18.4 21.1 %collective-permute-start.11 = (bf16[34,256]{1,0:T(8,128)(2,1)S(1)}, bf16[34,256]{1,0:T(8,128)(2,1)S(1)}, u32[]{:S(2)}, u32[]{:S(2)}) collective-permute-start(bf16[34,256]{1,0:T(8,128)(2,1)S(1)} %pad_maximum_fusion.3), channel_id=1, source_target_pairs={{0,12},{1,13},{2,14},{3,15},{4,0},{5,1},{6,2},{7,3},{8,4},{9,5},{1... | collective-permute-start | bytes 52232 | tf_op jit(solution)/shard_map/ppermute | solution.py:340
  36.0 8.6 %collective-permute-start.7 = (f32[2,256]{1,0:T(2,128)S(1)}, f32[2,256]{1,0:T(2,128)S(1)}, u32[]{:S(2)}, u32[]{:S(2)}) collective-permute-start(f32[2,256]{1,0:T(2,128)S(1)} %add.80.refs_0_), channel_id=1, source_target_pairs={{0,12},{1,13},{2,14},{3,15},{4,8},{5,9},{6,10},{7,11},{8,4},{9,5},... | collective-permute-start | bytes 6152 | tf_op jit(solution)/shard_map/ppermute | solution.py:331
  36.6 8.0 %collective-permute-start.6 = (f32[2,256]{1,0:T(2,128)S(1)}, f32[2,256]{1,0:T(2,128)S(1)}, u32[]{:S(2)}, u32[]{:S(2)}) collective-permute-start(f32[2,256]{1,0:T(2,128)S(1)} %add.80.refs_0_), channel_id=1, source_target_pairs={{0,8},{1,9},{2,10},{3,11},{4,12},{5,13},{6,14},{7,15},{8,0},{9,1},... | collective-permute-start | bytes 6152 | tf_op jit(solution)/shard_map/ppermute | solution.py:331
  36.6 8.0 %collective-permute-start.5 = (f32[2,256]{1,0:T(2,128)S(1)}, f32[2,256]{1,0:T(2,128)S(1)}, u32[]{:S(2)}, u32[]{:S(2)}) collective-permute-start(f32[2,256]{1,0:T(2,128)S(1)} %add.80.refs_0_), channel_id=1, source_target_pairs={{0,4},{1,5},{2,6},{3,7},{4,0},{5,1},{6,2},{7,3},{8,12},{9,13},{10,... | collective-permute-start | bytes 6152 | tf_op jit(solution)/shard_map/ppermute | solution.py:331
  48.4 18.3 %collective-permute-start.20 = (f32[4,288,256]{2,1,0:T(8,128)S(1)}, f32[4,288,256]{2,1,0:T(8,128)S(1)}, u32[]{:S(2)}, u32[]{:S(2)}) collective-permute-start(f32[4,288,256]{2,1,0:T(8,128)S(1)} %slice.130), channel_id=1, source_target_pairs={{0,1},{1,0},{2,3},{3,2},{4,5},{5,4},{6,7},{7,6},{8,9},{9,8},{10,11... | collective-permute-start | bytes 3538952 | tf_op jit(solution)/shard_map/ppermute | solution.py:331
  67.0 8.7 %collective-permute-start.21 = (bf16[288,256]{1,0:T(8,128)(2,1)S(1)}, bf16[288,256]{1,0:T(8,128)(2,1)S(1)}, u32[]{:S(2)}, u32[]{:S(2)}) collective-permute-start(bf16[288,256]{1,0:T(8,128)(2,1)S(1)} %get-tuple-element.45), channel_id=1, source_target_pairs={{0,2},{1,3},{2,0},{3,1},{4,6},{5,7},{6,4},{7,5},{8,10},{9,11},{10,... | collective-permute-start | bytes 442376 | tf_op jit(solution)/shard_map/ppermute | solution.py:331
  68.0 7.7 %collective-permute-start.23 = (bf16[288,256]{1,0:T(8,128)(2,1)S(1)}, bf16[288,256]{1,0:T(8,128)(2,1)S(1)}, u32[]{:S(2)}, u32[]{:S(2)}) collective-permute-start(bf16[288,256]{1,0:T(8,128)(2,1)S(1)} %get-tuple-element.46), channel_id=1, source_target_pairs={{0,18},{1,19},{2,16},{3,17},{4,22},{5,23},{6,20},{7,21},{8,26},{9,... | collective-permute-start | bytes 442376 | tf_op jit(solution)/shard_map/ppermute | solution.py:331
  78.8 14.2 %collective-permute-start.25 = (bf16[288,256]{1,0:T(8,128)(2,1)S(1)}, bf16[288,256]{1,0:T(8,128)(2,1)S(1)}, u32[]{:S(2)}, u32[]{:S(2)}) collective-permute-start(bf16[288,256]{1,0:T(8,128)(2,1)S(1)} %fusion.2), channel_id=1, source_target_pairs={{0,8},{1,9},{2,10},{3,11},{4,12},{5,13},{6,14},{7,15},{8,0},{9,1},... | collective-permute-start | bytes 442376 | tf_op jit(solution)/shard_map/ppermute | solution.py:331
  79.6 13.4 %collective-permute-start.24 = (bf16[288,256]{1,0:T(8,128)(2,1)S(1)}, bf16[288,256]{1,0:T(8,128)(2,1)S(1)}, u32[]{:S(2)}, u32[]{:S(2)}) collective-permute-start(bf16[288,256]{1,0:T(8,128)(2,1)S(1)} %fusion.2), channel_id=1, source_target_pairs={{0,4},{1,5},{2,6},{3,7},{4,0},{5,1},{6,2},{7,3},{8,12},{9,13},{10,... | collective-permute-start | bytes 442376 | tf_op jit(solution)/shard_map/ppermute | solution.py:331
  80.3 14.2 %collective-permute-start.32 = (bf16[144,256]{1,0:T(8,128)(2,1)S(1)}, bf16[144,256]{1,0:T(8,128)(2,1)S(1)}, u32[]{:S(2)}, u32[]{:S(2)}) collective-permute-start(bf16[144,256]{1,0:T(8,128)(2,1)S(1)} %get-tuple-element.48), channel_id=1, source_target_pairs={{0,2},{1,3},{2,0},{3,1},{4,6},{5,7},{6,4},{7,5},{8,10},{9,11},{10,... | collective-permute-start | bytes 221192 | tf_op jit(solution)/shard_map/ppermute | solution.py:331
  81.3 14.6 %collective-permute-start.34 = (bf16[144,256]{1,0:T(8,128)(2,1)S(1)}, bf16[144,256]{1,0:T(8,128)(2,1)S(1)}, u32[]{:S(2)}, u32[]{:S(2)}) collective-permute-start(bf16[144,256]{1,0:T(8,128)(2,1)S(1)} %get-tuple-element.49), channel_id=1, source_target_pairs={{0,18},{1,19},{2,16},{3,17},{4,22},{5,23},{6,20},{7,21},{8,26},{9,... | collective-permute-start | bytes 221192 | tf_op jit(solution)/shard_map/ppermute | solution.py:331
  82.7 13.1 %collective-permute-start.33 = (bf16[144,256]{1,0:T(8,128)(2,1)S(1)}, bf16[144,256]{1,0:T(8,128)(2,1)S(1)}, u32[]{:S(2)}, u32[]{:S(2)}) collective-permute-start(bf16[144,256]{1,0:T(8,128)(2,1)S(1)} %get-tuple-element.50), channel_id=1, source_target_pairs={{0,16},{1,17},{2,18},{3,19},{4,20},{5,21},{6,22},{7,23},{8,24},{9,... | collective-permute-start | bytes 221192 | tf_op jit(solution)/shard_map/ppermute | solution.py:331
  94.5 8.1 %collective-permute-start.27 = (bf16[288,256]{1,0:T(8,128)(2,1)S(1)}, bf16[288,256]{1,0:T(8,128)(2,1)S(1)}, u32[]{:S(2)}, u32[]{:S(2)}) collective-permute-start(bf16[288,256]{1,0:T(8,128)(2,1)S(1)} %add_convert_fusion.refs_0_), channel_id=1, source_target_pairs={{0,2},{1,3},{2,0},{3,1},{4,6},{5,7},{6,4},{7,5},{8,10},{9,11},{10,... | collective-permute-start | bytes 442376 | tf_op jit(solution)/shard_map/ppermute | solution.py:331
  95.9 7.8 %collective-permute-start.37 = (bf16[144,256]{1,0:T(8,128)(2,1)S(1)}, bf16[144,256]{1,0:T(8,128)(2,1)S(1)}, u32[]{:S(2)}, u32[]{:S(2)}) collective-permute-start(bf16[144,256]{1,0:T(8,128)(2,1)S(1)} %fusion.5), channel_id=1, source_target_pairs={{0,12},{1,13},{2,14},{3,15},{4,8},{5,9},{6,10},{7,11},{8,4},{9,5},... | collective-permute-start | bytes 221192 | tf_op jit(solution)/shard_map/ppermute | solution.py:331
  102.7 24.1 %collective-permute-start.30 = (bf16[4,288,256]{2,1,0:T(8,128)(2,1)S(1)}, bf16[4,288,256]{2,1,0:T(8,128)(2,1)S(1)}, u32[]{:S(2)}, u32[]{:S(2)}) collective-permute-start(bf16[4,288,256]{2,1,0:T(8,128)(2,1)S(1)} %pad_maximum_fusion), channel_id=1, source_target_pairs={{0,1},{1,0},{2,3},{3,2},{4,5},{5,4},{6,7},{7,6},{8,9},{9,8},{10,11... | collective-permute-start | bytes 1769480 | tf_op jit(solution)/shard_map/ppermute | solution.py:331
  103.7 12.7 %collective-permute-start.40 = (bf16[144,256]{1,0:T(8,128)(2,1)S(1)}, bf16[144,256]{1,0:T(8,128)(2,1)S(1)}, u32[]{:S(2)}, u32[]{:S(2)}) collective-permute-start(bf16[144,256]{1,0:T(8,128)(2,1)S(1)} %add_convert_fusion.1.refs_5_), channel_id=1, source_target_pairs={{0,18},{1,19},{2,16},{3,17},{4,22},{5,23},{6,20},{7,21},{8,26},{9,... | collective-permute-start | bytes 221192 | tf_op jit(solution)/shard_map/ppermute | solution.py:331
  106.3 12.0 %collective-permute-start.39 = (bf16[144,256]{1,0:T(8,128)(2,1)S(1)}, bf16[144,256]{1,0:T(8,128)(2,1)S(1)}, u32[]{:S(2)}, u32[]{:S(2)}) collective-permute-start(bf16[144,256]{1,0:T(8,128)(2,1)S(1)} %add_convert_fusion.1.refs_5_), channel_id=1, source_target_pairs={{0,16},{1,17},{2,18},{3,19},{4,20},{5,21},{6,22},{7,23},{8,24},{9,... | collective-permute-start | bytes 221192 | tf_op jit(solution)/shard_map/ppermute | solution.py:331
  106.7 13.3 %collective-permute-start.38 = (bf16[144,256]{1,0:T(8,128)(2,1)S(1)}, bf16[144,256]{1,0:T(8,128)(2,1)S(1)}, u32[]{:S(2)}, u32[]{:S(2)}) collective-permute-start(bf16[144,256]{1,0:T(8,128)(2,1)S(1)} %add_convert_fusion.1.refs_5_), channel_id=1, source_target_pairs={{0,2},{1,3},{2,0},{3,1},{4,6},{5,7},{6,4},{7,5},{8,10},{9,11},{10,... | collective-permute-start | bytes 221192 | tf_op jit(solution)/shard_map/ppermute | solution.py:331
  109.5 12.4 %collective-permute-start.19 = (bf16[1,256]{1,0:T(2,128)(2,1)S(1)}, bf16[1,256]{1,0:T(2,128)(2,1)S(1)}, u32[]{:S(2)}, u32[]{:S(2)}) collective-permute-start(bf16[1,256]{1,0:T(2,128)(2,1)S(1)} %slice.106), channel_id=1, source_target_pairs={{0,11},{1,12},{3,14},{4,15},{5,0},{7,2},{8,3},{9,4},{15,10},{16,27... | collective-permute-start | bytes 1544 | tf_op jit(solution)/shard_map/ppermute | solution.py:340
  (27 other events, 145.5 us)
where the time goes:
time: 131 us; the launch traced here: 129 us
  starting transfers between devices  67.7 us (52%)
  waiting for transfers between devices  30.4 us (23%)
  Pallas kernels  22 us (17%)
  local copies, waits for them, and re-layouts  6.92 us (5%)
    ppermute x33, starting transfers between devices, flip(): return lax.ppermute(value, axes, [(i, i ^ mask) for i in range(devices)])  39.3 us
    ppermute x33, waiting for transfers between devices, flip(): return lax.ppermute(value, axes, [(i, i ^ mask) for i in range(devices)])  30.4 us
    ppermute x10, starting transfers between devices, moved(): return lax.ppermute(value, 'space', pairs)  28.4 us
    pallas_call x9, Pallas kernels, call(): pl.pallas_call(kernel, out_shape=list(outs), in_specs=specs, out_specs=[p...  22 us
    unnamed x18, local copies, waits for them, and re-layouts  5.31 us
  transfers between devices with their start and end apart: 43, of which 11 were waited for; matrix products, arithmetic and copies ran while one was open for 3% of the time, Pallas kernels for 13%

commit v1 on v0

v1 whole, which is shorter than its diff:
```python
import functools

import jax
import jax.numpy as jnp
from jax import lax
from jax.experimental import pallas as pl
from jax.experimental.pallas import tpu as pltpu
from jax.sharding import PartitionSpec as P

GROUPS = 32
TCOLS = 4
F32 = jnp.float32
BF16 = jnp.bfloat16
MIB = 1024 * 1024
CHUNK = 256
LONG = 512


def call(kernel, outs, args, scratch=(), flops=0, limit=20, smem=0, after=(), specs=None, grid=()):
    if specs is None:
        specs = [pl.BlockSpec(memory_space=pltpu.SMEM)] * smem
        specs += [pl.BlockSpec(memory_space=pltpu.VMEM)] * (len(args) - smem)
    moved = sum(a.size * a.dtype.itemsize for a in list(args) + list(outs))
    count = len(args)

    def body(*refs):
        kernel(*refs[:count], *refs[count + len(after) :])

    return pl.pallas_call(
        body,
        out_shape=list(outs),
        grid=grid,
        in_specs=list(specs) + [pl.BlockSpec(memory_space=pl.ANY)] * len(after),
        out_specs=[pl.BlockSpec(memory_space=pltpu.VMEM)] * len(outs),
        scratch_shapes=list(scratch),
        compiler_params=pltpu.CompilerParams(vmem_limit_bytes=limit * MIB),
        cost_estimate=pl.CostEstimate(flops=flops, bytes_accessed=moved, transcendentals=0),
    )(*args, *after)


def shape(dims, dtype):
    return jax.ShapeDtypeStruct(tuple(dims), dtype)


def dot(a, b):
    return lax.dot_general(a, b, (((1,), (0,)), ((), ())), preferred_element_type=F32)


def tree_sum(values):
    while len(values) > 1:
        values = [
            values[i] + values[i + 1] if i + 1 < len(values) else values[i]
            for i in range(0, len(values), 2)
        ]
    return values[0]


def pack_kernel(rows, cols, place_ref, x_first, x_last, g_first, g_last, one_ref, two_ref, own_ref, wide, flat):
    cin = x_first.shape[2]
    even = place_ref[0] == 0

    def x_column(ref, index):
        wide[...] = ref[...].astype(F32).reshape(2 * rows * 16, cin)
        return wide[pl.ds(index, 2 * rows, stride=16), :]

    def g_column(ref, index):
        halves = []
        for half in range(ref.shape[2] // 128):
            flat[...] = ref[:, :, half * 128 : (half + 1) * 128].astype(F32).reshape(rows * 16, 128)
            halves.append(flat[pl.ds(index, rows, stride=16), :])
        return jnp.concatenate(halves, 0)

    size = 2 * rows
    rightwards = (x_column(x_last, 15), g_column(g_last, 15))
    leftwards = (x_column(x_first, 0), x_column(x_first, 1))
    for k in range(2):
        part = slice(k * size, (k + 1) * size)
        own_ref[part, :] = rightwards[k].astype(BF16)
        one_ref[part, :] = jnp.where(even, rightwards[k], leftwards[k]).astype(BF16)
        two_ref[part, :] = jnp.where(even, leftwards[k], rightwards[k]).astype(BF16)
        both = g_column(g_first, k).astype(BF16)
        one_ref[(k + 2) * size : (k + 3) * size, :] = both
        two_ref[(k + 2) * size : (k + 3) * size, :] = both


def choose(even, one, two):
    return jnp.where(even, one.astype(F32), two.astype(F32)).astype(BF16)


def rows_kernel(
    rows, cols, place_ref, x_last, x_first, g_last, g_first, got_one, got_two,
    left_ref, right_ref, one_ref, two_ref, own_ref, x_wide, g_wide,
):
    cin = x_last.shape[2]
    depth = g_last.shape[2]
    even_col = place_ref[0] == 0
    even_row = place_ref[1] == 0
    size = 2 * rows
    left_ref[...] = choose(even_col, got_two[0 : 2 * size, :], got_one[0 : 2 * size, :])
    right_ref[...] = choose(even_col, got_one[...], got_two[...])

    def cell(ref, index):
        first = index // 16 * 16
        return ref[first : first + 16, :].astype(F32)[index - first : index - first + 1, :]

    def x_line(cells, r):
        x_wide[...] = jnp.zeros((2 * cols + 32, cin), F32)
        x_wide[16 : 16 + 2 * cols, :] = cells.astype(F32)
        x_wide[15:16, :] = cell(left_ref, r)
        x_wide[16 + 2 * cols : 17 + 2 * cols, :] = cell(right_ref, r)
        x_wide[17 + 2 * cols : 18 + 2 * cols, :] = cell(right_ref, size + r)
        return x_wide[...]

    def g_line(cells, p):
        halves = []
        for half in range(depth // 128):
            g_wide[...] = jnp.zeros((cols + 16, 128), F32)
            g_wide[8 : 8 + cols, :] = cells[:, half * 128 : (half + 1) * 128].astype(F32)
            g_wide[7:8, :] = cell(left_ref, size + half * rows + p)
            g_wide[8 + cols : 9 + cols, :] = cell(right_ref, 2 * size + half * rows + p)
            g_wide[9 + cols : 10 + cols, :] = cell(right_ref, 3 * size + half * rows + p)
            halves.append(g_wide[...])
        return jnp.concatenate(halves, 0)

    line = 2 * cols + 32
    down = (x_line(x_last[0], 2 * rows - 1), g_line(g_last[0], rows - 1))
    up = (x_line(x_first[0], 0), x_line(x_first[1], 1))
    for k in range(2):
        part = slice(k * line, (k + 1) * line)
        own_ref[part, :] = down[k].astype(BF16)
        one_ref[part, :] = jnp.where(even_row, down[k], up[k]).astype(BF16)
        two_ref[part, :] = jnp.where(even_row, up[k], down[k]).astype(BF16)
        both = g_line(g_first[k], k).astype(BF16)
        one_ref[(k + 2) * line : (k + 3) * line, :] = both
        two_ref[(k + 2) * line : (k + 3) * line, :] = both


def planes_kernel(rows, cols, x_ref, planes_ref, wide):
    cin = x_ref.shape[2]
    planes_ref[0:cols, :] = jnp.zeros((cols, 6 * cin), BF16)
    step = CHUNK // cols
    wide[:, 0:8, :] = jnp.zeros((2 * step, 8, cin), F32)

    def deinterleave(i, carry):
        base = pl.multiple_of(i * 2 * step, 2 * step)
        wide[:, 8 : 8 + 2 * cols, :] = x_ref[pl.ds(base, 2 * step)].astype(F32)
        row = pl.multiple_of((i * step + 1) * cols, cols)
        for parity in range(2):
            for slot, first in enumerate((7, 8, 9)):
                part = wide[pl.ds(parity, step, stride=2), pl.ds(first, cols, stride=2), :]
                lane = (parity * 3 + slot) * cin
                planes_ref[pl.ds(row, CHUNK), lane : lane + cin] = part.reshape(CHUNK, cin).astype(BF16)
        return carry

    lax.fori_loop(0, rows // step, deinterleave, 0)


def stride_kernel(rows, cols, planes_ref, w_ref, z_ref):
    cin = planes_ref.shape[1] // 6

    def convolve(i, carry):
        row = pl.multiple_of(i * LONG, LONG)
        above = planes_ref[pl.ds(row, LONG), 3 * cin :]
        here = planes_ref[pl.ds(pl.multiple_of(row + cols, cols), LONG), :]
        z_ref[pl.ds(row, LONG), :] = dot(jnp.concatenate([above, here], 1), w_ref[...])
        return carry

    lax.fori_loop(0, rows * cols // LONG, convolve, 0)


def edge_parts(rows, cols, xcol_ref, xrow_ref, col_pad, row_pad):
    col_pad[0:8, :] = xrow_ref[0:16, :].astype(F32)[8:16, :]
    col_pad[8 : 8 + 2 * rows, :] = xcol_ref[0 : 2 * rows, :].astype(F32)
    row_pad[0:8, :] = jnp.zeros((8, xrow_ref.shape[1]), F32)
    row_pad[8 : 8 + 2 * cols, :] = xrow_ref[16 : 16 + 2 * cols, :].astype(F32)
    left = [col_pad[pl.ds(first, rows, stride=2), :] for first in (7, 8, 9)]
    over = [row_pad[pl.ds(first, cols, stride=2), :] for first in (7, 8, 9)]
    return left, over


def edges_kernel(
    rows, cols, place_ref, z_in, xcol_ref, right_ref, own_col_ref, own_row_ref, got_one, got_two, w_ref,
    z_ref, stats_ref, xrow_ref, below_ref, z_rim_ref, col_pad, row_pad, rim, bottom, side,
):
    cin = xcol_ref.shape[1]
    even_row = place_ref[1] == 0
    line = 2 * cols + 32
    xrow_ref[...] = choose(even_row, got_two[0 : 2 * line, :], got_one[0 : 2 * line, :])
    below_ref[...] = choose(even_row, got_one[...], got_two[...])
    left, over = edge_parts(rows, cols, xcol_ref, xrow_ref, col_pad, row_pad)
    z_ref[...] = z_in[...]
    from_above = dot(jnp.concatenate(over, 1).astype(BF16), w_ref[0 : 3 * cin])
    from_left = (
        dot(left[0].astype(BF16), w_ref[0:cin])
        + dot(left[1].astype(BF16), w_ref[3 * cin : 4 * cin])
        + dot(left[2].astype(BF16), w_ref[6 * cin : 7 * cin])
    )
    z_ref[0:cols, :] = z_ref[0:cols, :] + from_above
    rim[...] = from_left
    for p in range(rows):
        z_ref[p * cols : p * cols + 1, :] = z_ref[p * cols : p * cols + 1, :] + rim[p : p + 1, :]
    z = z_ref[...]
    stats_ref[0:1, :] = jnp.sum(z, axis=0, keepdims=True)
    stats_ref[1:2, :] = jnp.sum(z * z, axis=0, keepdims=True)
    bottom[0] = own_row_ref[0:line, :].astype(F32)
    bottom[1] = below_ref[0:line, :].astype(F32)
    bottom[2] = below_ref[line : 2 * line, :].astype(F32)
    over_end = xrow_ref[2 * cols : 2 * cols + 32, :].astype(F32)
    for b, ref in enumerate((own_col_ref, right_ref, right_ref)):
        first = 2 * rows if b == 2 else 0
        side[b, 8:, :] = ref[first : first + 2 * rows, :].astype(F32)
        side[b, 7:8, :] = over_end[15 + b : 16 + b, :]
    parts = []
    for a in range(3):
        for b in range(3):
            low = bottom[a, pl.ds(15 + b, cols + 8, stride=2), :]
            beside = side[b, pl.ds(7 + a, rows, stride=2), :]
            parts.append(jnp.concatenate([low, beside], 0).astype(BF16))
    z_rim_ref[...] = dot(jnp.concatenate(parts, 1), w_ref[...])


def windows_kernel(rows, cols, planes_ref, xcol_ref, xrow_ref, t_ref, col_pad, row_pad, wide):
    cin = xrow_ref.shape[1]
    cells = rows * cols
    left, over = edge_parts(rows, cols, xcol_ref, xrow_ref, col_pad, row_pad)
    for half, parts in ((0, left[1]), (3, left[2])):
        wide[...] = planes_ref[cols:, half * cin : (half + 1) * cin].astype(F32)
        wide[pl.ds(0, rows, stride=cols), :] = parts
        window = wide[...].astype(BF16)
        t_ref[(half + 3) * cin : (half + 4) * cin, :] = window.T
    wide[cols:, :] = planes_ref[cols:cells, 3 * cin : 4 * cin].astype(F32)
    wide[0:cols, :] = over[0]
    wide[pl.ds(0, rows, stride=cols), :] = left[0]
    t_ref[0:cin, :] = wide[...].astype(BF16).T
    for slot in (1, 2):
        lane = (3 + slot) * cin
        below = planes_ref[cols:cells, lane : lane + cin]
        window = jnp.concatenate([over[slot].astype(BF16), below], 0)
        t_ref[slot * cin : (slot + 1) * cin, :] = window.T
    for slot in (1, 2, 4, 5):
        lane = slot * cin
        t_ref[lane + 3 * cin : lane + 4 * cin, :] = planes_ref[cols:, lane : lane + cin].T


def upstream_kernel(
    rows, cols, g_ref, left_ref, right_ref, own_col_ref, own_row_ref, above_ref, below_ref, w_ref,
    taps_ref, act_grad_ref, rim_ref, wide, w_t, rims, bottom, side,
):
    pitch = cols + 16
    depth = g_ref.shape[1]
    last = (rows + 1) * pitch
    size = 2 * rows
    line = 2 * cols + 32
    for p in range(rows):
        wide[(p + 1) * pitch + 8 : (p + 1) * pitch + 8 + cols, :] = g_ref[p * cols : (p + 1) * cols, :].astype(F32)
    for half in range(depth // 128):
        lanes = slice(half * 128, (half + 1) * 128)
        own = own_col_ref[size + half * rows : size + (half + 1) * rows, :].astype(F32)
        rims[0, :, lanes] = left_ref[size + half * rows : size + (half + 1) * rows, :].astype(F32)
        rims[1, :, lanes] = right_ref[2 * size + half * rows : 2 * size + (half + 1) * rows, :].astype(F32)
        side[0, 8 : 8 + rows, lanes] = right_ref[3 * size + half * rows : 3 * size + (half + 1) * rows, :].astype(F32)
        side[1, 8 : 8 + rows, lanes] = rims[1, :, lanes]
        side[2, 8 : 8 + rows, lanes] = own
        over = above_ref[line + half * pitch : line + (half + 1) * pitch, :].astype(F32)
        under = below_ref[2 * line + half * pitch : 2 * line + (half + 1) * pitch, :].astype(F32)
        wide[0:pitch, lanes] = over
        wide[last : last + pitch, lanes] = under
        for b in range(3):
            side[b, 7:8, lanes] = over[9 + cols - b : 10 + cols - b, :]
            side[b, 8 + rows : 9 + rows, lanes] = under[9 + cols - b : 10 + cols - b, :]
        bottom[0, 0:pitch, lanes] = below_ref[3 * line + half * pitch : 3 * line + (half + 1) * pitch, :].astype(F32)
        bottom[1, 0:pitch, lanes] = under
        bottom[2, 0:pitch, lanes] = own_row_ref[line + half * pitch : line + (half + 1) * pitch, :].astype(F32)
    bottom[:, pitch:, :] = jnp.zeros((3, 8, depth), F32)
    for p in range(rows):
        first = (p + 1) * pitch + 7
        wide[first : first + 1, :] = rims[0, p : p + 1, :]
        wide[first + 1 + cols : first + 2 + cols, :] = rims[1, p : p + 1, :]
    for r in range(rows + 2):
        for b in (0, 2):
            first = r * pitch + 9 - b
            taps_ref[b, r * cols : (r + 1) * cols, :] = wide[first : first + cols, :].astype(BF16)
    taps_ref[1, cols : (rows + 1) * cols, :] = g_ref[...]
    taps_ref[1, 0:cols, :] = wide[8 : 8 + cols, :].astype(BF16)
    taps_ref[1, (rows + 1) * cols :, :] = wide[last + 8 : last + 8 + cols, :].astype(BF16)
    for tap in range(9):
        w_t[tap * depth : (tap + 1) * depth, :] = w_ref[tap * depth : (tap + 1) * depth, :].T

    def convolve(i, carry):
        row = pl.multiple_of(i * LONG, LONG)
        parts = []
        for a in range(3):
            for b in range(3):
                parts.append(taps_ref[b, pl.ds(pl.multiple_of(row + (2 - a) * cols, cols), LONG), :])
        act_grad_ref[pl.ds(row, LONG), :] = dot(jnp.concatenate(parts, 1), w_t[...])
        return carry

    lax.fori_loop(0, rows * cols // LONG, convolve, 0)
    parts = []
    for a in range(3):
        for b in range(3):
            low = bottom[a, 9 - b : 17 - b + cols, :]
            beside = side[b, 9 - a : 9 - a + rows, :]
            parts.append(jnp.concatenate([low, beside], 0).astype(BF16))
    rim_ref[...] = dot(jnp.concatenate(parts, 1), w_t[...])


def group_sum(value, depth):
    size = depth // GROUPS
    one = lax.broadcasted_iota(jnp.int32, (depth, depth), 0) // size
    two = lax.broadcasted_iota(jnp.int32, (depth, depth), 1) // size
    same = jnp.where(one == two, 1.0, 0.0).astype(F32)
    return lax.dot_general(
        value, same, (((1,), (0,)), ((), ())), precision=lax.Precision.HIGHEST, preferred_element_type=F32
    )


def space_sum(core_ref, own_ref, pair_ref):
    even = core_ref[0] == 0
    values = [own_ref[0]]
    for k in range(1, own_ref.shape[0]):
        values.append(jnp.where(even, own_ref[k], pair_ref[k]))
        values.append(jnp.where(even, pair_ref[k], own_ref[k]))
    return tree_sum(values[:-1])


def add_kernel(one_ref, two_ref, out_ref):
    out_ref[...] = one_ref[...] + two_ref[...]


def stack_kernel(*refs):
    for k, ref in enumerate(refs[:-1]):
        refs[-1][k] = ref[...]


def normalize(norm_count, core_ref, own_ref, pair_ref, z_ref, act_grad_ref, gain_ref, bias_ref, act_ref, pre_ref, sums_ref, moments_ref):
    cells, depth = z_ref.shape
    total = group_sum(space_sum(core_ref, own_ref, pair_ref), depth) / norm_count
    mean = total[0:1, :]
    inv_std = 1.0 / jnp.sqrt(total[1:2, :] - mean * mean + 1e-05)
    moments_ref[0:1, :] = mean
    moments_ref[1:2, :] = inv_std
    gain = gain_ref[...]
    bias = bias_ref[...]

    def chunk(i, carry):
        row = pl.multiple_of(i * 64, 64)
        normed = (z_ref[pl.ds(row, 64), :] - mean) * inv_std
        shifted = normed * gain + bias
        sig = 1.0 / (1.0 + jnp.exp(-shifted))
        act_ref[pl.ds(row, 64), :] = (shifted * sig).astype(BF16)
        pre = act_grad_ref[pl.ds(row, 64), :] * sig * (1.0 + shifted * (1.0 - sig))
        pre_ref[pl.ds(row, 64), :] = pre
        one = jnp.sum(pre.reshape(8, 8, depth), axis=0)
        two = jnp.sum((pre * normed).reshape(8, 8, depth), axis=0)
        return carry[0] + one, carry[1] + two

    zero = jnp.zeros((8, depth), F32)
    one, two = lax.fori_loop(0, cells // 64, chunk, (zero, zero))
    sums_ref[0:1, :] = jnp.sum(one, axis=0, keepdims=True)
    sums_ref[1:2, :] = jnp.sum(two, axis=0, keepdims=True)


def activate_kernel(norm_count, rows, cols, me_ref, *refs):
    *plain, taps_ref, pre_ref, sums_ref, moments_ref, out_ref, act_ref, whole = refs
    normalize(norm_count, *plain, act_ref, pre_ref, sums_ref, moments_ref)
    cells = rows * cols
    depth = act_ref.shape[1]
    act_t = act_ref[...].T
    for a in range(3):
        for b in range(3):
            first = (2 - a) * cols
            tap = a * 3 + b
            whole[tap * depth : (tap + 1) * depth, :] = dot(act_t, taps_ref[b, first : first + cells, :])
    spread(me_ref, whole, out_ref)


def spread(me_ref, whole, out_ref):
    size = out_ref.shape[1]
    for slot in range(8):
        first = pl.multiple_of((me_ref[0] ^ slot) * size, 16)
        out_ref[slot] = whole[pl.ds(first, size), :]


def conv_grad_kernel(norm_count, rows, cols, me_ref, *refs):
    count = 3
    sums = refs[:count]
    place_ref, z_ref, pre_ref, moments_ref, gain_ref, bias_ref, z_rim_ref, act_rim_ref, t_ref, grad_ref, rim_ref, total_ref, out_ref, whole = refs[count:]
    cells, depth = z_ref.shape
    total = space_sum(*sums)
    total_ref[...] = total
    gain = gain_ref[...]
    means = group_sum(total * gain, depth) / norm_count
    mean = moments_ref[0:1, :]
    inv_std = moments_ref[1:2, :]
    shift = means[0:1, :]
    scale = means[1:2, :]

    def value(z, pre):
        return ((gain * pre - shift - (z - mean) * inv_std * scale) * inv_std).astype(BF16)

    def chunk(i, carry):
        row = pl.multiple_of(i * 64, 64)
        grad_ref[pl.ds(row, 64), :] = value(z_ref[pl.ds(row, 64), :], pre_ref[pl.ds(row, 64), :])
        return carry

    lax.fori_loop(0, cells // 64, chunk, 0)
    z = z_rim_ref[...]
    shifted = (z - mean) * inv_std * gain + bias_ref[...]
    sig = 1.0 / (1.0 + jnp.exp(-shifted))
    pre = act_rim_ref[...] * sig * (1.0 + shifted * (1.0 - sig))
    cell = lax.broadcasted_iota(jnp.int32, z.shape, 0)
    to_right = jnp.where(cell >= cols, place_ref[2], 1)
    to_below = jnp.where(cell < cols + 8, place_ref[3], 1)
    rim_ref[...] = jnp.where(to_right * to_below == 1, value(z, pre).astype(F32), 0.0)

    def product(i, carry):
        row = pl.multiple_of(i * size, 128)
        whole[pl.ds(row, size), :] = dot(t_ref[pl.ds(row, size), :], grad_ref[...])
        return carry

    size = t_ref.shape[0] // 3
    lax.fori_loop(0, 3, product, 0)
    spread(me_ref, whole, out_ref)


def input_kernel(rows, cols, d_ref, rim_ref, w_ref, out_ref, plain, shifted, w_t, wide, mixed):
    cells = rows * cols
    cin = out_ref.shape[2]
    depth = d_ref.shape[1]
    pitch = cols + 8
    plain[0:cells, :] = d_ref[...]
    plain[cells:, :] = rim_ref[0:cols, :].astype(BF16)
    for p in range(rows + 1):
        first = p * pitch
        wide[first : first + cols, :] = plain[p * cols : (p + 1) * cols, :].astype(F32)
        next_cell = cols + 8 + p if p < rows else cols
        wide[first + cols : first + cols + 1, :] = rim_ref[next_cell : next_cell + 1, :]
        shifted[p * cols : (p + 1) * cols, :] = wide[first + 1 : first + 1 + cols, :].astype(BF16)
    for place, tap in enumerate((4, 5, 7, 8, 3, 6, 1, 2, 0)):
        w_t[:, place * cin : (place + 1) * cin] = w_ref[tap * cin : (tap + 1) * cin, :].T
    step = CHUNK // cols

    def chunk(i, carry):
        row = pl.multiple_of(i * CHUNK, CHUNK)
        under = pl.multiple_of(row + cols, cols)
        own = dot(plain[pl.ds(row, CHUNK), :], w_t[:, 0 : 4 * cin])
        right = dot(shifted[pl.ds(row, CHUNK), :], w_t[:, 4 * cin : 6 * cin])
        below = dot(plain[pl.ds(under, CHUNK), :], w_t[:, 6 * cin : 8 * cin])
        corner = dot(shifted[pl.ds(under, CHUNK), :], w_t[:, 8 * cin :])
        even_even = own[:, 0:cin]
        even_odd = own[:, cin : 2 * cin] + right[:, 0:cin]
        odd_even = own[:, 2 * cin : 3 * cin] + below[:, 0:cin]
        odd_odd = own[:, 3 * cin :] + right[:, cin:] + below[:, cin:] + corner
        for parity, pair in enumerate(((even_even, even_odd), (odd_even, odd_odd))):
            for side in range(2):
                mixed[pl.ds(parity, step, stride=2), pl.ds(side, cols, stride=2), :] = pair[side].reshape(
                    step, cols, cin
                )
        out_ref[pl.ds(pl.multiple_of(i * 2 * step, 2 * step), 2 * step)] = mixed[...].astype(BF16)
        return carry

    lax.fori_loop(0, rows // step, chunk, 0)


def half_kernel(slots_ref, other_ref, *refs):
    own_ref, one_ref, two_ref, three_ref = refs[-4:]
    rows = slots_ref.shape[1]
    own_ref[...] = slots_ref[0] + other_ref[0]
    for k, ref in enumerate((one_ref, two_ref, three_ref)):
        ref[0:rows, :] = (slots_ref[k + 1] + other_ref[k + 1]).astype(BF16)
    if len(refs) > 4:
        two_ref[rows:, :] = three_parts(refs[0][...])


def three_parts(pair):
    high = pair.astype(BF16).astype(F32)
    rest = pair - high
    middle = rest.astype(BF16).astype(F32)
    low = rest - middle
    zeros = jnp.zeros((10, pair.shape[1]), F32)
    return jnp.concatenate([high, middle, low, zeros], 0).astype(BF16)


def from_parts(parts):
    parts = parts.astype(F32)
    return parts[0:2, :] + parts[2:4, :] + parts[4:6, :]


def total_kernel(*refs):
    rows = refs[-1].shape[0]
    refs[-1][...] = tree_sum([r[0:rows, :].astype(F32) for r in refs[:-1]]).astype(BF16)


def both_kernel(count, *refs):
    second, first, out_ref = refs[:count], refs[count:-1], refs[-1]
    rows = second[0].shape[0]
    out_ref[0:rows, :] = tree_sum([r[...].astype(F32) for r in second]).astype(BF16)
    out_ref[rows:, :] = tree_sum([r[...].astype(F32) for r in first]).astype(BF16)


def first_total_kernel(own_ref, one_ref, two_ref, three_ref, pair_ref, out_ref, both_ref):
    total_kernel(own_ref, one_ref, two_ref, three_ref, out_ref)
    rows = out_ref.shape[0]
    both_ref[...] = from_parts(three_parts(pair_ref[...])) + from_parts(two_ref[rows:, :])


def gather_kernel(me_ref, *refs):
    me = me_ref[0]
    *own, other_ref, second_ref, first_ref = refs
    rows = second_ref.shape[1]
    for slot in range(4):
        second_ref[me ^ slot] = own[slot][0:rows, :].astype(F32)
        first_ref[me ^ slot] = own[slot][rows:, :].astype(F32)
        second_ref[me ^ slot ^ 4] = other_ref[slot, 0:rows, :].astype(F32)
        first_ref[me ^ slot ^ 4] = other_ref[slot, rows:, :].astype(F32)


def on_device(dp_size, tiles, images, first_weight, norm_gain, norm_bias, second_weight, upstream):
    rows, cols, depth = upstream.shape[2:]
    cin = images.shape[4]
    cells = rows * cols
    group_size = depth // GROUPS
    norm_count = float(cells * tiles * group_size)
    tile_rows = tiles // TCOLS
    axes = ("dp", "space")
    devices = dp_size * tiles

    def flip(value, mask):
        return lax.ppermute(value, axes, [(i, i ^ mask) for i in range(devices)])

    def swapped(value, down, right):
        pairs = []
        for t in range(tiles):
            spot = (t + TCOLS + 2) % tiles
            r, c = spot // TCOLS, spot % TCOLS
            r = r if not down else ((r + down - 1) ^ 1) - down + 1
            c = c if not right else ((c + right - 1) ^ 1) - right + 1
            if 0 <= r < tile_rows and 0 <= c < TCOLS:
                pairs.append((t, (r * TCOLS + c - TCOLS - 2) % tiles))
        return lax.ppermute(value, "space", pairs)

    def space_sums(value, after=()):
        (near,) = call(add_kernel, [shape(value.shape, F32)], [value, flip(value, 1)], after=after)
        parts = [near]
        chips = tiles // 2
        for k in range(1, chips, 2):
            pairs = [(i, i ^ (2 * (k + i % 2))) for i in range(devices) if k + i % 2 < chips]
            parts.append(lax.ppermute(near, axes, pairs))
        (own,) = call(stack_kernel, [shape((len(parts),) + near.shape, F32)], parts)
        return near, parts, [core, own, flip(own, 1)]

    def along(value, size, step):
        return [value] + [flip(value, step * k) for k in range(1, size)]

    def total(parts, after=()):
        if len(parts) == 1:
            return parts[0]
        return call(total_kernel, [shape(parts[0].shape, BF16)], parts, after=after)[0]

    def halved(slots, more=()):
        part = slots.shape[1:]
        longer = (part[0] + 16 * len(more), part[1])
        outs = [shape(part, F32), shape(part, BF16), shape(longer, BF16), shape(part, BF16)]
        return call(half_kernel, outs, [slots, flip(slots[4:8], 1), *more])

    masks = [0, 2, tiles, tiles + 2]

    def quartered(parts):
        return [parts[0]] + [flip(parts[k], masks[k]) for k in (1, 2, 3)]

    def quarters(shard):
        return [shard] + [flip(shard, masks[k]) for k in (1, 2, 3)]

    def gathered(own, after=()):
        (stacked,) = call(stack_kernel, [shape((4,) + own[0].shape, BF16)], own, after=after)
        return own + [flip(stacked, 1)]

    space = lax.axis_index("space")
    me = (space % 2) * 4 + (lax.axis_index("dp") % 2) * 2 + (space // 2) % 2
    me = me.astype(jnp.int32).reshape(1)
    core = (space % 2).astype(jnp.int32).reshape(1)
    spot = (space + TCOLS + 2) % tiles
    column, row = spot % TCOLS, spot // TCOLS
    place = jnp.stack([column % 2, row % 2, column < TCOLS - 1, row < tile_rows - 1]).astype(jnp.int32)
    x = images[0, 0]
    g3 = upstream[0, 0]
    w1 = first_weight.reshape(9 * cin, depth)
    w2 = second_weight.reshape(9 * depth, depth)
    gain = norm_gain.reshape(1, depth)
    bias = norm_bias.reshape(1, depth)

    g_block = (rows, 16, depth)
    smem = pl.BlockSpec(memory_space=pltpu.SMEM)
    vmem = pl.BlockSpec(memory_space=pltpu.VMEM)
    ends = shape((4 * 2 * rows, cin), BF16)
    half_ends = shape((2 * 2 * rows, cin), BF16)
    one, two, own_column = call(
        functools.partial(pack_kernel, rows, cols),
        [ends, ends, half_ends],
        [place, x, x, g3, g3],
        [pltpu.VMEM((2 * rows * 16, cin), F32), pltpu.VMEM((rows * 16, 128), F32)],
        specs=[
            smem,
            pl.BlockSpec((2 * rows, 16, cin), lambda i: (0, 0, 0)),
            pl.BlockSpec((2 * rows, 16, cin), lambda i: (0, 2 * cols // 16 - 1, 0)),
            pl.BlockSpec(g_block, lambda i: (0, 0, 0)),
            pl.BlockSpec(g_block, lambda i: (0, cols // 16 - 1, 0)),
        ],
        grid=(1,),
    )
    one = swapped(one, 0, 1)
    two = swapped(two, 0, 2)
    (planes,) = call(
        functools.partial(planes_kernel, rows, cols),
        [shape((cells + cols, 6 * cin), BF16)],
        [x],
        [pltpu.VMEM((2 * CHUNK // cols, 2 * cols + 8, cin), F32)],
        flops=cells * 9 * cin * depth,
    )
    lines = shape((4 * (2 * cols + 32), cin), BF16)
    half_lines = shape((2 * (2 * cols + 32), cin), BF16)
    from_left, from_right, one, two, own_row = call(
        functools.partial(rows_kernel, rows, cols),
        [half_ends, ends, lines, lines, half_lines],
        [place, x, x, g3, g3, one, two],
        [pltpu.VMEM((2 * cols + 32, cin), F32), pltpu.VMEM((cols + 16, 128), F32)],
        specs=[
            smem,
            pl.BlockSpec((1, 2 * cols, cin), lambda i: (2 * rows - 1, 0, 0)),
            pl.BlockSpec((2, 2 * cols, cin), lambda i: (0, 0, 0)),
            pl.BlockSpec((1, cols, depth), lambda i: (rows - 1, 0, 0)),
            pl.BlockSpec((2, cols, depth), lambda i: (0, 0, 0)),
            vmem,
            vmem,
        ],
        grid=(1,),
        after=[planes],
    )
    got_one = swapped(one, 1, 0)
    got_two = swapped(two, 2, 0)
    (z,) = call(
        functools.partial(stride_kernel, rows, cols),
        [shape((cells, depth), F32)],
        [planes, w1],
        flops=2 * cells * 9 * cin * depth,
        after=[one],
    )
    pads = [pltpu.VMEM((2 * rows + 8, cin), F32), pltpu.VMEM((2 * cols + 8, cin), F32)]
    rim = rows + cols + 8
    z, stats, from_above, from_below, z_rim = call(
        functools.partial(edges_kernel, rows, cols),
        [shape((cells, depth), F32), shape((2, depth), F32), half_lines, lines, shape((rim, depth), F32)],
        [place, z, from_left, from_right, own_column, own_row, got_one, got_two, w1],
        pads
        + [
            pltpu.VMEM((rows, depth), F32),
            pltpu.VMEM((3, 2 * cols + 32, cin), F32),
            pltpu.VMEM((3, 2 * rows + 8, cin), F32),
        ],
        smem=1,
        flops=2 * 80 * 3 * cin * depth,
    )
    _, _, stats = space_sums(stats)
    taps, act_grad, act_rim = call(
        functools.partial(upstream_kernel, rows, cols),
        [shape((3, cells + 2 * cols, depth), BF16), shape((cells, depth), F32), shape((rim, depth), F32)],
        [g3.reshape(cells, depth), from_left, from_right, own_column, own_row, from_above, from_below, w2],
        [
            pltpu.VMEM(((rows + 2) * (cols + 16), depth), F32),
            pltpu.VMEM((9 * depth, depth), BF16),
            pltpu.VMEM((2, rows, depth), F32),
            pltpu.VMEM((3, cols + 24, depth), F32),
            pltpu.VMEM((3, rows + 16, depth), F32),
        ],
        flops=2 * cells * 9 * depth * depth,
    )
    pre_grad, sums, moments, second_slots = call(
        functools.partial(activate_kernel, norm_count, rows, cols),
        [
            shape((cells, depth), F32),
            shape((2, depth), F32),
            shape((2, depth), F32),
            shape((8, 9 * depth // 8, depth), F32),
        ],
        [me] + stats + [z, act_grad, gain, bias, taps],
        [pltpu.VMEM((cells, depth), BF16), pltpu.VMEM((9 * depth, depth), F32)],
        flops=2 * cells * 9 * depth * depth,
        smem=2,
    )
    second_parts = quartered(halved(second_slots))
    near, parts, sums = space_sums(sums, second_parts[:1])
    (windows,) = call(
        functools.partial(windows_kernel, rows, cols),
        [shape((9 * cin, cells), BF16)],
        [planes, from_left, from_above],
        pads + [pltpu.VMEM((cells, cin), F32)],
        flops=2 * cells * 9 * cin * depth,
        after=[parts[0]],
    )
    second_shard = along(total(along(total(second_parts), dp_size // 2, 2 * tiles)), tiles // 4, 4)
    conv_grad, grad_rim, sum_pair, first_slots = call(
        functools.partial(conv_grad_kernel, norm_count, rows, cols),
        [
            shape((cells, depth), BF16),
            shape((rim, depth), F32),
            shape((2, depth), F32),
            shape((8, 9 * cin // 8, depth), F32),
        ],
        [me] + sums + [place, z, pre_grad, moments, gain, bias, z_rim, act_rim, windows],
        [pltpu.VMEM((9 * cin, depth), F32)],
        flops=2 * cells * 9 * cin * depth,
        specs=[smem, smem, vmem, vmem, smem] + [vmem] * 8,
        after=second_shard[:1],
    )
    first_parts = quartered(halved(first_slots, [sum_pair]))
    first_shard, sum_pair = call(
        first_total_kernel,
        [shape(first_slots.shape[1:], BF16), shape((2, depth), F32)],
        first_parts + [sum_pair],
        after=second_shard[1:],
    )
    first_shard = along(total(along(first_shard, dp_size // 2, 2 * tiles)), tiles // 4, 4)
    (input_grad,) = call(
        functools.partial(input_kernel, rows, cols),
        [shape((2 * rows, 2 * cols, cin), BF16)],
        [conv_grad, grad_rim, w1],
        [
            pltpu.VMEM((cells + cols, depth), BF16),
            pltpu.VMEM((cells + cols, depth), BF16),
            pltpu.VMEM((depth, 9 * cin), BF16),
            pltpu.VMEM(((rows + 1) * (cols + 8), depth), F32),
            pltpu.VMEM((2 * CHUNK // cols, 2 * cols, cin), F32),
        ],
        flops=2 * cells * 9 * cin * depth,
    )
    sizes = second_slots.shape[1], first_slots.shape[1]
    (shard,) = call(
        functools.partial(both_kernel, len(second_shard)),
        [shape((sum(sizes), depth), BF16)],
        second_shard + first_shard,
        after=[input_grad],
    )
    for k in range(1, dp_size.bit_length() - 1):
        sum_pair = sum_pair + flip(sum_pair, tiles << k)
    second_grad, first_grad = call(
        gather_kernel,
        [shape((8, sizes[0], depth), F32), shape((8, sizes[1], depth), F32)],
        [me] + gathered(quarters(shard)),
        smem=1,
    )
    return (
        input_grad[None, None],
        first_grad.reshape(first_weight.shape),
        second_grad.reshape(second_weight.shape),
        sum_pair[1],
        sum_pair[0],
    )


def solution(mesh):
    placed = (
        P("dp", "space", None, None, None),
        P(),
        P(),
        P(),
        P(),
        P("dp", "space", None, None, None),
    )
    return jax.shard_map(
        functools.partial(on_device, mesh.shape["dp"], mesh.shape["space"]),
        mesh=mesh,
        in_specs=placed,
        out_specs=(P("dp", "space", None, None, None), P(), P(), P(), P()),
        check_vma=False,
    )
```

time: 131 us -> 119 us (0.908)
  starting transfers between devices: 67.7 us -> 55.4 us
  local copies, waits for them, and re-layouts: 6.92 us -> 9.4 us
    ppermute x10 -> x12, starting transfers between devices: 28.4 us -> 13 us  [the longest x8 6.69 us: space_sums(): parts.append(lax.ppermute(near, axes, pairs))]
    ppermute x33 -> x22, waiting for transfers between devices: 30.4 us -> 20.1 us  [flip(): return lax.ppermute(value, axes, [(i, i ^ mask) for i in range(devices)])]
    ppermute x10 -> x12, waiting for transfers between devices: 0.05 us -> 9.16 us  [the longest x8 6.22 us: space_sums(): parts.append(lax.ppermute(near, axes, pairs))]
    unnamed x18 -> x30, local copies, waits for them, and re-layouts: 5.31 us -> 8.72 us
    ppermute x33 -> x22, starting transfers between devices: 39.3 us -> 42.5 us  [flip(): return lax.ppermute(value, axes, [(i, i ^ mask) for i in range(devices)])]
    pallas_call x9 -> x21, Pallas kernels: 22 us -> 22.7 us  [call(): pl.pallas_call(body, out_shape=list(outs), grid=grid, in_specs=list(specs...]
  transfers between devices with their start and end apart: 43 -> 34, of which waited for: 11 -> 16; matrix products, arithmetic and copies ran while one was open for 3% -> 0% of each run, Pallas kernels for 13% -> 9%
where the time goes in v1:
time: 119 us; the launch traced here: 118 us
  starting transfers between devices  55.4 us (47%)
  waiting for transfers between devices  29.2 us (25%)
  Pallas kernels  22.7 us (19%)
  local copies, waits for them, and re-layouts  9.4 us (8%)
    ppermute x22, starting transfers between devices, flip(): return lax.ppermute(value, axes, [(i, i ^ mask) for i in range(devices)])  42.5 us
    pallas_call x21, Pallas kernels, call(): pl.pallas_call(body, out_shape=list(outs), grid=grid, in_specs=list(specs...  22.7 us
    ppermute x22, waiting for transfers between devices, flip(): return lax.ppermute(value, axes, [(i, i ^ mask) for i in range(devices)])  20.1 us
    unnamed x30, local copies, waits for them, and re-layouts  8.72 us
    ppermute x8, starting transfers between devices, space_sums(): parts.append(lax.ppermute(near, axes, pairs))  6.69 us
    ppermute x4, starting transfers between devices, swapped(): return lax.ppermute(value, 'space', pairs)  6.28 us
    ppermute x8, waiting for transfers between devices, space_sums(): parts.append(lax.ppermute(near, axes, pairs))  6.22 us
    ppermute x4, waiting for transfers between devices, swapped(): return lax.ppermute(value, 'space', pairs)  2.94 us
  transfers between devices with their start and end apart: 34, of which 16 were waited for; matrix products, arithmetic and copies ran while one was open for 0% of the time, Pallas kernels for 9%

profile of v1, /device:TPU:1, one launch (start us, length us, event | category | flops | bytes accessed | tf_op | source)
XLA Modules:
  0.0 117.9 jit_solution(5293151558561624259)
XLA Ops:
  6.3 4.7 %collective-permute-start.3 = (bf16[384,128]{1,0:T(8,128)(2,1)S(1)}, bf16[384,128]{1,0:T(8,128)(2,1)S(1)}, u32[]{:S(2)}, u32[]{:S(2)}) collective-permute-start(bf16[384,128]{1,0:T(8,128)(2,1)S(1)} %get-tuple-element.48), channel_id=1, source_target_pairs={{0,4},{1,5},{2,14},{3,15},{4,0},{5,1},{14,2},{15,3},{16,20},{17,21... | collective-permute-start | bytes 294920 | tf_op jit(solution)/shard_map/ppermute | solution.py:541
  11.8 1.5 %shard_map.104.refs_1_ = f32[1536,256]{1,0:T(8,128)S(1)} custom-call(bf16[1568,768]{1,0:T(8,128)(2,1)S(1)} %shard_map.101.refs_7_.refs_0_, bf16[1152,256]{1,0:T(8,128)(2,1)S(1)} %bitcast.28, bf16[384,128]{1,0:T(8,128)(2,1)S(1)} %get-tuple-element.43.refs_2_), custom_call_target="tpu_custom_call" | custom-call | flops 905969664 | bytes 4571136 | tf_op jit(solution)/shard_map/pallas_call | solution.py:29
  14.0 2.3 %collective-permute-done.2.refs_6_ = bf16[384,128]{1,0:T(8,128)(2,1)S(1)} collective-permute-done((bf16[384,128]{1,0:T(8,128)(2,1)S(1)}, bf16[384,128]{1,0:T(8,128)(2,1)S(1)}, u32[]{:S(2)}, u32[]{:S(2)}) %collective-permute-start.2) | collective-permute-done | bytes 98336 | tf_op jit(solution)/shard_map/ppermute | solution.py:541
  19.1 7.9 %collective-permute-start.4 = (f32[2,256]{1,0:T(2,128)S(1)}, f32[2,256]{1,0:T(2,128)S(1)}, u32[]{:S(2)}, u32[]{:S(2)}) collective-permute-start(f32[2,256]{1,0:T(2,128)S(1)} %get-tuple-element.49.refs_0_), channel_id=1, source_target_pairs={{0,1},{1,0},{2,3},{3,2},{4,5},{5,4},{6,7},{7,6},{8,9},{9,8},{10,11... | collective-permute-start | bytes 6152 | tf_op jit(solution)/shard_map/ppermute | solution.py:530
  33.0 7.3 %collective-permute-start.9 = (f32[5,2,256]{2,1,0:T(2,128)S(1)}, f32[5,2,256]{2,1,0:T(2,128)S(1)}, u32[]{:S(2)}, u32[]{:S(2)}) collective-permute-start(f32[5,2,256]{2,1,0:T(2,128)S(1)} %shard_map.107.refs_2_), channel_id=1, source_target_pairs={{0,1},{1,0},{2,3},{3,2},{4,5},{5,4},{6,7},{7,6},{8,9},{9,8},{10,11... | collective-permute-start | bytes 30728 | tf_op jit(solution)/shard_map/ppermute | solution.py:530
  43.2 3.6 %shard_map.108 = (bf16[3,1600,256]{2,1,0:T(8,128)(2,1)S(1)}, f32[1536,256]{1,0:T(8,128)S(1)}, f32[88,256]{1,0:T(8,128)S(1)}) custom-call(bf16[1536,256]{1,0:T(8,128)(2,1)S(1)} %bitcast.27, bf16[192,128]{1,0:T(8,128)(2,1)S(1)} %get-tuple-element.44.refs_2_.refs_1_, bf16[384,128]{1,0:T(8,128)(2,1)S(1)} %get-tuple-element.45.refs_3_.refs_2_, ...), custom_call_target="tpu_custom_call" | custom-call | flops 1811939328 | bytes 6479872 | tf_op jit(solution)/shard_map/pallas_call | solution.py:29
  46.9 3.8 %shard_map.109 = (f32[1536,256]{1,0:T(8,128)S(1)}, f32[2,256]{1,0:T(2,128)S(1)}, f32[2,256]{1,0:T(2,128)S(1)}, f32[8,288,256]{2,1,0:T(8,128)S(1)}) custom-call(s32[1]{0:T(128)} %bitcast.refs_0_, s32[1]{0:T(128)} %bitcast.1.refs_1_, f32[5,2,256]{2,1,0:T(2,128)S(1)} %shard_map.107.refs_2_, f32[5,2,256]{2,1,0:T(2,128)S(1)} %collective-permute-done.9.refs_3_, ...), custom_call_target="tpu_custom_call" | custom-call | flops 1811939328 | bytes 9562120 | tf_op jit(solution)/shard_map/pallas_call | solution.py:29
  50.9 2.8 %collective-permute-done.11.refs_1_ = f32[4,288,256]{2,1,0:T(8,128)S(1)} collective-permute-done((f32[4,288,256]{2,1,0:T(8,128)S(1)}, f32[4,288,256]{2,1,0:T(8,128)S(1)}, u32[]{:S(2)}, u32[]{:S(2)}) %collective-permute-start.11) | collective-permute-done | bytes 1179680 | tf_op jit(solution)/shard_map/ppermute | solution.py:530
  59.1 1.8 %collective-permute-start.14 = (f32[2,256]{1,0:T(2,128)S(1)}, f32[2,256]{1,0:T(2,128)S(1)}, u32[]{:S(2)}, u32[]{:S(2)}) collective-permute-start(f32[2,256]{1,0:T(2,128)S(1)} %shard_map.111.refs_0_.refs_3_), channel_id=1, source_target_pairs={{0,10},{1,13},{2,8},{3,15},{4,14},{5,9},{6,12},{7,11},{8,2},{9,5},... | collective-permute-start | bytes 6152 | tf_op jit(solution)/shard_map/ppermute | solution.py:549
  60.9 2.5 %collective-permute-done.14.refs_3_ = f32[2,256]{1,0:T(2,128)S(1)} collective-permute-done((f32[2,256]{1,0:T(2,128)S(1)}, f32[2,256]{1,0:T(2,128)S(1)}, u32[]{:S(2)}, u32[]{:S(2)}) %collective-permute-start.14) | collective-permute-done | bytes 2080 | tf_op jit(solution)/shard_map/ppermute | solution.py:549
  64.2 1.9 %collective-permute-done.12.refs_1_ = f32[2,256]{1,0:T(2,128)S(1)} collective-permute-done((f32[2,256]{1,0:T(2,128)S(1)}, f32[2,256]{1,0:T(2,128)S(1)}, u32[]{:S(2)}, u32[]{:S(2)}) %collective-permute-start.12) | collective-permute-done | bytes 2080 | tf_op jit(solution)/shard_map/ppermute | solution.py:549
  66.1 5.4 %collective-permute-start.16 = (f32[5,2,256]{2,1,0:T(2,128)S(1)}, f32[5,2,256]{2,1,0:T(2,128)S(1)}, u32[]{:S(2)}, u32[]{:S(2)}) collective-permute-start(f32[5,2,256]{2,1,0:T(2,128)S(1)} %shard_map.112.refs_2_), channel_id=1, source_target_pairs={{0,1},{1,0},{2,3},{3,2},{4,5},{5,4},{6,7},{7,6},{8,9},{9,8},{10,11... | collective-permute-start | bytes 30728 | tf_op jit(solution)/shard_map/ppermute | solution.py:530
  72.7 2.9 %shard_map.115 = (bf16[1536,256]{1,0:T(8,128)(2,1)S(1)}, f32[88,256]{1,0:T(8,128)S(1)}, f32[2,256]{1,0:T(2,128)S(1)}, f32[8,144,256]{2,1,0:T(8,128)S(1)}) custom-call(s32[1]{0:T(128)} %bitcast.refs_0_, s32[1]{0:T(128)} %bitcast.1.refs_1_, f32[5,2,256]{2,1,0:T(2,128)S(1)} %shard_map.112.refs_2_, f32[5,2,256]{2,1,0:T(2,128)S(1)} %collective-permute-done.16.refs_3_, ...), custom_call_target="tpu_custom_call" | custom-call | flops 905969664 | bytes 8947736 | tf_op jit(solution)/shard_map/pallas_call | solution.py:29
  75.7 1.8 %collective-permute-start.22 = (bf16[288,256]{1,0:T(8,128)(2,1)S(1)}, bf16[288,256]{1,0:T(8,128)(2,1)S(1)}, u32[]{:S(2)}, u32[]{:S(2)}) collective-permute-start(bf16[288,256]{1,0:T(8,128)(2,1)S(1)} %shard_map.114.refs_13_.refs_0_), channel_id=1, source_target_pairs={{0,12},{1,13},{2,14},{3,15},{4,8},{5,9},{6,10},{7,11},{8,4},{9,5},... | collective-permute-start | bytes 442376 | tf_op jit(solution)/shard_map/ppermute | solution.py:530
  77.5 1.8 %collective-permute-start.20 = (bf16[288,256]{1,0:T(8,128)(2,1)S(1)}, bf16[288,256]{1,0:T(8,128)(2,1)S(1)}, u32[]{:S(2)}, u32[]{:S(2)}) collective-permute-start(bf16[288,256]{1,0:T(8,128)(2,1)S(1)} %shard_map.114.refs_13_.refs_0_), channel_id=1, source_target_pairs={{0,4},{1,5},{2,6},{3,7},{4,0},{5,1},{6,2},{7,3},{8,12},{9,13},{10,... | collective-permute-start | bytes 442376 | tf_op jit(solution)/shard_map/ppermute | solution.py:530
  82.6 2.3 %collective-permute-start.26 = (bf16[144,256]{1,0:T(8,128)(2,1)S(1)}, bf16[144,256]{1,0:T(8,128)(2,1)S(1)}, u32[]{:S(2)}, u32[]{:S(2)}) collective-permute-start(bf16[144,256]{1,0:T(8,128)(2,1)S(1)} %get-tuple-element.72), channel_id=1, source_target_pairs={{0,18},{1,19},{2,16},{3,17},{4,22},{5,23},{6,20},{7,21},{8,26},{9,... | collective-permute-start | bytes 221192 | tf_op jit(solution)/shard_map/ppermute | solution.py:530
  84.9 5.4 %collective-permute-done.21.refs_6_.refs_2_ = bf16[288,256]{1,0:T(8,128)(2,1)S(1)} collective-permute-done((bf16[288,256]{1,0:T(8,128)(2,1)S(1)}, bf16[288,256]{1,0:T(8,128)(2,1)S(1)}, u32[]{:S(2)}, u32[]{:S(2)}) %collective-permute-start.21) | collective-permute-done | bytes 147488 | tf_op jit(solution)/shard_map/ppermute | solution.py:530
  90.4 1.7 %collective-permute-start.29 = (bf16[144,256]{1,0:T(8,128)(2,1)S(1)}, bf16[144,256]{1,0:T(8,128)(2,1)S(1)}, u32[]{:S(2)}, u32[]{:S(2)}) collective-permute-start(bf16[144,256]{1,0:T(8,128)(2,1)S(1)} %get-tuple-element.73.refs_4_), channel_id=1, source_target_pairs={{0,12},{1,13},{2,14},{3,15},{4,8},{5,9},{6,10},{7,11},{8,4},{9,5},... | collective-permute-start | bytes 221192 | tf_op jit(solution)/shard_map/ppermute | solution.py:530
  94.0 4.1 %shard_map.116.refs_8_ = bf16[96,64,128]{2,1,0:T(8,128)(2,1)} custom-call(bf16[1536,256]{1,0:T(8,128)(2,1)S(1)} %get-tuple-element.65.refs_0_, f32[88,256]{1,0:T(8,128)S(1)} %get-tuple-element.66.refs_1_, bf16[1152,256]{1,0:T(8,128)(2,1)S(1)} %bitcast.30), custom_call_target="tpu_custom_call" | custom-call | flops 905969664 | bytes 3039232 | tf_op jit(solution)/shard_map/pallas_call | solution.py:29
  99.7 2.6 %collective-permute-start.32 = (bf16[432,256]{1,0:T(8,128)(2,1)S(1)}, bf16[432,256]{1,0:T(8,128)(2,1)S(1)}, u32[]{:S(2)}, u32[]{:S(2)}) collective-permute-start(bf16[432,256]{1,0:T(8,128)(2,1)S(1)} %shard_map.119.refs_0_.refs_1_), channel_id=1, source_target_pairs={{0,18},{1,19},{2,16},{3,17},{4,22},{5,23},{6,20},{7,21},{8,26},{9,... | collective-permute-start | bytes 663560 | tf_op jit(solution)/shard_map/ppermute | solution.py:530
  102.6 3.0 %collective-permute-done.32.refs_3_.refs_4_ = bf16[432,256]{1,0:T(8,128)(2,1)S(1)} collective-permute-done((bf16[432,256]{1,0:T(8,128)(2,1)S(1)}, bf16[432,256]{1,0:T(8,128)(2,1)S(1)}, u32[]{:S(2)}, u32[]{:S(2)}) %collective-permute-start.32) | collective-permute-done | bytes 221216 | tf_op jit(solution)/shard_map/ppermute | solution.py:530
  105.6 4.2 %collective-permute-done.31.refs_2_.refs_3_ = bf16[432,256]{1,0:T(8,128)(2,1)S(1)} collective-permute-done((bf16[432,256]{1,0:T(8,128)(2,1)S(1)}, bf16[432,256]{1,0:T(8,128)(2,1)S(1)}, u32[]{:S(2)}, u32[]{:S(2)}) %collective-permute-start.31) | collective-permute-done | bytes 221216 | tf_op jit(solution)/shard_map/ppermute | solution.py:530
  110.8 3.0 %collective-permute-start.33 = (bf16[4,432,256]{2,1,0:T(8,128)(2,1)S(1)}, bf16[4,432,256]{2,1,0:T(8,128)(2,1)S(1)}, u32[]{:S(2)}, u32[]{:S(2)}) collective-permute-start(bf16[4,432,256]{2,1,0:T(8,128)(2,1)S(1)} %shard_map.120), channel_id=1, source_target_pairs={{0,1},{1,0},{2,3},{3,2},{4,5},{5,4},{6,7},{7,6},{8,9},{9,8},{10,11... | collective-permute-start | bytes 2654216 | tf_op jit(solution)/shard_map/ppermute | solution.py:530
  115.9 2.0 %shard_map.121 = (f32[8,288,256]{2,1,0:T(8,128)}, f32[8,144,256]{2,1,0:T(8,128)}) custom-call(s32[1]{0:T(128)} %bitcast.refs_0_, bf16[432,256]{1,0:T(8,128)(2,1)S(1)} %shard_map.119.refs_0_.refs_1_, bf16[432,256]{1,0:T(8,128)(2,1)S(1)} %collective-permute-done.30.refs_1_.refs_2_, bf16[432,256]{1,0:T(8,128)(2,1)S(1)} %collective-permute-done.31.refs_2_.refs_3_, ...), custom_call_target="tpu_custom_call" | custom-call | bytes 5308420 | tf_op jit(solution)/shard_map/pallas_call | solution.py:29
  (99 shorter events, 36.6 us)
Async XLA Ops:
  6.3 7.7 %collective-permute-start.3 = (bf16[384,128]{1,0:T(8,128)(2,1)S(1)}, bf16[384,128]{1,0:T(8,128)(2,1)S(1)}, u32[]{:S(2)}, u32[]{:S(2)}) collective-permute-start(bf16[384,128]{1,0:T(8,128)(2,1)S(1)} %get-tuple-element.48), channel_id=1, source_target_pairs={{0,4},{1,5},{2,14},{3,15},{4,0},{5,1},{14,2},{15,3},{16,20},{17,21... | collective-permute-start | bytes 294920 | tf_op jit(solution)/shard_map/ppermute | solution.py:541
  10.9 5.3 %collective-permute-start.2 = (bf16[384,128]{1,0:T(8,128)(2,1)S(1)}, bf16[384,128]{1,0:T(8,128)(2,1)S(1)}, u32[]{:S(2)}, u32[]{:S(2)}) collective-permute-start(bf16[384,128]{1,0:T(8,128)(2,1)S(1)} %get-tuple-element.43.refs_2_), channel_id=1, source_target_pairs={{0,12},{1,13},{2,6},{3,7},{4,8},{5,9},{6,2},{7,3},{8,4},{9,5},{10,... | collective-permute-start | bytes 294920 | tf_op jit(solution)/shard_map/ppermute | solution.py:541
  19.1 8.7 %collective-permute-start.4 = (f32[2,256]{1,0:T(2,128)S(1)}, f32[2,256]{1,0:T(2,128)S(1)}, u32[]{:S(2)}, u32[]{:S(2)}) collective-permute-start(f32[2,256]{1,0:T(2,128)S(1)} %get-tuple-element.49.refs_0_), channel_id=1, source_target_pairs={{0,1},{1,0},{2,3},{3,2},{4,5},{5,4},{6,7},{7,6},{8,9},{9,8},{10,11... | collective-permute-start | bytes 6152 | tf_op jit(solution)/shard_map/ppermute | solution.py:530
  27.8 4.3 %collective-permute-start.8 = (f32[2,256]{1,0:T(2,128)S(1)}, f32[2,256]{1,0:T(2,128)S(1)}, u32[]{:S(2)}, u32[]{:S(2)}) collective-permute-start(f32[2,256]{1,0:T(2,128)S(1)} %shard_map.106.refs_0_), channel_id=1, source_target_pairs={{0,14},{2,12},{4,10},{6,8},{8,6},{10,4},{12,2},{14,0},{16,30},{18,... | collective-permute-start | bytes 6152 | tf_op jit(solution)/shard_map/ppermute | solution.py:549
  28.4 4.3 %collective-permute-start.7 = (f32[2,256]{1,0:T(2,128)S(1)}, f32[2,256]{1,0:T(2,128)S(1)}, u32[]{:S(2)}, u32[]{:S(2)}) collective-permute-start(f32[2,256]{1,0:T(2,128)S(1)} %shard_map.106.refs_0_), channel_id=1, source_target_pairs={{0,10},{1,13},{2,8},{3,15},{4,14},{5,9},{6,12},{7,11},{8,2},{9,5},... | collective-permute-start | bytes 6152 | tf_op jit(solution)/shard_map/ppermute | solution.py:549
  33.0 13.9 %collective-permute-start.9 = (f32[5,2,256]{2,1,0:T(2,128)S(1)}, f32[5,2,256]{2,1,0:T(2,128)S(1)}, u32[]{:S(2)}, u32[]{:S(2)}) collective-permute-start(f32[5,2,256]{2,1,0:T(2,128)S(1)} %shard_map.107.refs_2_), channel_id=1, source_target_pairs={{0,1},{1,0},{2,3},{3,2},{4,5},{5,4},{6,7},{7,6},{8,9},{9,8},{10,11... | collective-permute-start | bytes 30728 | tf_op jit(solution)/shard_map/ppermute | solution.py:530
  53.9 18.7 %collective-permute-start.17 = (bf16[288,256]{1,0:T(8,128)(2,1)S(1)}, bf16[288,256]{1,0:T(8,128)(2,1)S(1)}, u32[]{:S(2)}, u32[]{:S(2)}) collective-permute-start(bf16[288,256]{1,0:T(8,128)(2,1)S(1)} %get-tuple-element.62), channel_id=1, source_target_pairs={{0,2},{1,3},{2,0},{3,1},{4,6},{5,7},{6,4},{7,5},{8,10},{9,11},{10,... | collective-permute-start | bytes 442376 | tf_op jit(solution)/shard_map/ppermute | solution.py:530
  54.0 18.6 %collective-permute-start.18 = (bf16[288,256]{1,0:T(8,128)(2,1)S(1)}, bf16[288,256]{1,0:T(8,128)(2,1)S(1)}, u32[]{:S(2)}, u32[]{:S(2)}) collective-permute-start(bf16[288,256]{1,0:T(8,128)(2,1)S(1)} %get-tuple-element.63), channel_id=1, source_target_pairs={{0,16},{1,17},{2,18},{3,19},{4,20},{5,21},{6,22},{7,23},{8,24},{9,... | collective-permute-start | bytes 442376 | tf_op jit(solution)/shard_map/ppermute | solution.py:530
  55.2 17.3 %collective-permute-start.19 = (bf16[288,256]{1,0:T(8,128)(2,1)S(1)}, bf16[288,256]{1,0:T(8,128)(2,1)S(1)}, u32[]{:S(2)}, u32[]{:S(2)}) collective-permute-start(bf16[288,256]{1,0:T(8,128)(2,1)S(1)} %get-tuple-element.64), channel_id=1, source_target_pairs={{0,18},{1,19},{2,16},{3,17},{4,22},{5,23},{6,20},{7,21},{8,26},{9,... | collective-permute-start | bytes 442376 | tf_op jit(solution)/shard_map/ppermute | solution.py:530
  59.1 4.3 %collective-permute-start.14 = (f32[2,256]{1,0:T(2,128)S(1)}, f32[2,256]{1,0:T(2,128)S(1)}, u32[]{:S(2)}, u32[]{:S(2)}) collective-permute-start(f32[2,256]{1,0:T(2,128)S(1)} %shard_map.111.refs_0_.refs_3_), channel_id=1, source_target_pairs={{0,10},{1,13},{2,8},{3,15},{4,14},{5,9},{6,12},{7,11},{8,2},{9,5},... | collective-permute-start | bytes 6152 | tf_op jit(solution)/shard_map/ppermute | solution.py:549
  66.1 6.5 %collective-permute-start.16 = (f32[5,2,256]{2,1,0:T(2,128)S(1)}, f32[5,2,256]{2,1,0:T(2,128)S(1)}, u32[]{:S(2)}, u32[]{:S(2)}) collective-permute-start(f32[5,2,256]{2,1,0:T(2,128)S(1)} %shard_map.112.refs_2_), channel_id=1, source_target_pairs={{0,1},{1,0},{2,3},{3,2},{4,5},{5,4},{6,7},{7,6},{8,9},{9,8},{10,11... | collective-permute-start | bytes 30728 | tf_op jit(solution)/shard_map/ppermute | solution.py:530
  75.7 6.9 %collective-permute-start.22 = (bf16[288,256]{1,0:T(8,128)(2,1)S(1)}, bf16[288,256]{1,0:T(8,128)(2,1)S(1)}, u32[]{:S(2)}, u32[]{:S(2)}) collective-permute-start(bf16[288,256]{1,0:T(8,128)(2,1)S(1)} %shard_map.114.refs_13_.refs_0_), channel_id=1, source_target_pairs={{0,12},{1,13},{2,14},{3,15},{4,8},{5,9},{6,10},{7,11},{8,4},{9,5},... | collective-permute-start | bytes 442376 | tf_op jit(solution)/shard_map/ppermute | solution.py:530
  77.5 12.8 %collective-permute-start.21 = (bf16[288,256]{1,0:T(8,128)(2,1)S(1)}, bf16[288,256]{1,0:T(8,128)(2,1)S(1)}, u32[]{:S(2)}, u32[]{:S(2)}) collective-permute-start(bf16[288,256]{1,0:T(8,128)(2,1)S(1)} %shard_map.114.refs_13_.refs_0_), channel_id=1, source_target_pairs={{0,8},{1,9},{2,10},{3,11},{4,12},{5,13},{6,14},{7,15},{8,0},{9,1},... | collective-permute-start | bytes 442376 | tf_op jit(solution)/shard_map/ppermute | solution.py:530
  77.5 12.8 %collective-permute-start.20 = (bf16[288,256]{1,0:T(8,128)(2,1)S(1)}, bf16[288,256]{1,0:T(8,128)(2,1)S(1)}, u32[]{:S(2)}, u32[]{:S(2)}) collective-permute-start(bf16[288,256]{1,0:T(8,128)(2,1)S(1)} %shard_map.114.refs_13_.refs_0_), channel_id=1, source_target_pairs={{0,4},{1,5},{2,6},{3,7},{4,0},{5,1},{6,2},{7,3},{8,12},{9,13},{10,... | collective-permute-start | bytes 442376 | tf_op jit(solution)/shard_map/ppermute | solution.py:530
  79.5 10.9 %collective-permute-start.25 = (bf16[160,256]{1,0:T(8,128)(2,1)S(1)}, bf16[160,256]{1,0:T(8,128)(2,1)S(1)}, u32[]{:S(2)}, u32[]{:S(2)}) collective-permute-start(bf16[160,256]{1,0:T(8,128)(2,1)S(1)} %get-tuple-element.71), channel_id=1, source_target_pairs={{0,16},{1,17},{2,18},{3,19},{4,20},{5,21},{6,22},{7,23},{8,24},{9,... | collective-permute-start | bytes 245768 | tf_op jit(solution)/shard_map/ppermute | solution.py:530
  80.7 9.6 %collective-permute-start.24 = (bf16[144,256]{1,0:T(8,128)(2,1)S(1)}, bf16[144,256]{1,0:T(8,128)(2,1)S(1)}, u32[]{:S(2)}, u32[]{:S(2)}) collective-permute-start(bf16[144,256]{1,0:T(8,128)(2,1)S(1)} %get-tuple-element.70), channel_id=1, source_target_pairs={{0,2},{1,3},{2,0},{3,1},{4,6},{5,7},{6,4},{7,5},{8,10},{9,11},{10,... | collective-permute-start | bytes 221192 | tf_op jit(solution)/shard_map/ppermute | solution.py:530
  82.6 7.7 %collective-permute-start.26 = (bf16[144,256]{1,0:T(8,128)(2,1)S(1)}, bf16[144,256]{1,0:T(8,128)(2,1)S(1)}, u32[]{:S(2)}, u32[]{:S(2)}) collective-permute-start(bf16[144,256]{1,0:T(8,128)(2,1)S(1)} %get-tuple-element.72), channel_id=1, source_target_pairs={{0,18},{1,19},{2,16},{3,17},{4,22},{5,23},{6,20},{7,21},{8,26},{9,... | collective-permute-start | bytes 221192 | tf_op jit(solution)/shard_map/ppermute | solution.py:530
  90.4 7.7 %collective-permute-start.29 = (bf16[144,256]{1,0:T(8,128)(2,1)S(1)}, bf16[144,256]{1,0:T(8,128)(2,1)S(1)}, u32[]{:S(2)}, u32[]{:S(2)}) collective-permute-start(bf16[144,256]{1,0:T(8,128)(2,1)S(1)} %get-tuple-element.73.refs_4_), channel_id=1, source_target_pairs={{0,12},{1,13},{2,14},{3,15},{4,8},{5,9},{6,10},{7,11},{8,4},{9,5},... | collective-permute-start | bytes 221192 | tf_op jit(solution)/shard_map/ppermute | solution.py:530
  92.1 6.0 %collective-permute-start.28 = (bf16[144,256]{1,0:T(8,128)(2,1)S(1)}, bf16[144,256]{1,0:T(8,128)(2,1)S(1)}, u32[]{:S(2)}, u32[]{:S(2)}) collective-permute-start(bf16[144,256]{1,0:T(8,128)(2,1)S(1)} %get-tuple-element.73.refs_4_), channel_id=1, source_target_pairs={{0,8},{1,9},{2,10},{3,11},{4,12},{5,13},{6,14},{7,15},{8,0},{9,1},... | collective-permute-start | bytes 221192 | tf_op jit(solution)/shard_map/ppermute | solution.py:530
  92.9 5.3 %collective-permute-start.27 = (bf16[144,256]{1,0:T(8,128)(2,1)S(1)}, bf16[144,256]{1,0:T(8,128)(2,1)S(1)}, u32[]{:S(2)}, u32[]{:S(2)}) collective-permute-start(bf16[144,256]{1,0:T(8,128)(2,1)S(1)} %get-tuple-element.73.refs_4_), channel_id=1, source_target_pairs={{0,4},{1,5},{2,6},{3,7},{4,0},{5,1},{6,2},{7,3},{8,12},{9,13},{10,... | collective-permute-start | bytes 221192 | tf_op jit(solution)/shard_map/ppermute | solution.py:530
  99.7 6.0 %collective-permute-start.32 = (bf16[432,256]{1,0:T(8,128)(2,1)S(1)}, bf16[432,256]{1,0:T(8,128)(2,1)S(1)}, u32[]{:S(2)}, u32[]{:S(2)}) collective-permute-start(bf16[432,256]{1,0:T(8,128)(2,1)S(1)} %shard_map.119.refs_0_.refs_1_), channel_id=1, source_target_pairs={{0,18},{1,19},{2,16},{3,17},{4,22},{5,23},{6,20},{7,21},{8,26},{9,... | collective-permute-start | bytes 663560 | tf_op jit(solution)/shard_map/ppermute | solution.py:530
  102.3 7.6 %collective-permute-start.31 = (bf16[432,256]{1,0:T(8,128)(2,1)S(1)}, bf16[432,256]{1,0:T(8,128)(2,1)S(1)}, u32[]{:S(2)}, u32[]{:S(2)}) collective-permute-start(bf16[432,256]{1,0:T(8,128)(2,1)S(1)} %shard_map.119.refs_0_.refs_1_), channel_id=1, source_target_pairs={{0,16},{1,17},{2,18},{3,19},{4,20},{5,21},{6,22},{7,23},{8,24},{9,... | collective-permute-start | bytes 663560 | tf_op jit(solution)/shard_map/ppermute | solution.py:530
  102.5 8.3 %collective-permute-start.30 = (bf16[432,256]{1,0:T(8,128)(2,1)S(1)}, bf16[432,256]{1,0:T(8,128)(2,1)S(1)}, u32[]{:S(2)}, u32[]{:S(2)}) collective-permute-start(bf16[432,256]{1,0:T(8,128)(2,1)S(1)} %shard_map.119.refs_0_.refs_1_), channel_id=1, source_target_pairs={{0,2},{1,3},{2,0},{3,1},{4,6},{5,7},{6,4},{7,5},{8,10},{9,11},{10,... | collective-permute-start | bytes 663560 | tf_op jit(solution)/shard_map/ppermute | solution.py:530
  110.8 5.0 %collective-permute-start.33 = (bf16[4,432,256]{2,1,0:T(8,128)(2,1)S(1)}, bf16[4,432,256]{2,1,0:T(8,128)(2,1)S(1)}, u32[]{:S(2)}, u32[]{:S(2)}) collective-permute-start(bf16[4,432,256]{2,1,0:T(8,128)(2,1)S(1)} %shard_map.120), channel_id=1, source_target_pairs={{0,1},{1,0},{2,3},{3,2},{4,5},{5,4},{6,7},{7,6},{8,9},{9,8},{10,11... | collective-permute-start | bytes 2654216 | tf_op jit(solution)/shard_map/ppermute | solution.py:530
  (25 other events, 107.0 us)

commit v2 on v1

--- a/solution.py
+++ b/solution.py
@@ -315,17 +315,8 @@
     )
 
 
-def space_sum(core_ref, own_ref, pair_ref):
-    even = core_ref[0] == 0
-    values = [own_ref[0]]
-    for k in range(1, own_ref.shape[0]):
-        values.append(jnp.where(even, own_ref[k], pair_ref[k]))
-        values.append(jnp.where(even, pair_ref[k], own_ref[k]))
-    return tree_sum(values[:-1])
-
-
-def add_kernel(one_ref, two_ref, out_ref):
-    out_ref[...] = one_ref[...] + two_ref[...]
+def add_kernel(*refs):
+    refs[-1][...] = tree_sum([r[...] for r in refs[:-1]])
 
 
 def stack_kernel(*refs):
@@ -333,9 +324,9 @@
         refs[-1][k] = ref[...]
 
 
-def normalize(norm_count, core_ref, own_ref, pair_ref, z_ref, act_grad_ref, gain_ref, bias_ref, act_ref, pre_ref, sums_ref, moments_ref):
+def activate_kernel(norm_count, own_ref, pair_ref, z_ref, act_grad_ref, gain_ref, bias_ref, act_ref, pre_ref, sums_ref, moments_ref):
     cells, depth = z_ref.shape
-    total = group_sum(space_sum(core_ref, own_ref, pair_ref), depth) / norm_count
+    total = group_sum(own_ref[...] + pair_ref[...], depth) / norm_count
     mean = total[0:1, :]
     inv_std = 1.0 / jnp.sqrt(total[1:2, :] - mean * mean + 1e-05)
     moments_ref[0:1, :] = mean
@@ -361,9 +352,7 @@
     sums_ref[1:2, :] = jnp.sum(two, axis=0, keepdims=True)
 
 
-def activate_kernel(norm_count, rows, cols, me_ref, *refs):
-    *plain, taps_ref, pre_ref, sums_ref, moments_ref, out_ref, act_ref, whole = refs
-    normalize(norm_count, *plain, act_ref, pre_ref, sums_ref, moments_ref)
+def second_kernel(rows, cols, place_ref, act_ref, taps_ref, keep_ref, send_ref, whole):
     cells = rows * cols
     depth = act_ref.shape[1]
     act_t = act_ref[...].T
@@ -372,22 +361,23 @@
             first = (2 - a) * cols
             tap = a * 3 + b
             whole[tap * depth : (tap + 1) * depth, :] = dot(act_t, taps_ref[b, first : first + cells, :])
-    spread(me_ref, whole, out_ref)
-
-
-def spread(me_ref, whole, out_ref):
-    size = out_ref.shape[1]
-    for slot in range(8):
-        first = pl.multiple_of((me_ref[0] ^ slot) * size, 16)
-        out_ref[slot] = whole[pl.ds(first, size), :]
-
-
-def conv_grad_kernel(norm_count, rows, cols, me_ref, *refs):
-    count = 3
-    sums = refs[:count]
-    place_ref, z_ref, pre_ref, moments_ref, gain_ref, bias_ref, z_rim_ref, act_rim_ref, t_ref, grad_ref, rim_ref, total_ref, out_ref, whole = refs[count:]
+    spread(place_ref, whole, keep_ref, send_ref)
+
+
+def spread(place_ref, whole, keep_ref, send_ref):
+    size = keep_ref.shape[1]
+    for slot in range(4):
+        first = pl.multiple_of((place_ref[5] ^ slot) * size, 16)
+        keep_ref[slot] = whole[pl.ds(first, size), :]
+        first = pl.multiple_of((place_ref[5] ^ slot ^ 4) * size, 16)
+        send_ref[slot] = whole[pl.ds(first, size), :].astype(BF16)
+
+
+def conv_grad_kernel(norm_count, rows, cols, place_ref, own_ref, pair_ref, *refs):
+    z_ref, pre_ref, moments_ref, gain_ref, bias_ref, z_rim_ref, act_rim_ref, t_ref = refs[:8]
+    grad_ref, rim_ref, total_ref, keep_ref, send_ref, whole = refs[8:]
     cells, depth = z_ref.shape
-    total = space_sum(*sums)
+    total = own_ref[...] + pair_ref[...]
     total_ref[...] = total
     gain = gain_ref[...]
     means = group_sum(total * gain, depth) / norm_count
@@ -421,10 +411,10 @@
 
     size = t_ref.shape[0] // 3
     lax.fori_loop(0, 3, product, 0)
-    spread(me_ref, whole, out_ref)
-
-
-def input_kernel(rows, cols, d_ref, rim_ref, w_ref, out_ref, plain, shifted, w_t, wide, mixed):
+    spread(place_ref, whole, keep_ref, send_ref)
+
+
+def input_kernel(rows, cols, d_ref, rim_ref, w_ref, out_ref, done_ref, plain, shifted, w_t, wide, mixed):
     cells = rows * cols
     cin = out_ref.shape[2]
     depth = d_ref.shape[1]
@@ -439,6 +429,7 @@
         shifted[p * cols : (p + 1) * cols, :] = wide[first + 1 : first + 1 + cols, :].astype(BF16)
     for place, tap in enumerate((4, 5, 7, 8, 3, 6, 1, 2, 0)):
         w_t[:, place * cin : (place + 1) * cin] = w_ref[tap * cin : (tap + 1) * cin, :].T
+    done_ref[...] = jnp.zeros(done_ref.shape, F32)
     step = CHUNK // cols
 
     def chunk(i, carry):
@@ -463,6 +454,20 @@
     lax.fori_loop(0, rows // step, chunk, 0)
 
 
+def first_split_kernel(place_ref, mine_ref, other_ref, keep_ref, send_ref):
+    even = place_ref[4] == 0
+    none, along_y, along_x, both = [mine_ref[k] + other_ref[k].astype(F32) for k in range(4)]
+    keep_ref[0] = none
+    keep_ref[1] = jnp.where(even, along_y, along_x)
+    send_ref[0] = jnp.where(even, along_x, along_y).astype(BF16)
+    send_ref[1] = both.astype(BF16)
+
+
+def second_split_kernel(mine_ref, other_ref, keep_ref, send_ref):
+    keep_ref[...] = mine_ref[0] + other_ref[0].astype(F32)
+    send_ref[...] = (mine_ref[1] + other_ref[1].astype(F32)).astype(BF16)
+
+
 def half_kernel(slots_ref, other_ref, *refs):
     own_ref, one_ref, two_ref, three_ref = refs[-4:]
     rows = slots_ref.shape[1]
@@ -499,14 +504,16 @@
     out_ref[rows:, :] = tree_sum([r[...].astype(F32) for r in first]).astype(BF16)
 
 
-def first_total_kernel(own_ref, one_ref, two_ref, three_ref, pair_ref, out_ref, both_ref):
+def first_total_kernel(own_ref, one_ref, two_ref, three_ref, pair_ref, out_ref, bias_ref, gain_ref):
     total_kernel(own_ref, one_ref, two_ref, three_ref, out_ref)
     rows = out_ref.shape[0]
-    both_ref[...] = from_parts(three_parts(pair_ref[...])) + from_parts(two_ref[rows:, :])
-
-
-def gather_kernel(me_ref, *refs):
-    me = me_ref[0]
+    both = from_parts(three_parts(pair_ref[...])) + from_parts(two_ref[rows:, :])
+    bias_ref[...] = both[0:1, :]
+    gain_ref[...] = both[1:2, :]
+
+
+def gather_kernel(place_ref, *refs):
+    me = place_ref[5]
     *own, other_ref, second_ref, first_ref = refs
     rows = second_ref.shape[1]
     for slot in range(4):
@@ -540,15 +547,18 @@
                 pairs.append((t, (r * TCOLS + c - TCOLS - 2) % tiles))
         return lax.ppermute(value, "space", pairs)
 
-    def space_sums(value, after=()):
-        (near,) = call(add_kernel, [shape(value.shape, F32)], [value, flip(value, 1)], after=after)
-        parts = [near]
-        chips = tiles // 2
-        for k in range(1, chips, 2):
-            pairs = [(i, i ^ (2 * (k + i % 2))) for i in range(devices) if k + i % 2 < chips]
-            parts.append(lax.ppermute(near, axes, pairs))
-        (own,) = call(stack_kernel, [shape((len(parts),) + near.shape, F32)], parts)
-        return near, parts, [core, own, flip(own, 1)]
+    def added(parts, after=()):
+        return call(add_kernel, [shape(parts[0].shape, F32)], parts, after=after)[0]
+
+    def fetched(value, after=()):
+        parts = [value] + [flip(value, 2 * k) for k in (1, 2, 3)]
+        for k in range(3, tiles.bit_length() - 1):
+            total = added(parts, after)
+            parts, after = [total, flip(total, 1 << k)], ()
+        return parts
+
+    def crossed(value, even, odd):
+        return lax.ppermute(value, axes, [(i, i ^ (odd if i % 2 else even)) for i in range(devices)])
 
     def along(value, size, step):
         return [value] + [flip(value, step * k) for k in range(1, size)]
@@ -558,11 +568,11 @@
             return parts[0]
         return call(total_kernel, [shape(parts[0].shape, BF16)], parts, after=after)[0]
 
-    def halved(slots, more=()):
-        part = slots.shape[1:]
+    def halved(slots, more=(), after=()):
+        part = slots[0].shape[1:]
         longer = (part[0] + 16 * len(more), part[1])
         outs = [shape(part, F32), shape(part, BF16), shape(longer, BF16), shape(part, BF16)]
-        return call(half_kernel, outs, [slots, flip(slots[4:8], 1), *more])
+        return call(half_kernel, outs, [slots[0], flip(slots[1], 1), *more], after=after)
 
     masks = [0, 2, tiles, tiles + 2]
 
@@ -577,12 +587,10 @@
         return own + [flip(stacked, 1)]
 
     space = lax.axis_index("space")
-    me = (space % 2) * 4 + (lax.axis_index("dp") % 2) * 2 + (space // 2) % 2
-    me = me.astype(jnp.int32).reshape(1)
-    core = (space % 2).astype(jnp.int32).reshape(1)
     spot = (space + TCOLS + 2) % tiles
     column, row = spot % TCOLS, spot // TCOLS
-    place = jnp.stack([column % 2, row % 2, column < TCOLS - 1, row < tile_rows - 1]).astype(jnp.int32)
+    me = (space % 2) * 4 + (lax.axis_index("dp") % 2) * 2 + (space // 2) % 2
+    place = jnp.stack([column % 2, row % 2, column < TCOLS - 1, row < tile_rows - 1, space % 2, me]).astype(jnp.int32)
     x = images[0, 0]
     g3 = upstream[0, 0]
     w1 = first_weight.reshape(9 * cin, depth)
@@ -661,7 +669,7 @@
         smem=1,
         flops=2 * 80 * 3 * cin * depth,
     )
-    _, _, stats = space_sums(stats)
+    stats = fetched(added([stats, flip(stats, 1)]))
     taps, act_grad, act_rim = call(
         functools.partial(upstream_kernel, rows, cols),
         [shape((3, cells + 2 * cols, depth), BF16), shape((cells, depth), F32), shape((rim, depth), F32)],
@@ -675,55 +683,72 @@
         ],
         flops=2 * cells * 9 * depth * depth,
     )
-    pre_grad, sums, moments, second_slots = call(
-        functools.partial(activate_kernel, norm_count, rows, cols),
-        [
-            shape((cells, depth), F32),
-            shape((2, depth), F32),
-            shape((2, depth), F32),
-            shape((8, 9 * depth // 8, depth), F32),
-        ],
-        [me] + stats + [z, act_grad, gain, bias, taps],
-        [pltpu.VMEM((cells, depth), BF16), pltpu.VMEM((9 * depth, depth), F32)],
+    activated, pre_grad, sums, moments = call(
+        functools.partial(activate_kernel, norm_count),
+        [shape((cells, depth), BF16), shape((cells, depth), F32), shape((2, depth), F32), shape((2, depth), F32)],
+        stats + [z, act_grad, gain, bias],
+        flops=cells * depth * 30,
+    )
+    other = flip(sums, 1)
+    second_slots = call(
+        functools.partial(second_kernel, rows, cols),
+        [shape((4, 9 * depth // 8, depth), F32), shape((4, 9 * depth // 8, depth), BF16)],
+        [place, activated, taps],
+        [pltpu.VMEM((9 * depth, depth), F32)],
         flops=2 * cells * 9 * depth * depth,
-        smem=2,
-    )
-    second_parts = quartered(halved(second_slots))
-    near, parts, sums = space_sums(sums, second_parts[:1])
+        smem=1,
+    )
+    near = added([sums, other], second_slots[1:])
+    part = second_slots[0].shape[1:]
+    kept, sent = call(
+        first_split_kernel,
+        [shape((2,) + part, F32), shape((2,) + part, BF16)],
+        [place, second_slots[0], flip(second_slots[1], 1)],
+        smem=1,
+        after=[near],
+    )
+    parts = fetched(near, [kept])
+    second_parts = call(
+        second_split_kernel,
+        [shape(part, F32), shape(part, BF16)],
+        [kept, crossed(sent, tiles, 2)],
+        after=parts[:1],
+    )
     (windows,) = call(
         functools.partial(windows_kernel, rows, cols),
         [shape((9 * cin, cells), BF16)],
         [planes, from_left, from_above],
         pads + [pltpu.VMEM((cells, cin), F32)],
         flops=2 * cells * 9 * cin * depth,
-        after=[parts[0]],
-    )
-    second_shard = along(total(along(total(second_parts), dp_size // 2, 2 * tiles)), tiles // 4, 4)
-    conv_grad, grad_rim, sum_pair, first_slots = call(
+        after=second_parts[:1],
+    )
+    second_shard = total([second_parts[0], crossed(second_parts[1], 2, tiles)])
+    pair = along(total(along(second_shard, dp_size // 2, 2 * tiles)), tiles // 4, 4)
+    conv_grad, grad_rim, sum_pair, *first_slots = call(
         functools.partial(conv_grad_kernel, norm_count, rows, cols),
         [
             shape((cells, depth), BF16),
             shape((rim, depth), F32),
             shape((2, depth), F32),
-            shape((8, 9 * cin // 8, depth), F32),
+            shape((4, 9 * cin // 8, depth), F32),
+            shape((4, 9 * cin // 8, depth), BF16),
         ],
-        [me] + sums + [place, z, pre_grad, moments, gain, bias, z_rim, act_rim, windows],
+        [place] + parts + [z, pre_grad, moments, gain, bias, z_rim, act_rim, windows],
         [pltpu.VMEM((9 * cin, depth), F32)],
         flops=2 * cells * 9 * cin * depth,
-        specs=[smem, smem, vmem, vmem, smem] + [vmem] * 8,
-        after=second_shard[:1],
+        smem=1,
+        after=[second_shard],
     )
     first_parts = quartered(halved(first_slots, [sum_pair]))
-    first_shard, sum_pair = call(
+    first_shard, bias_grad, gain_grad = call(
         first_total_kernel,
-        [shape(first_slots.shape[1:], BF16), shape((2, depth), F32)],
+        [shape(first_slots[0].shape[1:], BF16), shape((1, depth), F32), shape((1, depth), F32)],
         first_parts + [sum_pair],
-        after=second_shard[1:],
     )
     first_shard = along(total(along(first_shard, dp_size // 2, 2 * tiles)), tiles // 4, 4)
-    (input_grad,) = call(
+    input_grad, done = call(
         functools.partial(input_kernel, rows, cols),
-        [shape((2 * rows, 2 * cols, cin), BF16)],
+        [shape((2 * rows, 2 * cols, cin), BF16), shape((8, 128), F32)],
         [conv_grad, grad_rim, w1],
         [
             pltpu.VMEM((cells + cols, depth), BF16),
@@ -734,27 +759,28 @@
         ],
         flops=2 * cells * 9 * cin * depth,
     )
-    sizes = second_slots.shape[1], first_slots.shape[1]
+    sizes = second_slots[0].shape[1], first_slots[0].shape[1]
     (shard,) = call(
-        functools.partial(both_kernel, len(second_shard)),
+        functools.partial(both_kernel, len(pair)),
         [shape((sum(sizes), depth), BF16)],
-        second_shard + first_shard,
-        after=[input_grad],
+        pair + first_shard,
+        after=[done],
     )
     for k in range(1, dp_size.bit_length() - 1):
-        sum_pair = sum_pair + flip(sum_pair, tiles << k)
+        bias_grad = bias_grad + flip(bias_grad, tiles << k)
+        gain_grad = gain_grad + flip(gain_grad, tiles << k)
     second_grad, first_grad = call(
         gather_kernel,
         [shape((8, sizes[0], depth), F32), shape((8, sizes[1], depth), F32)],
-        [me] + gathered(quarters(shard)),
+        [place] + gathered(quarters(shard)),
         smem=1,
     )
     return (
         input_grad[None, None],
         first_grad.reshape(first_weight.shape),
         second_grad.reshape(second_weight.shape),
-        sum_pair[1],
-        sum_pair[0],
+        gain_grad.reshape(depth),
+        bias_grad.reshape(depth),
     )
 
 

time: 119 us -> 102 us (0.86)
  starting transfers between devices: 55.4 us -> 42.3 us
  local copies, waits for them, and re-layouts: 9.4 us -> 2.65 us
  Pallas kernels: 22.7 us -> 24.7 us
  waiting for transfers between devices: 29.2 us -> 31.2 us
    ppermute x22 -> x25, waiting for transfers between devices: 20.1 us -> 28.2 us  [flip(): return lax.ppermute(value, axes, [(i, i ^ mask) for i in range(devices)])]
    ppermute x22 -> x25, starting transfers between devices: 42.5 us -> 34.6 us  [flip(): return lax.ppermute(value, axes, [(i, i ^ mask) for i in range(devices)])]
    ppermute x8 -> x2, waiting for transfers between devices: 6.22 us -> 0.01 us  [crossed(): lax.ppermute(value, axes, [(i, i ^ (odd if i % 2 else even)) for i in ran...]
    unnamed x30 -> x14, local copies, waits for them, and re-layouts: 8.72 us -> 2.57 us
    ppermute x8 -> x2, starting transfers between devices: 6.69 us -> 1.41 us  [crossed(): lax.ppermute(value, axes, [(i, i ^ (odd if i % 2 else even)) for i in ran...]
    pallas_call x21 -> x23, Pallas kernels: 22.7 us -> 24.7 us  [call(): pl.pallas_call(body, out_shape=list(outs), grid=grid, in_specs=list(specs...]
  transfers between devices with their start and end apart: 34 -> 31, of which waited for: 16 -> 19; matrix products, arithmetic and copies ran while one was open for 0% -> 0% of each run, Pallas kernels for 9% -> 11%
where the time goes in v2:
time: 102 us
  starting transfers between devices  42.3 us (41%)
  waiting for transfers between devices  31.2 us (31%)
  Pallas kernels  24.7 us (24%)
  local copies, waits for them, and re-layouts  2.65 us (3%)
    ppermute x25, starting transfers between devices, flip(): return lax.ppermute(value, axes, [(i, i ^ mask) for i in range(devices)])  34.6 us
    ppermute x25, waiting for transfers between devices, flip(): return lax.ppermute(value, axes, [(i, i ^ mask) for i in range(devices)])  28.2 us
    pallas_call x23, Pallas kernels, call(): pl.pallas_call(body, out_shape=list(outs), grid=grid, in_specs=list(specs...  24.7 us
    ppermute x4, starting transfers between devices, swapped(): return lax.ppermute(value, 'space', pairs)  6.28 us
    ppermute x4, waiting for transfers between devices, swapped(): return lax.ppermute(value, 'space', pairs)  2.93 us
    unnamed x14, local copies, waits for them, and re-layouts  2.57 us
  transfers between devices with their start and end apart: 31, of which 19 were waited for; matrix products, arithmetic and copies ran while one was open for 0% of the time, Pallas kernels for 11%

profile of v2, /device:TPU:1, one launch (start us, length us, event | category | flops | bytes accessed | tf_op | source)
XLA Modules:
  0.0 101.8 jit_solution(11109046306268064508)
XLA Ops:
  6.3 4.7 %collective-permute-start.3 = (bf16[384,128]{1,0:T(8,128)(2,1)S(1)}, bf16[384,128]{1,0:T(8,128)(2,1)S(1)}, u32[]{:S(2)}, u32[]{:S(2)}) collective-permute-start(bf16[384,128]{1,0:T(8,128)(2,1)S(1)} %get-tuple-element.54), channel_id=1, source_target_pairs={{0,4},{1,5},{2,14},{3,15},{4,0},{5,1},{14,2},{15,3},{16,20},{17,21... | collective-permute-start | bytes 294920 | tf_op jit(solution)/shard_map/ppermute | solution.py:548
  14.0 2.3 %collective-permute-done.2.refs_6_ = bf16[384,128]{1,0:T(8,128)(2,1)S(1)} collective-permute-done((bf16[384,128]{1,0:T(8,128)(2,1)S(1)}, bf16[384,128]{1,0:T(8,128)(2,1)S(1)}, u32[]{:S(2)}, u32[]{:S(2)}) %collective-permute-start.2) | collective-permute-done | bytes 98336 | tf_op jit(solution)/shard_map/ppermute | solution.py:548
  17.3 7.9 %collective-permute-start.4 = (f32[2,256]{1,0:T(2,128)S(1)}, f32[2,256]{1,0:T(2,128)S(1)}, u32[]{:S(2)}, u32[]{:S(2)}) collective-permute-start(f32[2,256]{1,0:T(2,128)S(1)} %get-tuple-element.55.refs_0_), channel_id=1, source_target_pairs={{0,1},{1,0},{2,3},{3,2},{4,5},{5,4},{6,7},{7,6},{8,9},{9,8},{10,11... | collective-permute-start | bytes 6152 | tf_op jit(solution)/shard_map/ppermute | solution.py:537
  26.1 2.4 %collective-permute-start.7 = (f32[2,256]{1,0:T(2,128)S(1)}, f32[2,256]{1,0:T(2,128)S(1)}, u32[]{:S(2)}, u32[]{:S(2)}) collective-permute-start(f32[2,256]{1,0:T(2,128)S(1)} %shard_map.106.refs_0_), channel_id=1, source_target_pairs={{0,6},{1,7},{2,4},{3,5},{4,2},{5,3},{6,0},{7,1},{8,14},{9,15},{10,... | collective-permute-start | bytes 6152 | tf_op jit(solution)/shard_map/ppermute | solution.py:537
  32.1 3.6 %shard_map.108 = (bf16[3,1600,256]{2,1,0:T(8,128)(2,1)S(1)}, f32[1536,256]{1,0:T(8,128)S(1)}, f32[88,256]{1,0:T(8,128)S(1)}) custom-call(bf16[1536,256]{1,0:T(8,128)(2,1)S(1)} %bitcast.27, bf16[192,128]{1,0:T(8,128)(2,1)S(1)} %get-tuple-element.50.refs_2_.refs_1_, bf16[384,128]{1,0:T(8,128)(2,1)S(1)} %get-tuple-element.51.refs_3_.refs_2_, ...), custom_call_target="tpu_custom_call" | custom-call | flops 1811939328 | bytes 6479872 | tf_op jit(solution)/shard_map/pallas_call | solution.py:29
  37.2 2.8 %shard_map.110 = (f32[4,288,256]{2,1,0:T(8,128)S(1)}, bf16[4,288,256]{2,1,0:T(8,128)(2,1)S(1)}) custom-call(s32[6]{0:T(128)S(1)} %stack.35.refs_0_, bf16[1536,256]{1,0:T(8,128)(2,1)S(1)} %get-tuple-element.61.refs_1_, bf16[3,1600,256]{2,1,0:T(8,128)(2,1)S(1)} %get-tuple-element.62.refs_2_), custom_call_target="tpu_custom_call" | custom-call | flops 1811939328 | bytes 5013528 | tf_op jit(solution)/shard_map/pallas_call | solution.py:29
  39.9 2.1 %collective-permute-start.13 = (bf16[4,288,256]{2,1,0:T(8,128)(2,1)S(1)}, bf16[4,288,256]{2,1,0:T(8,128)(2,1)S(1)}, u32[]{:S(2)}, u32[]{:S(2)}) collective-permute-start(bf16[4,288,256]{2,1,0:T(8,128)(2,1)S(1)} %get-tuple-element.63.refs_2_), channel_id=1, source_target_pairs={{0,1},{1,0},{2,3},{3,2},{4,5},{5,4},{6,7},{7,6},{8,9},{9,8},{10,11... | collective-permute-start | bytes 1769480 | tf_op jit(solution)/shard_map/ppermute | solution.py:537
  42.1 1.6 %collective-permute-done.9.refs_1_ = f32[2,256]{1,0:T(2,128)S(1)} collective-permute-done((f32[2,256]{1,0:T(2,128)S(1)}, f32[2,256]{1,0:T(2,128)S(1)}, u32[]{:S(2)}, u32[]{:S(2)}) %collective-permute-start.9) | collective-permute-done | bytes 2080 | tf_op jit(solution)/shard_map/ppermute | solution.py:537
  44.5 2.6 %collective-permute-start.12 = (f32[2,256]{1,0:T(2,128)S(1)}, f32[2,256]{1,0:T(2,128)S(1)}, u32[]{:S(2)}, u32[]{:S(2)}) collective-permute-start(f32[2,256]{1,0:T(2,128)S(1)} %shard_map.111.refs_3_.refs_0_), channel_id=1, source_target_pairs={{0,6},{1,7},{2,4},{3,5},{4,2},{5,3},{6,0},{7,1},{8,14},{9,15},{10,... | collective-permute-start | bytes 6152 | tf_op jit(solution)/shard_map/ppermute | solution.py:537
  48.2 1.7 %collective-permute-done.11.refs_2_ = f32[2,256]{1,0:T(2,128)S(1)} collective-permute-done((f32[2,256]{1,0:T(2,128)S(1)}, f32[2,256]{1,0:T(2,128)S(1)}, u32[]{:S(2)}, u32[]{:S(2)}) %collective-permute-start.11) | collective-permute-done | bytes 2080 | tf_op jit(solution)/shard_map/ppermute | solution.py:537
  51.8 1.9 %collective-permute-start.14 = (f32[2,256]{1,0:T(2,128)S(1)}, f32[2,256]{1,0:T(2,128)S(1)}, u32[]{:S(2)}, u32[]{:S(2)}) collective-permute-start(f32[2,256]{1,0:T(2,128)S(1)} %shard_map.113.refs_2_.refs_1_), channel_id=1, source_target_pairs={{0,8},{1,9},{2,10},{3,11},{4,12},{5,13},{6,14},{7,15},{8,0},{9,1},... | collective-permute-start | bytes 6152 | tf_op jit(solution)/shard_map/ppermute | solution.py:537
  55.1 2.9 %shard_map.117 = (bf16[1536,256]{1,0:T(8,128)(2,1)S(1)}, f32[88,256]{1,0:T(8,128)S(1)}, f32[2,256]{1,0:T(2,128)S(1)}, f32[4,144,256]{2,1,0:T(8,128)S(1)}, bf16[4,144,256]{2,1,0:T(8,128)(2,1)S(1)}) custom-call(s32[6]{0:T(128)S(1)} %stack.35.refs_0_, f32[2,256]{1,0:T(2,128)S(1)} %shard_map.113.refs_2_.refs_1_, f32[2,256]{1,0:T(2,128)S(1)} %collective-permute-done.14.refs_2_, ...), custom_call_target="tpu_custom_call" | custom-call | flops 905969664 | bytes 8636440 | tf_op jit(solution)/shard_map/pallas_call | solution.py:29
  58.0 3.0 %collective-permute-start.20 = (bf16[4,144,256]{2,1,0:T(8,128)(2,1)S(1)}, bf16[4,144,256]{2,1,0:T(8,128)(2,1)S(1)}, u32[]{:S(2)}, u32[]{:S(2)}) collective-permute-start(bf16[4,144,256]{2,1,0:T(8,128)(2,1)S(1)} %get-tuple-element.77), channel_id=1, source_target_pairs={{0,1},{1,0},{2,3},{3,2},{4,5},{5,4},{6,7},{7,6},{8,9},{9,8},{10,11... | collective-permute-start | bytes 884744 | tf_op jit(solution)/shard_map/ppermute | solution.py:537
  61.0 2.5 %collective-permute-start.19 = (bf16[288,256]{1,0:T(8,128)(2,1)S(1)}, bf16[288,256]{1,0:T(8,128)(2,1)S(1)}, u32[]{:S(2)}, u32[]{:S(2)}) collective-permute-start(bf16[288,256]{1,0:T(8,128)(2,1)S(1)} %shard_map.116.refs_11_.refs_0_), channel_id=1, source_target_pairs={{0,12},{1,13},{2,14},{3,15},{4,8},{5,9},{6,10},{7,11},{8,4},{9,5},... | collective-permute-start | bytes 442376 | tf_op jit(solution)/shard_map/ppermute | solution.py:537
  67.8 1.7 %collective-permute-done.23.refs_3_ = bf16[144,256]{1,0:T(8,128)(2,1)S(1)} collective-permute-done((bf16[144,256]{1,0:T(8,128)(2,1)S(1)}, bf16[144,256]{1,0:T(8,128)(2,1)S(1)}, u32[]{:S(2)}, u32[]{:S(2)}) %collective-permute-start.23) | collective-permute-done | bytes 73760 | tf_op jit(solution)/shard_map/ppermute | solution.py:537
  71.5 2.1 %collective-permute-start.24 = (bf16[144,256]{1,0:T(8,128)(2,1)S(1)}, bf16[144,256]{1,0:T(8,128)(2,1)S(1)}, u32[]{:S(2)}, u32[]{:S(2)}) collective-permute-start(bf16[144,256]{1,0:T(8,128)(2,1)S(1)} %get-tuple-element.83.refs_4_), channel_id=1, source_target_pairs={{0,4},{1,5},{2,6},{3,7},{4,0},{5,1},{6,2},{7,3},{8,12},{9,13},{10,... | collective-permute-start | bytes 221192 | tf_op jit(solution)/shard_map/ppermute | solution.py:537
  73.6 4.1 %shard_map.118 = (bf16[96,64,128]{2,1,0:T(8,128)(2,1)}, f32[8,128]{1,0:T(8,128)S(1)}) custom-call(bf16[1536,256]{1,0:T(8,128)(2,1)S(1)} %get-tuple-element.73.refs_0_, f32[88,256]{1,0:T(8,128)S(1)} %get-tuple-element.74.refs_1_, bf16[1152,256]{1,0:T(8,128)(2,1)S(1)} %bitcast.30), custom_call_target="tpu_custom_call" | custom-call | flops 905969664 | bytes 3043328 | tf_op jit(solution)/shard_map/pallas_call | solution.py:29
  77.7 2.5 %collective-permute-done.18.refs_2_ = bf16[288,256]{1,0:T(8,128)(2,1)S(1)} collective-permute-done((bf16[288,256]{1,0:T(8,128)(2,1)S(1)}, bf16[288,256]{1,0:T(8,128)(2,1)S(1)}, u32[]{:S(2)}, u32[]{:S(2)}) %collective-permute-start.18) | collective-permute-done | bytes 147488 | tf_op jit(solution)/shard_map/ppermute | solution.py:537
  80.2 3.2 %collective-permute-done.25.refs_6_ = bf16[144,256]{1,0:T(8,128)(2,1)S(1)} collective-permute-done((bf16[144,256]{1,0:T(8,128)(2,1)S(1)}, bf16[144,256]{1,0:T(8,128)(2,1)S(1)}, u32[]{:S(2)}, u32[]{:S(2)}) %collective-permute-start.25) | collective-permute-done | bytes 73760 | tf_op jit(solution)/shard_map/ppermute | solution.py:537
  86.2 4.4 %collective-permute-done.29.refs_3_.refs_4_ = bf16[432,256]{1,0:T(8,128)(2,1)S(1)} collective-permute-done((bf16[432,256]{1,0:T(8,128)(2,1)S(1)}, bf16[432,256]{1,0:T(8,128)(2,1)S(1)}, u32[]{:S(2)}, u32[]{:S(2)}) %collective-permute-start.29) | collective-permute-done | bytes 221216 | tf_op jit(solution)/shard_map/ppermute | solution.py:537
  90.6 4.0 %collective-permute-done.28.refs_2_.refs_3_ = bf16[432,256]{1,0:T(8,128)(2,1)S(1)} collective-permute-done((bf16[432,256]{1,0:T(8,128)(2,1)S(1)}, bf16[432,256]{1,0:T(8,128)(2,1)S(1)}, u32[]{:S(2)}, u32[]{:S(2)}) %collective-permute-start.28) | collective-permute-done | bytes 221216 | tf_op jit(solution)/shard_map/ppermute | solution.py:537
  94.6 2.0 %collective-permute-done.27.refs_1_.refs_2_ = bf16[432,256]{1,0:T(8,128)(2,1)S(1)} collective-permute-done((bf16[432,256]{1,0:T(8,128)(2,1)S(1)}, bf16[432,256]{1,0:T(8,128)(2,1)S(1)}, u32[]{:S(2)}, u32[]{:S(2)}) %collective-permute-start.27) | collective-permute-done | bytes 221216 | tf_op jit(solution)/shard_map/ppermute | solution.py:537
  97.2 2.1 %collective-permute-done.30.refs_5_ = bf16[4,432,256]{2,1,0:T(8,128)(2,1)S(1)} collective-permute-done((bf16[4,432,256]{2,1,0:T(8,128)(2,1)S(1)}, bf16[4,432,256]{2,1,0:T(8,128)(2,1)S(1)}, u32[]{:S(2)}, u32[]{:S(2)}) %collective-permute-start.30) | collective-permute-done | bytes 884768 | tf_op jit(solution)/shard_map/ppermute | solution.py:537
  99.2 2.6 %shard_map.123 = (f32[8,288,256]{2,1,0:T(8,128)}, f32[8,144,256]{2,1,0:T(8,128)}) custom-call(s32[6]{0:T(128)S(1)} %stack.35.refs_0_, bf16[432,256]{1,0:T(8,128)(2,1)S(1)} %shard_map.121.refs_0_.refs_1_, bf16[432,256]{1,0:T(8,128)(2,1)S(1)} %collective-permute-done.27.refs_1_.refs_2_, bf16[432,256]{1,0:T(8,128)(2,1)S(1)} %collective-permute-done.28.refs_2_.refs_3_, ...), custom_call_target="tpu_custom_call" | custom-call | bytes 5308440 | tf_op jit(solution)/shard_map/pallas_call | solution.py:29
  (76 shorter events, 30.4 us)
Async XLA Ops:
  6.3 7.7 %collective-permute-start.3 = (bf16[384,128]{1,0:T(8,128)(2,1)S(1)}, bf16[384,128]{1,0:T(8,128)(2,1)S(1)}, u32[]{:S(2)}, u32[]{:S(2)}) collective-permute-start(bf16[384,128]{1,0:T(8,128)(2,1)S(1)} %get-tuple-element.54), channel_id=1, source_target_pairs={{0,4},{1,5},{2,14},{3,15},{4,0},{5,1},{14,2},{15,3},{16,20},{17,21... | collective-permute-start | bytes 294920 | tf_op jit(solution)/shard_map/ppermute | solution.py:548
  11.0 5.3 %collective-permute-start.2 = (bf16[384,128]{1,0:T(8,128)(2,1)S(1)}, bf16[384,128]{1,0:T(8,128)(2,1)S(1)}, u32[]{:S(2)}, u32[]{:S(2)}) collective-permute-start(bf16[384,128]{1,0:T(8,128)(2,1)S(1)} %get-tuple-element.49.refs_2_), channel_id=1, source_target_pairs={{0,12},{1,13},{2,6},{3,7},{4,8},{5,9},{6,2},{7,3},{8,4},{9,5},{10,... | collective-permute-start | bytes 294920 | tf_op jit(solution)/shard_map/ppermute | solution.py:548
  17.3 8.7 %collective-permute-start.4 = (f32[2,256]{1,0:T(2,128)S(1)}, f32[2,256]{1,0:T(2,128)S(1)}, u32[]{:S(2)}, u32[]{:S(2)}) collective-permute-start(f32[2,256]{1,0:T(2,128)S(1)} %get-tuple-element.55.refs_0_), channel_id=1, source_target_pairs={{0,1},{1,0},{2,3},{3,2},{4,5},{5,4},{6,7},{7,6},{8,9},{9,8},{10,11... | collective-permute-start | bytes 6152 | tf_op jit(solution)/shard_map/ppermute | solution.py:537
  26.1 3.4 %collective-permute-start.7 = (f32[2,256]{1,0:T(2,128)S(1)}, f32[2,256]{1,0:T(2,128)S(1)}, u32[]{:S(2)}, u32[]{:S(2)}) collective-permute-start(f32[2,256]{1,0:T(2,128)S(1)} %shard_map.106.refs_0_), channel_id=1, source_target_pairs={{0,6},{1,7},{2,4},{3,5},{4,2},{5,3},{6,0},{7,1},{8,14},{9,15},{10,... | collective-permute-start | bytes 6152 | tf_op jit(solution)/shard_map/ppermute | solution.py:537
  31.5 4.3 %collective-permute-start.8 = (f32[2,256]{1,0:T(2,128)S(1)}, f32[2,256]{1,0:T(2,128)S(1)}, u32[]{:S(2)}, u32[]{:S(2)}) collective-permute-start(f32[2,256]{1,0:T(2,128)S(1)} %shard_map.107.refs_0_), channel_id=1, source_target_pairs={{0,8},{1,9},{2,10},{3,11},{4,12},{5,13},{6,14},{7,15},{8,0},{9,1},... | collective-permute-start | bytes 6152 | tf_op jit(solution)/shard_map/ppermute | solution.py:537
  39.9 3.8 %collective-permute-start.13 = (bf16[4,288,256]{2,1,0:T(8,128)(2,1)S(1)}, bf16[4,288,256]{2,1,0:T(8,128)(2,1)S(1)}, u32[]{:S(2)}, u32[]{:S(2)}) collective-permute-start(bf16[4,288,256]{2,1,0:T(8,128)(2,1)S(1)} %get-tuple-element.63.refs_2_), channel_id=1, source_target_pairs={{0,1},{1,0},{2,3},{3,2},{4,5},{5,4},{6,7},{7,6},{8,9},{9,8},{10,11... | collective-permute-start | bytes 1769480 | tf_op jit(solution)/shard_map/ppermute | solution.py:537
  44.4 6.0 %collective-permute-start.15 = (bf16[2,288,256]{2,1,0:T(8,128)(2,1)S(1)}, bf16[2,288,256]{2,1,0:T(8,128)(2,1)S(1)}, u32[]{:S(2)}, u32[]{:S(2)}) collective-permute-start(bf16[2,288,256]{2,1,0:T(8,128)(2,1)S(1)} %get-tuple-element.70), channel_id=1, source_target_pairs={{0,16},{1,3},{2,18},{3,1},{4,20},{5,7},{6,22},{7,5},{8,24},{9,11},... | collective-permute-start | bytes 884744 | tf_op jit(solution)/shard_map/ppermute | solution.py:561
  44.5 3.7 %collective-permute-start.12 = (f32[2,256]{1,0:T(2,128)S(1)}, f32[2,256]{1,0:T(2,128)S(1)}, u32[]{:S(2)}, u32[]{:S(2)}) collective-permute-start(f32[2,256]{1,0:T(2,128)S(1)} %shard_map.111.refs_3_.refs_0_), channel_id=1, source_target_pairs={{0,6},{1,7},{2,4},{3,5},{4,2},{5,3},{6,0},{7,1},{8,14},{9,15},{10,... | collective-permute-start | bytes 6152 | tf_op jit(solution)/shard_map/ppermute | solution.py:537
  47.1 3.2 %collective-permute-start.10 = (f32[2,256]{1,0:T(2,128)S(1)}, f32[2,256]{1,0:T(2,128)S(1)}, u32[]{:S(2)}, u32[]{:S(2)}) collective-permute-start(f32[2,256]{1,0:T(2,128)S(1)} %shard_map.111.refs_3_.refs_0_), channel_id=1, source_target_pairs={{0,2},{1,3},{2,0},{3,1},{4,6},{5,7},{6,4},{7,5},{8,10},{9,11},{10,... | collective-permute-start | bytes 6152 | tf_op jit(solution)/shard_map/ppermute | solution.py:537
  50.4 4.3 %collective-permute-start.16 = (bf16[288,256]{1,0:T(8,128)(2,1)S(1)}, bf16[288,256]{1,0:T(8,128)(2,1)S(1)}, u32[]{:S(2)}, u32[]{:S(2)}) collective-permute-start(bf16[288,256]{1,0:T(8,128)(2,1)S(1)} %get-tuple-element.72), channel_id=1, source_target_pairs={{0,2},{1,17},{2,0},{3,19},{4,6},{5,21},{6,4},{7,23},{8,10},{9,25},... | collective-permute-start | bytes 442376 | tf_op jit(solution)/shard_map/ppermute | solution.py:561
  51.8 3.3 %collective-permute-start.14 = (f32[2,256]{1,0:T(2,128)S(1)}, f32[2,256]{1,0:T(2,128)S(1)}, u32[]{:S(2)}, u32[]{:S(2)}) collective-permute-start(f32[2,256]{1,0:T(2,128)S(1)} %shard_map.113.refs_2_.refs_1_), channel_id=1, source_target_pairs={{0,8},{1,9},{2,10},{3,11},{4,12},{5,13},{6,14},{7,15},{8,0},{9,1},... | collective-permute-start | bytes 6152 | tf_op jit(solution)/shard_map/ppermute | solution.py:537
  58.0 5.5 %collective-permute-start.20 = (bf16[4,144,256]{2,1,0:T(8,128)(2,1)S(1)}, bf16[4,144,256]{2,1,0:T(8,128)(2,1)S(1)}, u32[]{:S(2)}, u32[]{:S(2)}) collective-permute-start(bf16[4,144,256]{2,1,0:T(8,128)(2,1)S(1)} %get-tuple-element.77), channel_id=1, source_target_pairs={{0,1},{1,0},{2,3},{3,2},{4,5},{5,4},{6,7},{7,6},{8,9},{9,8},{10,11... | collective-permute-start | bytes 884744 | tf_op jit(solution)/shard_map/ppermute | solution.py:537
  61.0 10.6 %collective-permute-start.19 = (bf16[288,256]{1,0:T(8,128)(2,1)S(1)}, bf16[288,256]{1,0:T(8,128)(2,1)S(1)}, u32[]{:S(2)}, u32[]{:S(2)}) collective-permute-start(bf16[288,256]{1,0:T(8,128)(2,1)S(1)} %shard_map.116.refs_11_.refs_0_), channel_id=1, source_target_pairs={{0,12},{1,13},{2,14},{3,15},{4,8},{5,9},{6,10},{7,11},{8,4},{9,5},... | collective-permute-start | bytes 442376 | tf_op jit(solution)/shard_map/ppermute | solution.py:537
  63.6 3.6 %collective-permute-start.21 = (bf16[144,256]{1,0:T(8,128)(2,1)S(1)}, bf16[144,256]{1,0:T(8,128)(2,1)S(1)}, u32[]{:S(2)}, u32[]{:S(2)}) collective-permute-start(bf16[144,256]{1,0:T(8,128)(2,1)S(1)} %get-tuple-element.80), channel_id=1, source_target_pairs={{0,2},{1,3},{2,0},{3,1},{4,6},{5,7},{6,4},{7,5},{8,10},{9,11},{10,... | collective-permute-start | bytes 221192 | tf_op jit(solution)/shard_map/ppermute | solution.py:537
  64.1 5.4 %collective-permute-start.22 = (bf16[160,256]{1,0:T(8,128)(2,1)S(1)}, bf16[160,256]{1,0:T(8,128)(2,1)S(1)}, u32[]{:S(2)}, u32[]{:S(2)}) collective-permute-start(bf16[160,256]{1,0:T(8,128)(2,1)S(1)} %get-tuple-element.81), channel_id=1, source_target_pairs={{0,16},{1,17},{2,18},{3,19},{4,20},{5,21},{6,22},{7,23},{8,24},{9,... | collective-permute-start | bytes 245768 | tf_op jit(solution)/shard_map/ppermute | solution.py:537
  64.8 4.7 %collective-permute-start.23 = (bf16[144,256]{1,0:T(8,128)(2,1)S(1)}, bf16[144,256]{1,0:T(8,128)(2,1)S(1)}, u32[]{:S(2)}, u32[]{:S(2)}) collective-permute-start(bf16[144,256]{1,0:T(8,128)(2,1)S(1)} %get-tuple-element.82), channel_id=1, source_target_pairs={{0,18},{1,19},{2,16},{3,17},{4,22},{5,23},{6,20},{7,21},{8,26},{9,... | collective-permute-start | bytes 221192 | tf_op jit(solution)/shard_map/ppermute | solution.py:537
  66.3 13.9 %collective-permute-start.18 = (bf16[288,256]{1,0:T(8,128)(2,1)S(1)}, bf16[288,256]{1,0:T(8,128)(2,1)S(1)}, u32[]{:S(2)}, u32[]{:S(2)}) collective-permute-start(bf16[288,256]{1,0:T(8,128)(2,1)S(1)} %shard_map.116.refs_11_.refs_0_), channel_id=1, source_target_pairs={{0,8},{1,9},{2,10},{3,11},{4,12},{5,13},{6,14},{7,15},{8,0},{9,1},... | collective-permute-start | bytes 442376 | tf_op jit(solution)/shard_map/ppermute | solution.py:537
  67.1 13.1 %collective-permute-start.17 = (bf16[288,256]{1,0:T(8,128)(2,1)S(1)}, bf16[288,256]{1,0:T(8,128)(2,1)S(1)}, u32[]{:S(2)}, u32[]{:S(2)}) collective-permute-start(bf16[288,256]{1,0:T(8,128)(2,1)S(1)} %shard_map.116.refs_11_.refs_0_), channel_id=1, source_target_pairs={{0,4},{1,5},{2,6},{3,7},{4,0},{5,1},{6,2},{7,3},{8,12},{9,13},{10,... | collective-permute-start | bytes 442376 | tf_op jit(solution)/shard_map/ppermute | solution.py:537
  70.1 10.2 %collective-permute-start.26 = (bf16[144,256]{1,0:T(8,128)(2,1)S(1)}, bf16[144,256]{1,0:T(8,128)(2,1)S(1)}, u32[]{:S(2)}, u32[]{:S(2)}) collective-permute-start(bf16[144,256]{1,0:T(8,128)(2,1)S(1)} %get-tuple-element.83.refs_4_), channel_id=1, source_target_pairs={{0,12},{1,13},{2,14},{3,15},{4,8},{5,9},{6,10},{7,11},{8,4},{9,5},... | collective-permute-start | bytes 221192 | tf_op jit(solution)/shard_map/ppermute | solution.py:537
  71.5 11.9 %collective-permute-start.25 = (bf16[144,256]{1,0:T(8,128)(2,1)S(1)}, bf16[144,256]{1,0:T(8,128)(2,1)S(1)}, u32[]{:S(2)}, u32[]{:S(2)}) collective-permute-start(bf16[144,256]{1,0:T(8,128)(2,1)S(1)} %get-tuple-element.83.refs_4_), channel_id=1, source_target_pairs={{0,8},{1,9},{2,10},{3,11},{4,12},{5,13},{6,14},{7,15},{8,0},{9,1},... | collective-permute-start | bytes 221192 | tf_op jit(solution)/shard_map/ppermute | solution.py:537
  71.5 11.9 %collective-permute-start.24 = (bf16[144,256]{1,0:T(8,128)(2,1)S(1)}, bf16[144,256]{1,0:T(8,128)(2,1)S(1)}, u32[]{:S(2)}, u32[]{:S(2)}) collective-permute-start(bf16[144,256]{1,0:T(8,128)(2,1)S(1)} %get-tuple-element.83.refs_4_), channel_id=1, source_target_pairs={{0,4},{1,5},{2,6},{3,7},{4,0},{5,1},{6,2},{7,3},{8,12},{9,13},{10,... | collective-permute-start | bytes 221192 | tf_op jit(solution)/shard_map/ppermute | solution.py:537
  83.5 7.1 %collective-permute-start.29 = (bf16[432,256]{1,0:T(8,128)(2,1)S(1)}, bf16[432,256]{1,0:T(8,128)(2,1)S(1)}, u32[]{:S(2)}, u32[]{:S(2)}) collective-permute-start(bf16[432,256]{1,0:T(8,128)(2,1)S(1)} %shard_map.121.refs_0_.refs_1_), channel_id=1, source_target_pairs={{0,18},{1,19},{2,16},{3,17},{4,22},{5,23},{6,20},{7,21},{8,26},{9,... | collective-permute-start | bytes 663560 | tf_op jit(solution)/shard_map/ppermute | solution.py:537
  84.4 10.2 %collective-permute-start.28 = (bf16[432,256]{1,0:T(8,128)(2,1)S(1)}, bf16[432,256]{1,0:T(8,128)(2,1)S(1)}, u32[]{:S(2)}, u32[]{:S(2)}) collective-permute-start(bf16[432,256]{1,0:T(8,128)(2,1)S(1)} %shard_map.121.refs_0_.refs_1_), channel_id=1, source_target_pairs={{0,16},{1,17},{2,18},{3,19},{4,20},{5,21},{6,22},{7,23},{8,24},{9,... | collective-permute-start | bytes 663560 | tf_op jit(solution)/shard_map/ppermute | solution.py:537
  85.2 11.4 %collective-permute-start.27 = (bf16[432,256]{1,0:T(8,128)(2,1)S(1)}, bf16[432,256]{1,0:T(8,128)(2,1)S(1)}, u32[]{:S(2)}, u32[]{:S(2)}) collective-permute-start(bf16[432,256]{1,0:T(8,128)(2,1)S(1)} %shard_map.121.refs_0_.refs_1_), channel_id=1, source_target_pairs={{0,2},{1,3},{2,0},{3,1},{4,6},{5,7},{6,4},{7,5},{8,10},{9,11},{10,... | collective-permute-start | bytes 663560 | tf_op jit(solution)/shard_map/ppermute | solution.py:537
  (14 other events, 68.1 us)

commit v3 on v2

--- a/solution.py
+++ b/solution.py
@@ -16,7 +16,7 @@
 LONG = 512
 
 
-def call(kernel, outs, args, scratch=(), flops=0, limit=20, smem=0, after=(), specs=None, grid=()):
+def call(kernel, outs, args, scratch=(), flops=0, limit=20, smem=0, after=(), specs=None, grid=(), out_specs=None, aliases=None):
     if specs is None:
         specs = [pl.BlockSpec(memory_space=pltpu.SMEM)] * smem
         specs += [pl.BlockSpec(memory_space=pltpu.VMEM)] * (len(args) - smem)
@@ -31,8 +31,9 @@
         out_shape=list(outs),
         grid=grid,
         in_specs=list(specs) + [pl.BlockSpec(memory_space=pl.ANY)] * len(after),
-        out_specs=[pl.BlockSpec(memory_space=pltpu.VMEM)] * len(outs),
+        out_specs=out_specs or [pl.BlockSpec(memory_space=pltpu.VMEM)] * len(outs),
         scratch_shapes=list(scratch),
+        input_output_aliases=aliases or {},
         compiler_params=pltpu.CompilerParams(vmem_limit_bytes=limit * MIB),
         cost_estimate=pl.CostEstimate(flops=flops, bytes_accessed=moved, transcendentals=0),
     )(*args, *after)
@@ -55,9 +56,28 @@
     return values[0]
 
 
-def pack_kernel(rows, cols, place_ref, x_first, x_last, g_first, g_last, one_ref, two_ref, own_ref, wide, flat):
+def pack_kernel(
+    rows, cols, place_ref, x_ref, g_ref, one_ref, two_ref, own_ref, x_lines, g_lines, x_first, x_last, g_first, g_last, wide, flat, sems,
+):
     cin = x_first.shape[2]
     even = place_ref[0] == 0
+    copies = [
+        pltpu.make_async_copy(source, target, sems.at[k])
+        for k, (source, target) in enumerate(
+            (
+                (x_ref.at[:, 2 * cols - 16 : 2 * cols, :], x_last),
+                (x_ref.at[:, 0:16, :], x_first),
+                (g_ref.at[:, cols - 16 : cols, :], g_last),
+                (g_ref.at[:, 0:16, :], g_first),
+                (x_ref.at[2 * rows - 1], x_lines.at[0]),
+                (x_ref.at[0:2], x_lines.at[1:3]),
+                (g_ref.at[rows - 1], g_lines.at[0]),
+                (g_ref.at[0:2], g_lines.at[1:3]),
+            )
+        )
+    ]
+    for copy in copies:
+        copy.start()
 
     def x_column(ref, index):
         wide[...] = ref[...].astype(F32).reshape(2 * rows * 16, cin)
@@ -71,8 +91,14 @@
         return jnp.concatenate(halves, 0)
 
     size = 2 * rows
-    rightwards = (x_column(x_last, 15), g_column(g_last, 15))
+    copies[0].wait()
+    last = x_column(x_last, 15)
+    copies[1].wait()
     leftwards = (x_column(x_first, 0), x_column(x_first, 1))
+    copies[2].wait()
+    rightwards = (last, g_column(g_last, 15))
+    for copy in copies[3:]:
+        copy.wait()
     for k in range(2):
         part = slice(k * size, (k + 1) * size)
         own_ref[part, :] = rightwards[k].astype(BF16)
@@ -88,11 +114,11 @@
 
 
 def rows_kernel(
-    rows, cols, place_ref, x_last, x_first, g_last, g_first, got_one, got_two,
+    rows, cols, place_ref, x_lines, g_lines, got_one, got_two,
     left_ref, right_ref, one_ref, two_ref, own_ref, x_wide, g_wide,
 ):
-    cin = x_last.shape[2]
-    depth = g_last.shape[2]
+    cin = x_lines.shape[2]
+    depth = g_lines.shape[2]
     even_col = place_ref[0] == 0
     even_row = place_ref[1] == 0
     size = 2 * rows
@@ -123,36 +149,42 @@
         return jnp.concatenate(halves, 0)
 
     line = 2 * cols + 32
-    down = (x_line(x_last[0], 2 * rows - 1), g_line(g_last[0], rows - 1))
-    up = (x_line(x_first[0], 0), x_line(x_first[1], 1))
+    down = (x_line(x_lines[0], 2 * rows - 1), g_line(g_lines[0], rows - 1))
+    up = (x_line(x_lines[1], 0), x_line(x_lines[2], 1))
     for k in range(2):
         part = slice(k * line, (k + 1) * line)
         own_ref[part, :] = down[k].astype(BF16)
         one_ref[part, :] = jnp.where(even_row, down[k], up[k]).astype(BF16)
         two_ref[part, :] = jnp.where(even_row, up[k], down[k]).astype(BF16)
-        both = g_line(g_first[k], k).astype(BF16)
+        both = g_line(g_lines[1 + k], k).astype(BF16)
         one_ref[(k + 2) * line : (k + 3) * line, :] = both
         two_ref[(k + 2) * line : (k + 3) * line, :] = both
 
 
-def planes_kernel(rows, cols, x_ref, planes_ref, wide):
+def planes_kernel(rows, cols, x_ref, planes_ref, wide, held, sems):
     cin = x_ref.shape[2]
     planes_ref[0:cols, :] = jnp.zeros((cols, 6 * cin), BF16)
     step = CHUNK // cols
+    copies = [
+        pltpu.make_async_copy(x_ref.at[2 * step * i : 2 * step * (i + 1)], held.at[i], sems.at[i])
+        for i in range(rows // step)
+    ]
+    for copy in copies:
+        copy.start()
     wide[:, 0:8, :] = jnp.zeros((2 * step, 8, cin), F32)
 
-    def deinterleave(i, carry):
-        base = pl.multiple_of(i * 2 * step, 2 * step)
-        wide[:, 8 : 8 + 2 * cols, :] = x_ref[pl.ds(base, 2 * step)].astype(F32)
-        row = pl.multiple_of((i * step + 1) * cols, cols)
+    def deinterleave(i):
+        copies[i].wait()
+        wide[:, 8 : 8 + 2 * cols, :] = held[i].astype(F32)
+        row = (i * step + 1) * cols
         for parity in range(2):
             for slot, first in enumerate((7, 8, 9)):
                 part = wide[pl.ds(parity, step, stride=2), pl.ds(first, cols, stride=2), :]
                 lane = (parity * 3 + slot) * cin
-                planes_ref[pl.ds(row, CHUNK), lane : lane + cin] = part.reshape(CHUNK, cin).astype(BF16)
-        return carry
-
-    lax.fori_loop(0, rows // step, deinterleave, 0)
+                planes_ref[row : row + CHUNK, lane : lane + cin] = part.reshape(CHUNK, cin).astype(BF16)
+
+    for i in range(rows // step):
+        deinterleave(i)
 
 
 def stride_kernel(rows, cols, planes_ref, w_ref, z_ref):
@@ -242,29 +274,59 @@
         t_ref[lane + 3 * cin : lane + 4 * cin, :] = planes_ref[cols:, lane : lane + cin].T
 
 
+def prepare_kernel(rows, cols, g_hbm, left_ref, right_ref, w_ref, body_ref, w_t_ref, done_ref, wide, rims, g_ref, sem):
+    pitch = cols + 16
+    depth = w_ref.shape[1]
+    size = 2 * rows
+    copy = pltpu.make_async_copy(g_hbm, g_ref, sem)
+    copy.start()
+    for tap in range(9):
+        w_t_ref[tap * depth : (tap + 1) * depth, :] = w_ref[tap * depth : (tap + 1) * depth, :].T
+    done_ref[...] = jnp.zeros(done_ref.shape, F32)
+    for half in range(depth // 128):
+        lanes = slice(half * 128, (half + 1) * 128)
+        rims[0, :, lanes] = left_ref[size + half * rows : size + (half + 1) * rows, :].astype(F32)
+        rims[1, :, lanes] = right_ref[2 * size + half * rows : 2 * size + (half + 1) * rows, :].astype(F32)
+    copy.wait()
+    for p in range(rows):
+        first = p * pitch
+        wide[first + 8 : first + 8 + cols, :] = g_ref[p].astype(F32)
+        wide[first + 7 : first + 8, :] = rims[0, p : p + 1, :]
+        wide[first + 8 + cols : first + 9 + cols, :] = rims[1, p : p + 1, :]
+        for b in (0, 2):
+            body_ref[b, p * cols : (p + 1) * cols, :] = wide[first + 9 - b : first + 9 - b + cols, :].astype(BF16)
+    body_ref[1] = g_ref[...].reshape(body_ref.shape[1:])
+
+
+def window(cols, body_ref, edge_ref, b, first, size):
+    cells = body_ref.shape[1]
+    parts = []
+    if first < cols:
+        parts.append(edge_ref[b, first:cols, :])
+    start, stop = max(first, cols) - cols, min(first + size, cells + cols) - cols
+    parts.append(body_ref[b, start:stop, :])
+    if first + size > cells + cols:
+        parts.append(edge_ref[b, cols : first + size - cells, :])
+    return parts[0] if len(parts) == 1 else jnp.concatenate(parts, 0)
+
+
 def upstream_kernel(
-    rows, cols, g_ref, left_ref, right_ref, own_col_ref, own_row_ref, above_ref, below_ref, w_ref,
-    taps_ref, act_grad_ref, rim_ref, wide, w_t, rims, bottom, side,
+    rows, cols, body_ref, w_t_ref, right_ref, own_col_ref, own_row_ref, above_ref, below_ref,
+    edge_ref, act_grad_ref, rim_ref, wide, bottom, side,
 ):
     pitch = cols + 16
-    depth = g_ref.shape[1]
-    last = (rows + 1) * pitch
+    depth = act_grad_ref.shape[1]
     size = 2 * rows
     line = 2 * cols + 32
-    for p in range(rows):
-        wide[(p + 1) * pitch + 8 : (p + 1) * pitch + 8 + cols, :] = g_ref[p * cols : (p + 1) * cols, :].astype(F32)
     for half in range(depth // 128):
         lanes = slice(half * 128, (half + 1) * 128)
-        own = own_col_ref[size + half * rows : size + (half + 1) * rows, :].astype(F32)
-        rims[0, :, lanes] = left_ref[size + half * rows : size + (half + 1) * rows, :].astype(F32)
-        rims[1, :, lanes] = right_ref[2 * size + half * rows : 2 * size + (half + 1) * rows, :].astype(F32)
         side[0, 8 : 8 + rows, lanes] = right_ref[3 * size + half * rows : 3 * size + (half + 1) * rows, :].astype(F32)
-        side[1, 8 : 8 + rows, lanes] = rims[1, :, lanes]
-        side[2, 8 : 8 + rows, lanes] = own
+        side[1, 8 : 8 + rows, lanes] = right_ref[2 * size + half * rows : 2 * size + (half + 1) * rows, :].astype(F32)
+        side[2, 8 : 8 + rows, lanes] = own_col_ref[size + half * rows : size + (half + 1) * rows, :].astype(F32)
         over = above_ref[line + half * pitch : line + (half + 1) * pitch, :].astype(F32)
         under = below_ref[2 * line + half * pitch : 2 * line + (half + 1) * pitch, :].astype(F32)
         wide[0:pitch, lanes] = over
-        wide[last : last + pitch, lanes] = under
+        wide[pitch : 2 * pitch, lanes] = under
         for b in range(3):
             side[b, 7:8, lanes] = over[9 + cols - b : 10 + cols - b, :]
             side[b, 8 + rows : 9 + rows, lanes] = under[9 + cols - b : 10 + cols - b, :]
@@ -272,37 +334,22 @@
         bottom[1, 0:pitch, lanes] = under
         bottom[2, 0:pitch, lanes] = own_row_ref[line + half * pitch : line + (half + 1) * pitch, :].astype(F32)
     bottom[:, pitch:, :] = jnp.zeros((3, 8, depth), F32)
-    for p in range(rows):
-        first = (p + 1) * pitch + 7
-        wide[first : first + 1, :] = rims[0, p : p + 1, :]
-        wide[first + 1 + cols : first + 2 + cols, :] = rims[1, p : p + 1, :]
-    for r in range(rows + 2):
-        for b in (0, 2):
-            first = r * pitch + 9 - b
-            taps_ref[b, r * cols : (r + 1) * cols, :] = wide[first : first + cols, :].astype(BF16)
-    taps_ref[1, cols : (rows + 1) * cols, :] = g_ref[...]
-    taps_ref[1, 0:cols, :] = wide[8 : 8 + cols, :].astype(BF16)
-    taps_ref[1, (rows + 1) * cols :, :] = wide[last + 8 : last + 8 + cols, :].astype(BF16)
-    for tap in range(9):
-        w_t[tap * depth : (tap + 1) * depth, :] = w_ref[tap * depth : (tap + 1) * depth, :].T
-
-    def convolve(i, carry):
-        row = pl.multiple_of(i * LONG, LONG)
+    for b in range(3):
+        edge_ref[b, 0:cols, :] = wide[9 - b : 9 - b + cols, :].astype(BF16)
+        edge_ref[b, cols:, :] = wide[pitch + 9 - b : pitch + 9 - b + cols, :].astype(BF16)
+    for row in range(0, rows * cols, LONG):
         parts = []
         for a in range(3):
             for b in range(3):
-                parts.append(taps_ref[b, pl.ds(pl.multiple_of(row + (2 - a) * cols, cols), LONG), :])
-        act_grad_ref[pl.ds(row, LONG), :] = dot(jnp.concatenate(parts, 1), w_t[...])
-        return carry
-
-    lax.fori_loop(0, rows * cols // LONG, convolve, 0)
+                parts.append(window(cols, body_ref, edge_ref, b, row + (2 - a) * cols, LONG))
+        act_grad_ref[row : row + LONG, :] = dot(jnp.concatenate(parts, 1), w_t_ref[...])
     parts = []
     for a in range(3):
         for b in range(3):
             low = bottom[a, 9 - b : 17 - b + cols, :]
             beside = side[b, 9 - a : 9 - a + rows, :]
             parts.append(jnp.concatenate([low, beside], 0).astype(BF16))
-    rim_ref[...] = dot(jnp.concatenate(parts, 1), w_t[...])
+    rim_ref[...] = dot(jnp.concatenate(parts, 1), w_t_ref[...])
 
 
 def group_sum(value, depth):
@@ -352,30 +399,28 @@
     sums_ref[1:2, :] = jnp.sum(two, axis=0, keepdims=True)
 
 
-def second_kernel(rows, cols, place_ref, act_ref, taps_ref, keep_ref, send_ref, whole):
+def second_kernel(rows, cols, place_ref, act_ref, body_ref, edge_ref, keep_ref, send_ref):
     cells = rows * cols
     depth = act_ref.shape[1]
     act_t = act_ref[...].T
+    half, size = depth // 2, depth // 8
+    even = place_ref[4] == 0
+    spot = place_ref[5] & 3
     for a in range(3):
         for b in range(3):
             first = (2 - a) * cols
             tap = a * 3 + b
-            whole[tap * depth : (tap + 1) * depth, :] = dot(act_t, taps_ref[b, first : first + cells, :])
-    spread(place_ref, whole, keep_ref, send_ref)
-
-
-def spread(place_ref, whole, keep_ref, send_ref):
-    size = keep_ref.shape[1]
-    for slot in range(4):
-        first = pl.multiple_of((place_ref[5] ^ slot) * size, 16)
-        keep_ref[slot] = whole[pl.ds(first, size), :]
-        first = pl.multiple_of((place_ref[5] ^ slot ^ 4) * size, 16)
-        send_ref[slot] = whole[pl.ds(first, size), :].astype(BF16)
+            both = dot(act_t, window(cols, body_ref, edge_ref, b, first, cells))
+            mine = jnp.where(even, both[0:half, :], both[half:, :])
+            theirs = jnp.where(even, both[half:, :], both[0:half, :]).astype(BF16)
+            for j in range(4):
+                keep_ref[j ^ spot, tap * size : (tap + 1) * size, :] = mine[j * size : (j + 1) * size, :]
+                send_ref[j ^ spot, tap * size : (tap + 1) * size, :] = theirs[j * size : (j + 1) * size, :]
 
 
 def conv_grad_kernel(norm_count, rows, cols, place_ref, own_ref, pair_ref, *refs):
     z_ref, pre_ref, moments_ref, gain_ref, bias_ref, z_rim_ref, act_rim_ref, t_ref = refs[:8]
-    grad_ref, rim_ref, total_ref, keep_ref, send_ref, whole = refs[8:]
+    grad_ref, rim_ref, total_ref, keep_ref, send_ref = refs[8:]
     cells, depth = z_ref.shape
     total = own_ref[...] + pair_ref[...]
     total_ref[...] = total
@@ -404,14 +449,15 @@
     to_below = jnp.where(cell < cols + 8, place_ref[3], 1)
     rim_ref[...] = jnp.where(to_right * to_below == 1, value(z, pre).astype(F32), 0.0)
 
-    def product(i, carry):
-        row = pl.multiple_of(i * size, 128)
-        whole[pl.ds(row, size), :] = dot(t_ref[pl.ds(row, size), :], grad_ref[...])
-        return carry
-
-    size = t_ref.shape[0] // 3
-    lax.fori_loop(0, 3, product, 0)
-    spread(place_ref, whole, keep_ref, send_ref)
+    half = t_ref.shape[0] // 2
+    size = half // 4
+    core = place_ref[4]
+    spot = place_ref[5] & 3
+    theirs = dot(t_ref[pl.ds(pl.multiple_of((1 - core) * half, 16), half), :], grad_ref[...]).astype(BF16)
+    mine = dot(t_ref[pl.ds(pl.multiple_of(core * half, 16), half), :], grad_ref[...])
+    for j in range(4):
+        send_ref[j ^ spot] = theirs[j * size : (j + 1) * size, :]
+        keep_ref[j ^ spot] = mine[j * size : (j + 1) * size, :]
 
 
 def input_kernel(rows, cols, d_ref, rim_ref, w_ref, out_ref, done_ref, plain, shifted, w_t, wide, mixed):
@@ -512,15 +558,22 @@
     gain_ref[...] = both[1:2, :]
 
 
-def gather_kernel(place_ref, *refs):
+def gather_kernel(slots, rows, place_ref, *refs):
     me = place_ref[5]
-    *own, other_ref, second_ref, first_ref = refs
-    rows = second_ref.shape[1]
-    for slot in range(4):
-        second_ref[me ^ slot] = own[slot][0:rows, :].astype(F32)
-        first_ref[me ^ slot] = own[slot][rows:, :].astype(F32)
-        second_ref[me ^ slot ^ 4] = other_ref[slot, 0:rows, :].astype(F32)
-        first_ref[me ^ slot ^ 4] = other_ref[slot, rows:, :].astype(F32)
+    count = len(slots)
+    shards = refs[: 2 * count]
+    second_ref, first_ref, second_stage, first_stage, sems = refs[-5:]
+    copies = []
+    for i, slot in enumerate(slots):
+        for k, where in ((i, me ^ slot), (i + count, me ^ slot ^ 4)):
+            second_stage[k] = shards[k][0:rows, :].astype(F32).reshape(second_stage.shape[1:])
+            first_stage[k] = shards[k][rows:, :].astype(F32)
+            copies.append(pltpu.make_async_copy(second_stage.at[k], second_ref.at[:, where], sems.at[2 * k]))
+            copies.append(pltpu.make_async_copy(first_stage.at[k], first_ref.at[where], sems.at[2 * k + 1]))
+            copies[-2].start()
+            copies[-1].start()
+    for copy in copies:
+        copy.wait()
 
 
 def on_device(dp_size, tiles, images, first_weight, norm_gain, norm_bias, second_weight, upstream):
@@ -582,40 +635,31 @@
     def quarters(shard):
         return [shard] + [flip(shard, masks[k]) for k in (1, 2, 3)]
 
-    def gathered(own, after=()):
-        (stacked,) = call(stack_kernel, [shape((4,) + own[0].shape, BF16)], own, after=after)
-        return own + [flip(stacked, 1)]
-
     space = lax.axis_index("space")
     spot = (space + TCOLS + 2) % tiles
     column, row = spot % TCOLS, spot // TCOLS
     me = (space % 2) * 4 + (lax.axis_index("dp") % 2) * 2 + (space // 2) % 2
     place = jnp.stack([column % 2, row % 2, column < TCOLS - 1, row < tile_rows - 1, space % 2, me]).astype(jnp.int32)
-    x = images[0, 0]
-    g3 = upstream[0, 0]
+    x = pltpu.with_memory_space_constraint(images[0, 0], pltpu.HBM)
+    g3 = pltpu.with_memory_space_constraint(upstream[0, 0], pltpu.HBM)
     w1 = first_weight.reshape(9 * cin, depth)
     w2 = second_weight.reshape(9 * depth, depth)
     gain = norm_gain.reshape(1, depth)
     bias = norm_bias.reshape(1, depth)
 
-    g_block = (rows, 16, depth)
+    hbm = pl.BlockSpec(memory_space=pltpu.HBM)
     smem = pl.BlockSpec(memory_space=pltpu.SMEM)
     vmem = pl.BlockSpec(memory_space=pltpu.VMEM)
     ends = shape((4 * 2 * rows, cin), BF16)
     half_ends = shape((2 * 2 * rows, cin), BF16)
-    one, two, own_column = call(
+    one, two, own_column, x_lines, g_lines = call(
         functools.partial(pack_kernel, rows, cols),
-        [ends, ends, half_ends],
-        [place, x, x, g3, g3],
-        [pltpu.VMEM((2 * rows * 16, cin), F32), pltpu.VMEM((rows * 16, 128), F32)],
-        specs=[
-            smem,
-            pl.BlockSpec((2 * rows, 16, cin), lambda i: (0, 0, 0)),
-            pl.BlockSpec((2 * rows, 16, cin), lambda i: (0, 2 * cols // 16 - 1, 0)),
-            pl.BlockSpec(g_block, lambda i: (0, 0, 0)),
-            pl.BlockSpec(g_block, lambda i: (0, cols // 16 - 1, 0)),
-        ],
-        grid=(1,),
+        [ends, ends, half_ends, shape((3, 2 * cols, cin), BF16), shape((3, cols, depth), BF16)],
+        [place, x, g3],
+        [pltpu.VMEM((2 * rows, 16, cin), BF16)] * 2
+        + [pltpu.VMEM((rows, 16, depth), BF16)] * 2
+        + [pltpu.VMEM((2 * rows * 16, cin), F32), pltpu.VMEM((rows * 16, 128), F32), pltpu.SemaphoreType.DMA((8,))],
+        specs=[smem, hbm, hbm],
     )
     one = swapped(one, 0, 1)
     two = swapped(two, 0, 2)
@@ -623,7 +667,12 @@
         functools.partial(planes_kernel, rows, cols),
         [shape((cells + cols, 6 * cin), BF16)],
         [x],
-        [pltpu.VMEM((2 * CHUNK // cols, 2 * cols + 8, cin), F32)],
+        [
+            pltpu.VMEM((2 * CHUNK // cols, 2 * cols + 8, cin), F32),
+            pltpu.VMEM((cells // CHUNK, 2 * CHUNK // cols, 2 * cols, cin), BF16),
+            pltpu.SemaphoreType.DMA((cells // CHUNK,)),
+        ],
+        specs=[hbm],
         flops=cells * 9 * cin * depth,
     )
     lines = shape((4 * (2 * cols + 32), cin), BF16)
@@ -631,18 +680,9 @@
     from_left, from_right, one, two, own_row = call(
         functools.partial(rows_kernel, rows, cols),
         [half_ends, ends, lines, lines, half_lines],
-        [place, x, x, g3, g3, one, two],
+        [place, x_lines, g_lines, one, two],
         [pltpu.VMEM((2 * cols + 32, cin), F32), pltpu.VMEM((cols + 16, 128), F32)],
-        specs=[
-            smem,
-            pl.BlockSpec((1, 2 * cols, cin), lambda i: (2 * rows - 1, 0, 0)),
-            pl.BlockSpec((2, 2 * cols, cin), lambda i: (0, 0, 0)),
-            pl.BlockSpec((1, cols, depth), lambda i: (rows - 1, 0, 0)),
-            pl.BlockSpec((2, cols, depth), lambda i: (0, 0, 0)),
-            vmem,
-            vmem,
-        ],
-        grid=(1,),
+        smem=1,
         after=[planes],
     )
     got_one = swapped(one, 1, 0)
@@ -655,6 +695,19 @@
         after=[one],
     )
     pads = [pltpu.VMEM((2 * rows + 8, cin), F32), pltpu.VMEM((2 * cols + 8, cin), F32)]
+    body, w_t, prepared = call(
+        functools.partial(prepare_kernel, rows, cols),
+        [shape((3, cells, depth), BF16), shape((9 * depth, depth), BF16), shape((8, 128), F32)],
+        [g3, from_left, from_right, w2],
+        [
+            pltpu.VMEM((rows * (cols + 16), depth), F32),
+            pltpu.VMEM((2, rows, depth), F32),
+            pltpu.VMEM((rows, cols, depth), BF16),
+            pltpu.SemaphoreType.DMA,
+        ],
+        specs=[hbm, vmem, vmem, vmem],
+        after=[one],
+    )
     rim = rows + cols + 8
     z, stats, from_above, from_below, z_rim = call(
         functools.partial(edges_kernel, rows, cols),
@@ -667,17 +720,16 @@
             pltpu.VMEM((3, 2 * rows + 8, cin), F32),
         ],
         smem=1,
+        after=[prepared],
         flops=2 * 80 * 3 * cin * depth,
     )
     stats = fetched(added([stats, flip(stats, 1)]))
-    taps, act_grad, act_rim = call(
+    edge, act_grad, act_rim = call(
         functools.partial(upstream_kernel, rows, cols),
-        [shape((3, cells + 2 * cols, depth), BF16), shape((cells, depth), F32), shape((rim, depth), F32)],
-        [g3.reshape(cells, depth), from_left, from_right, own_column, own_row, from_above, from_below, w2],
+        [shape((3, 2 * cols, depth), BF16), shape((cells, depth), F32), shape((rim, depth), F32)],
+        [body, w_t, from_right, own_column, own_row, from_above, from_below],
         [
-            pltpu.VMEM(((rows + 2) * (cols + 16), depth), F32),
-            pltpu.VMEM((9 * depth, depth), BF16),
-            pltpu.VMEM((2, rows, depth), F32),
+            pltpu.VMEM((2 * (cols + 16), depth), F32),
             pltpu.VMEM((3, cols + 24, depth), F32),
             pltpu.VMEM((3, rows + 16, depth), F32),
         ],
@@ -693,8 +745,7 @@
     second_slots = call(
         functools.partial(second_kernel, rows, cols),
         [shape((4, 9 * depth // 8, depth), F32), shape((4, 9 * depth // 8, depth), BF16)],
-        [place, activated, taps],
-        [pltpu.VMEM((9 * depth, depth), F32)],
+        [place, activated, body, edge],
         flops=2 * cells * 9 * depth * depth,
         smem=1,
     )
@@ -734,7 +785,6 @@
             shape((4, 9 * cin // 8, depth), BF16),
         ],
         [place] + parts + [z, pre_grad, moments, gain, bias, z_rim, act_rim, windows],
-        [pltpu.VMEM((9 * cin, depth), F32)],
         flops=2 * cells * 9 * cin * depth,
         smem=1,
         after=[second_shard],
@@ -769,12 +819,26 @@
     for k in range(1, dp_size.bit_length() - 1):
         bias_grad = bias_grad + flip(bias_grad, tiles << k)
         gain_grad = gain_grad + flip(gain_grad, tiles << k)
-    second_grad, first_grad = call(
-        gather_kernel,
-        [shape((8, sizes[0], depth), F32), shape((8, sizes[1], depth), F32)],
-        [place] + gathered(quarters(shard)),
-        smem=1,
-    )
+    own = quarters(shard)
+    grads = [shape((9, 8, depth // 8, depth), F32), shape((8, sizes[1], depth), F32)]
+    for slots in ((0,), (1, 2, 3)):
+        here = [own[slot] for slot in slots]
+        shards = here + [flip(value, 1) for value in here]
+        left = list(grads) if len(slots) > 1 else []
+        grads = call(
+            functools.partial(gather_kernel, slots, sizes[0]),
+            [shape(g.shape, F32) for g in grads],
+            [place] + shards + left,
+            [
+                pltpu.VMEM((len(shards), 9, depth // 8, depth), F32),
+                pltpu.VMEM((len(shards), sizes[1], depth), F32),
+                pltpu.SemaphoreType.DMA((2 * len(shards),)),
+            ],
+            specs=[smem] + [vmem] * len(shards) + [hbm] * len(left),
+            out_specs=[hbm] * 2,
+            aliases={1 + len(shards) + k: k for k in range(len(left))},
+        )
+    second_grad, first_grad = grads
     return (
         input_grad[None, None],
         first_grad.reshape(first_weight.shape),

time: 102 us -> 99.7 us (0.977)
  waiting for transfers between devices: 31.2 us -> 22.7 us
  starting transfers between devices: 42.3 us -> 48 us
  Pallas kernels: 24.7 us -> 27.8 us
  local copies, waits for them, and re-layouts: 2.65 us -> 0.1 us
    ppermute x25 -> x28, waiting for transfers between devices: 28.2 us -> 20.1 us  [flip(): return lax.ppermute(value, axes, [(i, i ^ mask) for i in range(devices)])]
    ppermute x25 -> x28, starting transfers between devices: 34.6 us -> 40.2 us  [flip(): return lax.ppermute(value, axes, [(i, i ^ mask) for i in range(devices)])]
    pallas_call x23 -> x24, Pallas kernels: 24.7 us -> 27.8 us  [call(): pl.pallas_call(body, out_shape=list(outs), grid=grid, in_specs=list(specs...]
    unnamed x14 -> x8, local copies, waits for them, and re-layouts: 2.57 us -> 0.02 us
    ppermute x4, waiting for transfers between devices: 2.93 us -> 1.21 us  [swapped(): return lax.ppermute(value, 'space', pairs)]
    ppermute x2, waiting for transfers between devices: 0.01 us -> 1.33 us  [crossed(): lax.ppermute(value, axes, [(i, i ^ (odd if i % 2 else even)) for i in ran...]
  transfers between devices with their start and end apart: 31 -> 34, of which waited for: 19 -> 19; matrix products, arithmetic and copies ran while one was open for 0% -> 0% of each run, Pallas kernels for 11% -> 14%
where the time goes in v3:
time: 99.7 us; the launch traced here: 99.4 us
  starting transfers between devices  48 us (48%)
  Pallas kernels  27.8 us (28%)
  waiting for transfers between devices  22.7 us (23%)
    ppermute x28, starting transfers between devices, flip(): return lax.ppermute(value, axes, [(i, i ^ mask) for i in range(devices)])  40.2 us
    pallas_call x24, Pallas kernels, call(): pl.pallas_call(body, out_shape=list(outs), grid=grid, in_specs=list(specs...  27.8 us
    ppermute x28, waiting for transfers between devices, flip(): return lax.ppermute(value, axes, [(i, i ^ mask) for i in range(devices)])  20.1 us
    ppermute x4, starting transfers between devices, swapped(): return lax.ppermute(value, 'space', pairs)  6.41 us
  transfers between devices with their start and end apart: 34, of which 19 were waited for; matrix products, arithmetic and copies ran while one was open for 0% of the time, Pallas kernels for 14%

profile of v3, /device:TPU:1, one launch (start us, length us, event | category | flops | bytes accessed | tf_op | source)
XLA Modules:
  0.0 99.4 jit_solution(11871782488050820014)
XLA Ops:
  0.8 2.1 %shard_map.102 = (bf16[384,128]{1,0:T(8,128)(2,1)S(1)}, bf16[384,128]{1,0:T(8,128)(2,1)S(1)}, bf16[192,128]{1,0:T(8,128)(2,1)S(1)}, bf16[3,64,128]{2,1,0:T(8,128)(2,1)S(1)}, bf16[3,32,256]{2,1,0:T(8,128)(2,1)S(1)}) custom-call(s32[6]{0:T(128)S(1)} %stack.35.refs_0_, bf16[96,64,128]{2,1,0:T(8,128)(2,1)} %bitcast.25, bf16[48,32,256]{2,1,0:T(8,128)(2,1)} %bitcast.27), custom_call_target="tpu_custom_call" | custom-call | bytes 2703384 | tf_op jit(solution)/shard_map/pallas_call | solution.py:29
  3.7 1.6 %shard_map.101.refs_5_.refs_0_ = bf16[1568,768]{1,0:T(8,128)(2,1)S(1)} custom-call(bf16[96,64,128]{2,1,0:T(8,128)(2,1)} %bitcast.26), custom_call_target="tpu_custom_call" | custom-call | flops 452984832 | bytes 3981312 | tf_op jit(solution)/shard_map/pallas_call | solution.py:29
  6.0 4.8 %collective-permute-start.3 = (bf16[384,128]{1,0:T(8,128)(2,1)S(1)}, bf16[384,128]{1,0:T(8,128)(2,1)S(1)}, u32[]{:S(2)}, u32[]{:S(2)}) collective-permute-start(bf16[384,128]{1,0:T(8,128)(2,1)S(1)} %get-tuple-element.63), channel_id=1, source_target_pairs={{0,4},{1,5},{2,14},{3,15},{4,0},{5,1},{14,2},{15,3},{16,20},{17,21... | collective-permute-start | bytes 294920 | tf_op jit(solution)/shard_map/ppermute | solution.py:601
  11.7 1.7 %shard_map.105 = (bf16[3,1536,256]{2,1,0:T(8,128)(2,1)S(1)}, bf16[2304,256]{1,0:T(8,128)(2,1)S(1)}, f32[8,128]{1,0:T(8,128)S(1)}) custom-call(bf16[48,32,256]{2,1,0:T(8,128)(2,1)} %bitcast.28, bf16[192,128]{1,0:T(8,128)(2,1)S(1)} %get-tuple-element.59.refs_1_.refs_2_, bf16[384,128]{1,0:T(8,128)(2,1)S(1)} %get-tuple-element.60.refs_2_.refs_3_, ...), custom_call_target="tpu_custom_call" | custom-call | bytes 5656576 | tf_op jit(solution)/shard_map/pallas_call | solution.py:29
  17.2 7.4 %collective-permute-start.4 = (f32[2,256]{1,0:T(2,128)S(1)}, f32[2,256]{1,0:T(2,128)S(1)}, u32[]{:S(2)}, u32[]{:S(2)}) collective-permute-start(f32[2,256]{1,0:T(2,128)S(1)} %get-tuple-element.65.refs_0_), channel_id=1, source_target_pairs={{0,1},{1,0},{2,3},{3,2},{4,5},{5,4},{6,7},{7,6},{8,9},{9,8},{10,11... | collective-permute-start | bytes 6152 | tf_op jit(solution)/shard_map/ppermute | solution.py:590
  25.4 2.8 %collective-permute-start.7 = (f32[2,256]{1,0:T(2,128)S(1)}, f32[2,256]{1,0:T(2,128)S(1)}, u32[]{:S(2)}, u32[]{:S(2)}) collective-permute-start(f32[2,256]{1,0:T(2,128)S(1)} %shard_map.107.refs_0_), channel_id=1, source_target_pairs={{0,6},{1,7},{2,4},{3,5},{4,2},{5,3},{6,0},{7,1},{8,14},{9,15},{10,... | collective-permute-start | bytes 6152 | tf_op jit(solution)/shard_map/ppermute | solution.py:590
  31.4 2.2 %shard_map.109 = (bf16[3,64,256]{2,1,0:T(8,128)(2,1)S(1)}, f32[1536,256]{1,0:T(8,128)S(1)}, f32[88,256]{1,0:T(8,128)S(1)}) custom-call(bf16[3,1536,256]{2,1,0:T(8,128)(2,1)S(1)} %get-tuple-element.67.refs_0_.refs_2_, bf16[2304,256]{1,0:T(8,128)(2,1)S(1)} %get-tuple-element.68.refs_1_, bf16[384,128]{1,0:T(8,128)(2,1)S(1)} %get-tuple-element.60.refs_2_.refs_3_, ...), custom_call_target="tpu_custom_call" | custom-call | flops 1811939328 | bytes 5644288 | tf_op jit(solution)/shard_map/pallas_call | solution.py:29
  35.5 2.6 %shard_map.111 = (f32[4,288,256]{2,1,0:T(8,128)S(1)}, bf16[4,288,256]{2,1,0:T(8,128)(2,1)S(1)}) custom-call(s32[6]{0:T(128)S(1)} %stack.35.refs_0_, bf16[1536,256]{1,0:T(8,128)(2,1)S(1)} %get-tuple-element.73.refs_1_, bf16[3,1536,256]{2,1,0:T(8,128)(2,1)S(1)} %get-tuple-element.67.refs_0_.refs_2_, bf16[3,64,256]{2,1,0:T(8,128)(2,1)S(1)} %get-tuple-element.74.refs_3_), custom_call_target="tpu_custom_call" | custom-call | flops 1811939328 | bytes 5013528 | tf_op jit(solution)/shard_map/pallas_call | solution.py:29
  38.1 3.1 %collective-permute-start.13 = (bf16[4,288,256]{2,1,0:T(8,128)(2,1)S(1)}, bf16[4,288,256]{2,1,0:T(8,128)(2,1)S(1)}, u32[]{:S(2)}, u32[]{:S(2)}) collective-permute-start(bf16[4,288,256]{2,1,0:T(8,128)(2,1)S(1)} %get-tuple-element.75.refs_2_), channel_id=1, source_target_pairs={{0,1},{1,0},{2,3},{3,2},{4,5},{5,4},{6,7},{7,6},{8,9},{9,8},{10,11... | collective-permute-start | bytes 1769480 | tf_op jit(solution)/shard_map/ppermute | solution.py:590
  43.6 2.5 %collective-permute-start.12 = (f32[2,256]{1,0:T(2,128)S(1)}, f32[2,256]{1,0:T(2,128)S(1)}, u32[]{:S(2)}, u32[]{:S(2)}) collective-permute-start(f32[2,256]{1,0:T(2,128)S(1)} %shard_map.112.refs_3_.refs_0_), channel_id=1, source_target_pairs={{0,6},{1,7},{2,4},{3,5},{4,2},{5,3},{6,0},{7,1},{8,14},{9,15},{10,... | collective-permute-start | bytes 6152 | tf_op jit(solution)/shard_map/ppermute | solution.py:590
  47.1 1.7 %collective-permute-done.11.refs_2_ = f32[2,256]{1,0:T(2,128)S(1)} collective-permute-done((f32[2,256]{1,0:T(2,128)S(1)}, f32[2,256]{1,0:T(2,128)S(1)}, u32[]{:S(2)}, u32[]{:S(2)}) %collective-permute-start.11) | collective-permute-done | bytes 2080 | tf_op jit(solution)/shard_map/ppermute | solution.py:590
  54.2 2.6 %shard_map.118 = (bf16[1536,256]{1,0:T(8,128)(2,1)S(1)}, f32[88,256]{1,0:T(8,128)S(1)}, f32[2,256]{1,0:T(2,128)S(1)}, f32[4,144,256]{2,1,0:T(8,128)S(1)}, bf16[4,144,256]{2,1,0:T(8,128)(2,1)S(1)}) custom-call(s32[6]{0:T(128)S(1)} %stack.35.refs_0_, f32[2,256]{1,0:T(2,128)S(1)} %shard_map.114.refs_2_.refs_1_, f32[2,256]{1,0:T(2,128)S(1)} %collective-permute-done.14.refs_2_, ...), custom_call_target="tpu_custom_call" | custom-call | flops 905969664 | bytes 8636440 | tf_op jit(solution)/shard_map/pallas_call | solution.py:29
  56.9 3.0 %collective-permute-start.20 = (bf16[4,144,256]{2,1,0:T(8,128)(2,1)S(1)}, bf16[4,144,256]{2,1,0:T(8,128)(2,1)S(1)}, u32[]{:S(2)}, u32[]{:S(2)}) collective-permute-start(bf16[4,144,256]{2,1,0:T(8,128)(2,1)S(1)} %get-tuple-element.89), channel_id=1, source_target_pairs={{0,1},{1,0},{2,3},{3,2},{4,5},{5,4},{6,7},{7,6},{8,9},{9,8},{10,11... | collective-permute-start | bytes 884744 | tf_op jit(solution)/shard_map/ppermute | solution.py:590
  59.8 1.7 %collective-permute-start.19 = (bf16[288,256]{1,0:T(8,128)(2,1)S(1)}, bf16[288,256]{1,0:T(8,128)(2,1)S(1)}, u32[]{:S(2)}, u32[]{:S(2)}) collective-permute-start(bf16[288,256]{1,0:T(8,128)(2,1)S(1)} %shard_map.117.refs_11_.refs_0_), channel_id=1, source_target_pairs={{0,12},{1,13},{2,14},{3,15},{4,8},{5,9},{6,10},{7,11},{8,4},{9,5},... | collective-permute-start | bytes 442376 | tf_op jit(solution)/shard_map/ppermute | solution.py:590
  68.2 1.7 %collective-permute-start.26 = (bf16[144,256]{1,0:T(8,128)(2,1)S(1)}, bf16[144,256]{1,0:T(8,128)(2,1)S(1)}, u32[]{:S(2)}, u32[]{:S(2)}) collective-permute-start(bf16[144,256]{1,0:T(8,128)(2,1)S(1)} %get-tuple-element.95.refs_4_), channel_id=1, source_target_pairs={{0,12},{1,13},{2,14},{3,15},{4,8},{5,9},{6,10},{7,11},{8,4},{9,5},... | collective-permute-start | bytes 221192 | tf_op jit(solution)/shard_map/ppermute | solution.py:590
  70.1 2.1 %collective-permute-start.24 = (bf16[144,256]{1,0:T(8,128)(2,1)S(1)}, bf16[144,256]{1,0:T(8,128)(2,1)S(1)}, u32[]{:S(2)}, u32[]{:S(2)}) collective-permute-start(bf16[144,256]{1,0:T(8,128)(2,1)S(1)} %get-tuple-element.95.refs_4_), channel_id=1, source_target_pairs={{0,4},{1,5},{2,6},{3,7},{4,0},{5,1},{6,2},{7,3},{8,12},{9,13},{10,... | collective-permute-start | bytes 221192 | tf_op jit(solution)/shard_map/ppermute | solution.py:590
  72.1 4.1 %shard_map.119 = (bf16[96,64,128]{2,1,0:T(8,128)(2,1)}, f32[8,128]{1,0:T(8,128)S(1)}) custom-call(bf16[1536,256]{1,0:T(8,128)(2,1)S(1)} %get-tuple-element.85.refs_0_, f32[88,256]{1,0:T(8,128)S(1)} %get-tuple-element.86.refs_1_, bf16[1152,256]{1,0:T(8,128)(2,1)S(1)} %bitcast.19), custom_call_target="tpu_custom_call" | custom-call | flops 905969664 | bytes 3043328 | tf_op jit(solution)/shard_map/pallas_call | solution.py:29
  76.2 2.7 %collective-permute-done.18.refs_2_ = bf16[288,256]{1,0:T(8,128)(2,1)S(1)} collective-permute-done((bf16[288,256]{1,0:T(8,128)(2,1)S(1)}, bf16[288,256]{1,0:T(8,128)(2,1)S(1)}, u32[]{:S(2)}, u32[]{:S(2)}) %collective-permute-start.18) | collective-permute-done | bytes 147488 | tf_op jit(solution)/shard_map/ppermute | solution.py:590
  78.9 3.2 %collective-permute-done.25.refs_6_ = bf16[144,256]{1,0:T(8,128)(2,1)S(1)} collective-permute-done((bf16[144,256]{1,0:T(8,128)(2,1)S(1)}, bf16[144,256]{1,0:T(8,128)(2,1)S(1)}, u32[]{:S(2)}, u32[]{:S(2)}) %collective-permute-start.25) | collective-permute-done | bytes 73760 | tf_op jit(solution)/shard_map/ppermute | solution.py:590
  84.9 1.7 %collective-permute-start.33 = (bf16[432,256]{1,0:T(8,128)(2,1)S(1)}, bf16[432,256]{1,0:T(8,128)(2,1)S(1)}, u32[]{:S(2)}, u32[]{:S(2)}) collective-permute-start(bf16[432,256]{1,0:T(8,128)(2,1)S(1)} %shard_map.122.refs_1_), channel_id=1, source_target_pairs={{0,1},{1,0},{2,3},{3,2},{4,5},{5,4},{6,7},{7,6},{8,9},{9,8},{10,11... | collective-permute-start | bytes 663560 | tf_op jit(solution)/shard_map/ppermute | solution.py:590
  86.6 2.7 %collective-permute-done.29.refs_3_ = bf16[432,256]{1,0:T(8,128)(2,1)S(1)} collective-permute-done((bf16[432,256]{1,0:T(8,128)(2,1)S(1)}, bf16[432,256]{1,0:T(8,128)(2,1)S(1)}, u32[]{:S(2)}, u32[]{:S(2)}) %collective-permute-start.29) | collective-permute-done | bytes 221216 | tf_op jit(solution)/shard_map/ppermute | solution.py:590
  89.3 3.1 %collective-permute-start.32 = (bf16[432,256]{1,0:T(8,128)(2,1)S(1)}, bf16[432,256]{1,0:T(8,128)(2,1)S(1)}, u32[]{:S(2)}, u32[]{:S(2)}) collective-permute-start(bf16[432,256]{1,0:T(8,128)(2,1)S(1)} %collective-permute-done.29.refs_3_), channel_id=1, source_target_pairs={{0,1},{1,0},{2,3},{3,2},{4,5},{5,4},{6,7},{7,6},{8,9},{9,8},{10,11... | collective-permute-start | bytes 663560 | tf_op jit(solution)/shard_map/ppermute | solution.py:590
  93.3 1.7 %collective-permute-start.31 = (bf16[432,256]{1,0:T(8,128)(2,1)S(1)}, bf16[432,256]{1,0:T(8,128)(2,1)S(1)}, u32[]{:S(2)}, u32[]{:S(2)}) collective-permute-start(bf16[432,256]{1,0:T(8,128)(2,1)S(1)} %collective-permute-done.28.refs_2_), channel_id=1, source_target_pairs={{0,1},{1,0},{2,3},{3,2},{4,5},{5,4},{6,7},{7,6},{8,9},{9,8},{10,11... | collective-permute-start | bytes 663560 | tf_op jit(solution)/shard_map/ppermute | solution.py:590
  97.3 2.2 %shard_map.124 = (f32[9,8,32,256]{3,2,1,0:T(8,128)}, f32[8,144,256]{2,1,0:T(8,128)}) custom-call(s32[6]{0:T(128)S(1)} %stack.35.refs_0_, bf16[432,256]{1,0:T(8,128)(2,1)S(1)} %collective-permute-done.27.refs_1_, bf16[432,256]{1,0:T(8,128)(2,1)S(1)} %collective-permute-done.28.refs_2_, ...), custom_call_target="tpu_custom_call", output_to_operand_aliasing={{0}: (7, {}), {1}: (8, {})} | custom-call | bytes 8405016 | tf_op jit(solution)/shard_map/pallas_call | solution.py:29
  (77 shorter events, 33.7 us)
Async XLA Ops:
  6.0 8.9 %collective-permute-start.3 = (bf16[384,128]{1,0:T(8,128)(2,1)S(1)}, bf16[384,128]{1,0:T(8,128)(2,1)S(1)}, u32[]{:S(2)}, u32[]{:S(2)}) collective-permute-start(bf16[384,128]{1,0:T(8,128)(2,1)S(1)} %get-tuple-element.63), channel_id=1, source_target_pairs={{0,4},{1,5},{2,14},{3,15},{4,0},{5,1},{14,2},{15,3},{16,20},{17,21... | collective-permute-start | bytes 294920 | tf_op jit(solution)/shard_map/ppermute | solution.py:601
  10.8 5.3 %collective-permute-start.2 = (bf16[384,128]{1,0:T(8,128)(2,1)S(1)}, bf16[384,128]{1,0:T(8,128)(2,1)S(1)}, u32[]{:S(2)}, u32[]{:S(2)}) collective-permute-start(bf16[384,128]{1,0:T(8,128)(2,1)S(1)} %get-tuple-element.58.refs_2_.refs_4_), channel_id=1, source_target_pairs={{0,12},{1,13},{2,6},{3,7},{4,8},{5,9},{6,2},{7,3},{8,4},{9,5},{10,... | collective-permute-start | bytes 294920 | tf_op jit(solution)/shard_map/ppermute | solution.py:601
  17.2 8.2 %collective-permute-start.4 = (f32[2,256]{1,0:T(2,128)S(1)}, f32[2,256]{1,0:T(2,128)S(1)}, u32[]{:S(2)}, u32[]{:S(2)}) collective-permute-start(f32[2,256]{1,0:T(2,128)S(1)} %get-tuple-element.65.refs_0_), channel_id=1, source_target_pairs={{0,1},{1,0},{2,3},{3,2},{4,5},{5,4},{6,7},{7,6},{8,9},{9,8},{10,11... | collective-permute-start | bytes 6152 | tf_op jit(solution)/shard_map/ppermute | solution.py:590
  25.4 3.7 %collective-permute-start.7 = (f32[2,256]{1,0:T(2,128)S(1)}, f32[2,256]{1,0:T(2,128)S(1)}, u32[]{:S(2)}, u32[]{:S(2)}) collective-permute-start(f32[2,256]{1,0:T(2,128)S(1)} %shard_map.107.refs_0_), channel_id=1, source_target_pairs={{0,6},{1,7},{2,4},{3,5},{4,2},{5,3},{6,0},{7,1},{8,14},{9,15},{10,... | collective-permute-start | bytes 6152 | tf_op jit(solution)/shard_map/ppermute | solution.py:590
  38.1 4.7 %collective-permute-start.13 = (bf16[4,288,256]{2,1,0:T(8,128)(2,1)S(1)}, bf16[4,288,256]{2,1,0:T(8,128)(2,1)S(1)}, u32[]{:S(2)}, u32[]{:S(2)}) collective-permute-start(bf16[4,288,256]{2,1,0:T(8,128)(2,1)S(1)} %get-tuple-element.75.refs_2_), channel_id=1, source_target_pairs={{0,1},{1,0},{2,3},{3,2},{4,5},{5,4},{6,7},{7,6},{8,9},{9,8},{10,11... | collective-permute-start | bytes 1769480 | tf_op jit(solution)/shard_map/ppermute | solution.py:590
  43.5 6.0 %collective-permute-start.15 = (bf16[2,288,256]{2,1,0:T(8,128)(2,1)S(1)}, bf16[2,288,256]{2,1,0:T(8,128)(2,1)S(1)}, u32[]{:S(2)}, u32[]{:S(2)}) collective-permute-start(bf16[2,288,256]{2,1,0:T(8,128)(2,1)S(1)} %get-tuple-element.82), channel_id=1, source_target_pairs={{0,16},{1,3},{2,18},{3,1},{4,20},{5,7},{6,22},{7,5},{8,24},{9,11},... | collective-permute-start | bytes 884744 | tf_op jit(solution)/shard_map/ppermute | solution.py:614
  43.6 3.5 %collective-permute-start.12 = (f32[2,256]{1,0:T(2,128)S(1)}, f32[2,256]{1,0:T(2,128)S(1)}, u32[]{:S(2)}, u32[]{:S(2)}) collective-permute-start(f32[2,256]{1,0:T(2,128)S(1)} %shard_map.112.refs_3_.refs_0_), channel_id=1, source_target_pairs={{0,6},{1,7},{2,4},{3,5},{4,2},{5,3},{6,0},{7,1},{8,14},{9,15},{10,... | collective-permute-start | bytes 6152 | tf_op jit(solution)/shard_map/ppermute | solution.py:590
  49.6 4.1 %collective-permute-start.16 = (bf16[288,256]{1,0:T(8,128)(2,1)S(1)}, bf16[288,256]{1,0:T(8,128)(2,1)S(1)}, u32[]{:S(2)}, u32[]{:S(2)}) collective-permute-start(bf16[288,256]{1,0:T(8,128)(2,1)S(1)} %get-tuple-element.84), channel_id=1, source_target_pairs={{0,2},{1,17},{2,0},{3,19},{4,6},{5,21},{6,4},{7,23},{8,10},{9,25},... | collective-permute-start | bytes 442376 | tf_op jit(solution)/shard_map/ppermute | solution.py:614
  56.9 4.7 %collective-permute-start.20 = (bf16[4,144,256]{2,1,0:T(8,128)(2,1)S(1)}, bf16[4,144,256]{2,1,0:T(8,128)(2,1)S(1)}, u32[]{:S(2)}, u32[]{:S(2)}) collective-permute-start(bf16[4,144,256]{2,1,0:T(8,128)(2,1)S(1)} %get-tuple-element.89), channel_id=1, source_target_pairs={{0,1},{1,0},{2,3},{3,2},{4,5},{5,4},{6,7},{7,6},{8,9},{9,8},{10,11... | collective-permute-start | bytes 884744 | tf_op jit(solution)/shard_map/ppermute | solution.py:590
  59.8 10.2 %collective-permute-start.19 = (bf16[288,256]{1,0:T(8,128)(2,1)S(1)}, bf16[288,256]{1,0:T(8,128)(2,1)S(1)}, u32[]{:S(2)}, u32[]{:S(2)}) collective-permute-start(bf16[288,256]{1,0:T(8,128)(2,1)S(1)} %shard_map.117.refs_11_.refs_0_), channel_id=1, source_target_pairs={{0,12},{1,13},{2,14},{3,15},{4,8},{5,9},{6,10},{7,11},{8,4},{9,5},... | collective-permute-start | bytes 442376 | tf_op jit(solution)/shard_map/ppermute | solution.py:590
  61.6 3.6 %collective-permute-start.21 = (bf16[144,256]{1,0:T(8,128)(2,1)S(1)}, bf16[144,256]{1,0:T(8,128)(2,1)S(1)}, u32[]{:S(2)}, u32[]{:S(2)}) collective-permute-start(bf16[144,256]{1,0:T(8,128)(2,1)S(1)} %get-tuple-element.92), channel_id=1, source_target_pairs={{0,2},{1,3},{2,0},{3,1},{4,6},{5,7},{6,4},{7,5},{8,10},{9,11},{10,... | collective-permute-start | bytes 221192 | tf_op jit(solution)/shard_map/ppermute | solution.py:590
  62.1 5.4 %collective-permute-start.22 = (bf16[160,256]{1,0:T(8,128)(2,1)S(1)}, bf16[160,256]{1,0:T(8,128)(2,1)S(1)}, u32[]{:S(2)}, u32[]{:S(2)}) collective-permute-start(bf16[160,256]{1,0:T(8,128)(2,1)S(1)} %get-tuple-element.93), channel_id=1, source_target_pairs={{0,16},{1,17},{2,18},{3,19},{4,20},{5,21},{6,22},{7,23},{8,24},{9,... | collective-permute-start | bytes 245768 | tf_op jit(solution)/shard_map/ppermute | solution.py:590
  62.8 4.8 %collective-permute-start.23 = (bf16[144,256]{1,0:T(8,128)(2,1)S(1)}, bf16[144,256]{1,0:T(8,128)(2,1)S(1)}, u32[]{:S(2)}, u32[]{:S(2)}) collective-permute-start(bf16[144,256]{1,0:T(8,128)(2,1)S(1)} %get-tuple-element.94), channel_id=1, source_target_pairs={{0,18},{1,19},{2,16},{3,17},{4,22},{5,23},{6,20},{7,21},{8,26},{9,... | collective-permute-start | bytes 221192 | tf_op jit(solution)/shard_map/ppermute | solution.py:590
  64.4 14.6 %collective-permute-start.18 = (bf16[288,256]{1,0:T(8,128)(2,1)S(1)}, bf16[288,256]{1,0:T(8,128)(2,1)S(1)}, u32[]{:S(2)}, u32[]{:S(2)}) collective-permute-start(bf16[288,256]{1,0:T(8,128)(2,1)S(1)} %shard_map.117.refs_11_.refs_0_), channel_id=1, source_target_pairs={{0,8},{1,9},{2,10},{3,11},{4,12},{5,13},{6,14},{7,15},{8,0},{9,1},... | collective-permute-start | bytes 442376 | tf_op jit(solution)/shard_map/ppermute | solution.py:590
  65.2 13.7 %collective-permute-start.17 = (bf16[288,256]{1,0:T(8,128)(2,1)S(1)}, bf16[288,256]{1,0:T(8,128)(2,1)S(1)}, u32[]{:S(2)}, u32[]{:S(2)}) collective-permute-start(bf16[288,256]{1,0:T(8,128)(2,1)S(1)} %shard_map.117.refs_11_.refs_0_), channel_id=1, source_target_pairs={{0,4},{1,5},{2,6},{3,7},{4,0},{5,1},{6,2},{7,3},{8,12},{9,13},{10,... | collective-permute-start | bytes 442376 | tf_op jit(solution)/shard_map/ppermute | solution.py:590
  68.2 10.8 %collective-permute-start.26 = (bf16[144,256]{1,0:T(8,128)(2,1)S(1)}, bf16[144,256]{1,0:T(8,128)(2,1)S(1)}, u32[]{:S(2)}, u32[]{:S(2)}) collective-permute-start(bf16[144,256]{1,0:T(8,128)(2,1)S(1)} %get-tuple-element.95.refs_4_), channel_id=1, source_target_pairs={{0,12},{1,13},{2,14},{3,15},{4,8},{5,9},{6,10},{7,11},{8,4},{9,5},... | collective-permute-start | bytes 221192 | tf_op jit(solution)/shard_map/ppermute | solution.py:590
  69.9 12.2 %collective-permute-start.25 = (bf16[144,256]{1,0:T(8,128)(2,1)S(1)}, bf16[144,256]{1,0:T(8,128)(2,1)S(1)}, u32[]{:S(2)}, u32[]{:S(2)}) collective-permute-start(bf16[144,256]{1,0:T(8,128)(2,1)S(1)} %get-tuple-element.95.refs_4_), channel_id=1, source_target_pairs={{0,8},{1,9},{2,10},{3,11},{4,12},{5,13},{6,14},{7,15},{8,0},{9,1},... | collective-permute-start | bytes 221192 | tf_op jit(solution)/shard_map/ppermute | solution.py:590
  70.1 12.0 %collective-permute-start.24 = (bf16[144,256]{1,0:T(8,128)(2,1)S(1)}, bf16[144,256]{1,0:T(8,128)(2,1)S(1)}, u32[]{:S(2)}, u32[]{:S(2)}) collective-permute-start(bf16[144,256]{1,0:T(8,128)(2,1)S(1)} %get-tuple-element.95.refs_4_), channel_id=1, source_target_pairs={{0,4},{1,5},{2,6},{3,7},{4,0},{5,1},{6,2},{7,3},{8,12},{9,13},{10,... | collective-permute-start | bytes 221192 | tf_op jit(solution)/shard_map/ppermute | solution.py:590
  82.2 7.1 %collective-permute-start.29 = (bf16[432,256]{1,0:T(8,128)(2,1)S(1)}, bf16[432,256]{1,0:T(8,128)(2,1)S(1)}, u32[]{:S(2)}, u32[]{:S(2)}) collective-permute-start(bf16[432,256]{1,0:T(8,128)(2,1)S(1)} %shard_map.122.refs_1_), channel_id=1, source_target_pairs={{0,18},{1,19},{2,16},{3,17},{4,22},{5,23},{6,20},{7,21},{8,26},{9,... | collective-permute-start | bytes 663560 | tf_op jit(solution)/shard_map/ppermute | solution.py:590
  83.1 10.2 %collective-permute-start.28 = (bf16[432,256]{1,0:T(8,128)(2,1)S(1)}, bf16[432,256]{1,0:T(8,128)(2,1)S(1)}, u32[]{:S(2)}, u32[]{:S(2)}) collective-permute-start(bf16[432,256]{1,0:T(8,128)(2,1)S(1)} %shard_map.122.refs_1_), channel_id=1, source_target_pairs={{0,16},{1,17},{2,18},{3,19},{4,20},{5,21},{6,22},{7,23},{8,24},{9,... | collective-permute-start | bytes 663560 | tf_op jit(solution)/shard_map/ppermute | solution.py:590
  83.9 11.4 %collective-permute-start.27 = (bf16[432,256]{1,0:T(8,128)(2,1)S(1)}, bf16[432,256]{1,0:T(8,128)(2,1)S(1)}, u32[]{:S(2)}, u32[]{:S(2)}) collective-permute-start(bf16[432,256]{1,0:T(8,128)(2,1)S(1)} %shard_map.122.refs_1_), channel_id=1, source_target_pairs={{0,2},{1,3},{2,0},{3,1},{4,6},{5,7},{6,4},{7,5},{8,10},{9,11},{10,... | collective-permute-start | bytes 663560 | tf_op jit(solution)/shard_map/ppermute | solution.py:590
  84.9 10.8 %collective-permute-start.33 = (bf16[432,256]{1,0:T(8,128)(2,1)S(1)}, bf16[432,256]{1,0:T(8,128)(2,1)S(1)}, u32[]{:S(2)}, u32[]{:S(2)}) collective-permute-start(bf16[432,256]{1,0:T(8,128)(2,1)S(1)} %shard_map.122.refs_1_), channel_id=1, source_target_pairs={{0,1},{1,0},{2,3},{3,2},{4,5},{5,4},{6,7},{7,6},{8,9},{9,8},{10,11... | collective-permute-start | bytes 663560 | tf_op jit(solution)/shard_map/ppermute | solution.py:590
  89.3 8.0 %collective-permute-start.32 = (bf16[432,256]{1,0:T(8,128)(2,1)S(1)}, bf16[432,256]{1,0:T(8,128)(2,1)S(1)}, u32[]{:S(2)}, u32[]{:S(2)}) collective-permute-start(bf16[432,256]{1,0:T(8,128)(2,1)S(1)} %collective-permute-done.29.refs_3_), channel_id=1, source_target_pairs={{0,1},{1,0},{2,3},{3,2},{4,5},{5,4},{6,7},{7,6},{8,9},{9,8},{10,11... | collective-permute-start | bytes 663560 | tf_op jit(solution)/shard_map/ppermute | solution.py:590
  93.3 4.0 %collective-permute-start.31 = (bf16[432,256]{1,0:T(8,128)(2,1)S(1)}, bf16[432,256]{1,0:T(8,128)(2,1)S(1)}, u32[]{:S(2)}, u32[]{:S(2)}) collective-permute-start(bf16[432,256]{1,0:T(8,128)(2,1)S(1)} %collective-permute-done.28.refs_2_), channel_id=1, source_target_pairs={{0,1},{1,0},{2,3},{3,2},{4,5},{5,4},{6,7},{7,6},{8,9},{9,8},{10,11... | collective-permute-start | bytes 663560 | tf_op jit(solution)/shard_map/ppermute | solution.py:590
  (14 other events, 45.1 us)

commit v4 on v3

--- a/solution.py
+++ b/solution.py
@@ -627,6 +627,13 @@
         outs = [shape(part, F32), shape(part, BF16), shape(longer, BF16), shape(part, BF16)]
         return call(half_kernel, outs, [slots[0], flip(slots[1], 1), *more], after=after)
 
+    def halves(value):
+        pair = [value]
+        for k in range(2, tiles.bit_length() - 1):
+            pair = [total(pair)]
+            pair.append(flip(pair[0], 1 << k))
+        return pair
+
     masks = [0, 2, tiles, tiles + 2]
 
     def quartered(parts):
@@ -774,7 +781,7 @@
         after=second_parts[:1],
     )
     second_shard = total([second_parts[0], crossed(second_parts[1], 2, tiles)])
-    pair = along(total(along(second_shard, dp_size // 2, 2 * tiles)), tiles // 4, 4)
+    pair = halves(total(along(second_shard, dp_size // 2, 2 * tiles)))
     conv_grad, grad_rim, sum_pair, *first_slots = call(
         functools.partial(conv_grad_kernel, norm_count, rows, cols),
         [

time: 99.7 us -> 97.8 us (0.981)
  waiting for transfers between devices: 22.7 us -> 19.4 us
  starting transfers between devices: 48 us -> 49.3 us
    ppermute x28 -> x27, waiting for transfers between devices: 20.1 us -> 16.8 us  [flip(): return lax.ppermute(value, axes, [(i, i ^ mask) for i in range(devices)])]
    ppermute x28 -> x27, starting transfers between devices: 40.2 us -> 41.5 us  [flip(): return lax.ppermute(value, axes, [(i, i ^ mask) for i in range(devices)])]
    pallas_call x24 -> x25, Pallas kernels: 27.8 us -> 27.7 us  [call(): pl.pallas_call(body, out_shape=list(outs), grid=grid, in_specs=list(specs...]
  transfers between devices with their start and end apart: 34 -> 33, of which waited for: 19 -> 17; matrix products, arithmetic and copies ran while one was open for 0% -> 0% of each run, Pallas kernels for 14% -> 15%
where the time goes in v4:
time: 97.8 us; the launch traced here: 97.5 us
  starting transfers between devices  49.3 us (50%)
  Pallas kernels  27.7 us (28%)
  waiting for transfers between devices  19.4 us (20%)
    ppermute x27, starting transfers between devices, flip(): return lax.ppermute(value, axes, [(i, i ^ mask) for i in range(devices)])  41.5 us
    pallas_call x25, Pallas kernels, call(): pl.pallas_call(body, out_shape=list(outs), grid=grid, in_specs=list(specs...  27.7 us
    ppermute x27, waiting for transfers between devices, flip(): return lax.ppermute(value, axes, [(i, i ^ mask) for i in range(devices)])  16.8 us
    ppermute x4, starting transfers between devices, swapped(): return lax.ppermute(value, 'space', pairs)  6.41 us
  transfers between devices with their start and end apart: 33, of which 17 were waited for; matrix products, arithmetic and copies ran while one was open for 0% of the time, Pallas kernels for 15%

profile of v4, /device:TPU:1, one launch (start us, length us, event | category | flops | bytes accessed | tf_op | source)
XLA Modules:
  0.0 97.5 jit_solution(5888775532723856785)
XLA Ops:
  0.8 2.1 %shard_map.102 = (bf16[384,128]{1,0:T(8,128)(2,1)S(1)}, bf16[384,128]{1,0:T(8,128)(2,1)S(1)}, bf16[192,128]{1,0:T(8,128)(2,1)S(1)}, bf16[3,64,128]{2,1,0:T(8,128)(2,1)S(1)}, bf16[3,32,256]{2,1,0:T(8,128)(2,1)S(1)}) custom-call(s32[6]{0:T(128)S(1)} %stack.35.refs_0_, bf16[96,64,128]{2,1,0:T(8,128)(2,1)} %bitcast.25, bf16[48,32,256]{2,1,0:T(8,128)(2,1)} %bitcast.27), custom_call_target="tpu_custom_call" | custom-call | bytes 2703384 | tf_op jit(solution)/shard_map/pallas_call | solution.py:29
  3.7 1.6 %shard_map.101.refs_5_.refs_0_ = bf16[1568,768]{1,0:T(8,128)(2,1)S(1)} custom-call(bf16[96,64,128]{2,1,0:T(8,128)(2,1)} %bitcast.26), custom_call_target="tpu_custom_call" | custom-call | flops 452984832 | bytes 3981312 | tf_op jit(solution)/shard_map/pallas_call | solution.py:29
  6.0 4.8 %collective-permute-start.3 = (bf16[384,128]{1,0:T(8,128)(2,1)S(1)}, bf16[384,128]{1,0:T(8,128)(2,1)S(1)}, u32[]{:S(2)}, u32[]{:S(2)}) collective-permute-start(bf16[384,128]{1,0:T(8,128)(2,1)S(1)} %get-tuple-element.63), channel_id=1, source_target_pairs={{0,4},{1,5},{2,14},{3,15},{4,0},{5,1},{14,2},{15,3},{16,20},{17,21... | collective-permute-start | bytes 294920 | tf_op jit(solution)/shard_map/ppermute | solution.py:601
  11.7 1.7 %shard_map.105 = (bf16[3,1536,256]{2,1,0:T(8,128)(2,1)S(1)}, bf16[2304,256]{1,0:T(8,128)(2,1)S(1)}, f32[8,128]{1,0:T(8,128)S(1)}) custom-call(bf16[48,32,256]{2,1,0:T(8,128)(2,1)} %bitcast.28, bf16[192,128]{1,0:T(8,128)(2,1)S(1)} %get-tuple-element.59.refs_1_.refs_2_, bf16[384,128]{1,0:T(8,128)(2,1)S(1)} %get-tuple-element.60.refs_2_.refs_3_, ...), custom_call_target="tpu_custom_call" | custom-call | bytes 5656576 | tf_op jit(solution)/shard_map/pallas_call | solution.py:29
  13.4 1.5 %shard_map.104.refs_1_ = f32[1536,256]{1,0:T(8,128)S(1)} custom-call(bf16[1568,768]{1,0:T(8,128)(2,1)S(1)} %shard_map.101.refs_5_.refs_0_, bf16[1152,256]{1,0:T(8,128)(2,1)S(1)} %bitcast.17, bf16[384,128]{1,0:T(8,128)(2,1)S(1)} %get-tuple-element.58.refs_2_.refs_4_), custom_call_target="tpu_custom_call" | custom-call | flops 905969664 | bytes 4571136 | tf_op jit(solution)/shard_map/pallas_call | solution.py:29
  17.2 7.4 %collective-permute-start.4 = (f32[2,256]{1,0:T(2,128)S(1)}, f32[2,256]{1,0:T(2,128)S(1)}, u32[]{:S(2)}, u32[]{:S(2)}) collective-permute-start(f32[2,256]{1,0:T(2,128)S(1)} %get-tuple-element.65.refs_0_), channel_id=1, source_target_pairs={{0,1},{1,0},{2,3},{3,2},{4,5},{5,4},{6,7},{7,6},{8,9},{9,8},{10,11... | collective-permute-start | bytes 6152 | tf_op jit(solution)/shard_map/ppermute | solution.py:590
  25.4 2.8 %collective-permute-start.7 = (f32[2,256]{1,0:T(2,128)S(1)}, f32[2,256]{1,0:T(2,128)S(1)}, u32[]{:S(2)}, u32[]{:S(2)}) collective-permute-start(f32[2,256]{1,0:T(2,128)S(1)} %shard_map.107.refs_0_), channel_id=1, source_target_pairs={{0,6},{1,7},{2,4},{3,5},{4,2},{5,3},{6,0},{7,1},{8,14},{9,15},{10,... | collective-permute-start | bytes 6152 | tf_op jit(solution)/shard_map/ppermute | solution.py:590
  31.4 2.2 %shard_map.109 = (bf16[3,64,256]{2,1,0:T(8,128)(2,1)S(1)}, f32[1536,256]{1,0:T(8,128)S(1)}, f32[88,256]{1,0:T(8,128)S(1)}) custom-call(bf16[3,1536,256]{2,1,0:T(8,128)(2,1)S(1)} %get-tuple-element.67.refs_0_.refs_2_, bf16[2304,256]{1,0:T(8,128)(2,1)S(1)} %get-tuple-element.68.refs_1_, bf16[384,128]{1,0:T(8,128)(2,1)S(1)} %get-tuple-element.60.refs_2_.refs_3_, ...), custom_call_target="tpu_custom_call" | custom-call | flops 1811939328 | bytes 5644288 | tf_op jit(solution)/shard_map/pallas_call | solution.py:29
  35.5 2.6 %shard_map.111 = (f32[4,288,256]{2,1,0:T(8,128)S(1)}, bf16[4,288,256]{2,1,0:T(8,128)(2,1)S(1)}) custom-call(s32[6]{0:T(128)S(1)} %stack.35.refs_0_, bf16[1536,256]{1,0:T(8,128)(2,1)S(1)} %get-tuple-element.73.refs_1_, bf16[3,1536,256]{2,1,0:T(8,128)(2,1)S(1)} %get-tuple-element.67.refs_0_.refs_2_, bf16[3,64,256]{2,1,0:T(8,128)(2,1)S(1)} %get-tuple-element.74.refs_3_), custom_call_target="tpu_custom_call" | custom-call | flops 1811939328 | bytes 5013528 | tf_op jit(solution)/shard_map/pallas_call | solution.py:29
  38.1 3.1 %collective-permute-start.13 = (bf16[4,288,256]{2,1,0:T(8,128)(2,1)S(1)}, bf16[4,288,256]{2,1,0:T(8,128)(2,1)S(1)}, u32[]{:S(2)}, u32[]{:S(2)}) collective-permute-start(bf16[4,288,256]{2,1,0:T(8,128)(2,1)S(1)} %get-tuple-element.75.refs_2_), channel_id=1, source_target_pairs={{0,1},{1,0},{2,3},{3,2},{4,5},{5,4},{6,7},{7,6},{8,9},{9,8},{10,11... | collective-permute-start | bytes 1769480 | tf_op jit(solution)/shard_map/ppermute | solution.py:590
  41.3 1.6 %collective-permute-done.9.refs_1_ = f32[2,256]{1,0:T(2,128)S(1)} collective-permute-done((f32[2,256]{1,0:T(2,128)S(1)}, f32[2,256]{1,0:T(2,128)S(1)}, u32[]{:S(2)}, u32[]{:S(2)}) %collective-permute-start.9) | collective-permute-done | bytes 2080 | tf_op jit(solution)/shard_map/ppermute | solution.py:590
  43.6 2.5 %collective-permute-start.12 = (f32[2,256]{1,0:T(2,128)S(1)}, f32[2,256]{1,0:T(2,128)S(1)}, u32[]{:S(2)}, u32[]{:S(2)}) collective-permute-start(f32[2,256]{1,0:T(2,128)S(1)} %shard_map.112.refs_3_.refs_0_), channel_id=1, source_target_pairs={{0,6},{1,7},{2,4},{3,5},{4,2},{5,3},{6,0},{7,1},{8,14},{9,15},{10,... | collective-permute-start | bytes 6152 | tf_op jit(solution)/shard_map/ppermute | solution.py:590
  47.1 1.7 %collective-permute-done.11.refs_2_ = f32[2,256]{1,0:T(2,128)S(1)} collective-permute-done((f32[2,256]{1,0:T(2,128)S(1)}, f32[2,256]{1,0:T(2,128)S(1)}, u32[]{:S(2)}, u32[]{:S(2)}) %collective-permute-start.11) | collective-permute-done | bytes 2080 | tf_op jit(solution)/shard_map/ppermute | solution.py:590
  54.2 2.6 %shard_map.118 = (bf16[1536,256]{1,0:T(8,128)(2,1)S(1)}, f32[88,256]{1,0:T(8,128)S(1)}, f32[2,256]{1,0:T(2,128)S(1)}, f32[4,144,256]{2,1,0:T(8,128)S(1)}, bf16[4,144,256]{2,1,0:T(8,128)(2,1)S(1)}) custom-call(s32[6]{0:T(128)S(1)} %stack.35.refs_0_, f32[2,256]{1,0:T(2,128)S(1)} %shard_map.114.refs_2_.refs_1_, f32[2,256]{1,0:T(2,128)S(1)} %collective-permute-done.14.refs_2_, ...), custom_call_target="tpu_custom_call" | custom-call | flops 905969664 | bytes 8636440 | tf_op jit(solution)/shard_map/pallas_call | solution.py:29
  56.9 3.0 %collective-permute-start.19 = (bf16[4,144,256]{2,1,0:T(8,128)(2,1)S(1)}, bf16[4,144,256]{2,1,0:T(8,128)(2,1)S(1)}, u32[]{:S(2)}, u32[]{:S(2)}) collective-permute-start(bf16[4,144,256]{2,1,0:T(8,128)(2,1)S(1)} %get-tuple-element.89), channel_id=1, source_target_pairs={{0,1},{1,0},{2,3},{3,2},{4,5},{5,4},{6,7},{7,6},{8,9},{9,8},{10,11... | collective-permute-start | bytes 884744 | tf_op jit(solution)/shard_map/ppermute | solution.py:590
  62.4 1.5 %collective-permute-start.22 = (bf16[144,256]{1,0:T(8,128)(2,1)S(1)}, bf16[144,256]{1,0:T(8,128)(2,1)S(1)}, u32[]{:S(2)}, u32[]{:S(2)}) collective-permute-start(bf16[144,256]{1,0:T(8,128)(2,1)S(1)} %get-tuple-element.94), channel_id=1, source_target_pairs={{0,18},{1,19},{2,16},{3,17},{4,22},{5,23},{6,20},{7,21},{8,26},{9,... | collective-permute-start | bytes 221192 | tf_op jit(solution)/shard_map/ppermute | solution.py:590
  67.2 2.2 %collective-permute-start.25 = (bf16[144,256]{1,0:T(8,128)(2,1)S(1)}, bf16[144,256]{1,0:T(8,128)(2,1)S(1)}, u32[]{:S(2)}, u32[]{:S(2)}) collective-permute-start(bf16[144,256]{1,0:T(8,128)(2,1)S(1)} %get-tuple-element.95.refs_2_), channel_id=1, source_target_pairs={{0,12},{1,13},{2,14},{3,15},{4,8},{5,9},{6,10},{7,11},{8,4},{9,5},... | collective-permute-start | bytes 221192 | tf_op jit(solution)/shard_map/ppermute | solution.py:590
  70.8 4.1 %shard_map.119 = (bf16[96,64,128]{2,1,0:T(8,128)(2,1)}, f32[8,128]{1,0:T(8,128)S(1)}) custom-call(bf16[1536,256]{1,0:T(8,128)(2,1)S(1)} %get-tuple-element.85.refs_0_, f32[88,256]{1,0:T(8,128)S(1)} %get-tuple-element.86.refs_1_, bf16[1152,256]{1,0:T(8,128)(2,1)S(1)} %bitcast.19), custom_call_target="tpu_custom_call" | custom-call | flops 905969664 | bytes 3043328 | tf_op jit(solution)/shard_map/pallas_call | solution.py:29
  74.8 2.5 %collective-permute-done.18.refs_1_ = bf16[288,256]{1,0:T(8,128)(2,1)S(1)} collective-permute-done((bf16[288,256]{1,0:T(8,128)(2,1)S(1)}, bf16[288,256]{1,0:T(8,128)(2,1)S(1)}, u32[]{:S(2)}, u32[]{:S(2)}) %collective-permute-start.18) | collective-permute-done | bytes 147488 | tf_op jit(solution)/shard_map/ppermute | solution.py:590
  77.3 2.9 %collective-permute-done.24.refs_4_ = bf16[144,256]{1,0:T(8,128)(2,1)S(1)} collective-permute-done((bf16[144,256]{1,0:T(8,128)(2,1)S(1)}, bf16[144,256]{1,0:T(8,128)(2,1)S(1)}, u32[]{:S(2)}, u32[]{:S(2)}) %collective-permute-start.24) | collective-permute-done | bytes 73760 | tf_op jit(solution)/shard_map/ppermute | solution.py:590
  83.0 2.7 %collective-permute-start.32 = (bf16[432,256]{1,0:T(8,128)(2,1)S(1)}, bf16[432,256]{1,0:T(8,128)(2,1)S(1)}, u32[]{:S(2)}, u32[]{:S(2)}) collective-permute-start(bf16[432,256]{1,0:T(8,128)(2,1)S(1)} %shard_map.123.refs_1_), channel_id=1, source_target_pairs={{0,1},{1,0},{2,3},{3,2},{4,5},{5,4},{6,7},{7,6},{8,9},{9,8},{10,11... | collective-permute-start | bytes 663560 | tf_op jit(solution)/shard_map/ppermute | solution.py:590
  86.3 5.1 %collective-permute-start.31 = (bf16[432,256]{1,0:T(8,128)(2,1)S(1)}, bf16[432,256]{1,0:T(8,128)(2,1)S(1)}, u32[]{:S(2)}, u32[]{:S(2)}) collective-permute-start(bf16[432,256]{1,0:T(8,128)(2,1)S(1)} %collective-permute-done.28.refs_3_), channel_id=1, source_target_pairs={{0,1},{1,0},{2,3},{3,2},{4,5},{5,4},{6,7},{7,6},{8,9},{9,8},{10,11... | collective-permute-start | bytes 663560 | tf_op jit(solution)/shard_map/ppermute | solution.py:590
  91.4 1.6 %collective-permute-start.30 = (bf16[432,256]{1,0:T(8,128)(2,1)S(1)}, bf16[432,256]{1,0:T(8,128)(2,1)S(1)}, u32[]{:S(2)}, u32[]{:S(2)}) collective-permute-start(bf16[432,256]{1,0:T(8,128)(2,1)S(1)} %collective-permute-done.27.refs_2_), channel_id=1, source_target_pairs={{0,1},{1,0},{2,3},{3,2},{4,5},{5,4},{6,7},{7,6},{8,9},{9,8},{10,11... | collective-permute-start | bytes 663560 | tf_op jit(solution)/shard_map/ppermute | solution.py:590
  95.3 2.2 %shard_map.125 = (f32[9,8,32,256]{3,2,1,0:T(8,128)}, f32[8,144,256]{2,1,0:T(8,128)}) custom-call(s32[6]{0:T(128)S(1)} %stack.35.refs_0_, bf16[432,256]{1,0:T(8,128)(2,1)S(1)} %collective-permute-done.26.refs_1_, bf16[432,256]{1,0:T(8,128)(2,1)S(1)} %collective-permute-done.27.refs_2_, ...), custom_call_target="tpu_custom_call", output_to_operand_aliasing={{0}: (7, {}), {1}: (8, {})} | custom-call | bytes 8405016 | tf_op jit(solution)/shard_map/pallas_call | solution.py:29
  (76 shorter events, 30.8 us)
Async XLA Ops:
  6.0 8.9 %collective-permute-start.3 = (bf16[384,128]{1,0:T(8,128)(2,1)S(1)}, bf16[384,128]{1,0:T(8,128)(2,1)S(1)}, u32[]{:S(2)}, u32[]{:S(2)}) collective-permute-start(bf16[384,128]{1,0:T(8,128)(2,1)S(1)} %get-tuple-element.63), channel_id=1, source_target_pairs={{0,4},{1,5},{2,14},{3,15},{4,0},{5,1},{14,2},{15,3},{16,20},{17,21... | collective-permute-start | bytes 294920 | tf_op jit(solution)/shard_map/ppermute | solution.py:601
  10.8 5.3 %collective-permute-start.2 = (bf16[384,128]{1,0:T(8,128)(2,1)S(1)}, bf16[384,128]{1,0:T(8,128)(2,1)S(1)}, u32[]{:S(2)}, u32[]{:S(2)}) collective-permute-start(bf16[384,128]{1,0:T(8,128)(2,1)S(1)} %get-tuple-element.58.refs_2_.refs_4_), channel_id=1, source_target_pairs={{0,12},{1,13},{2,6},{3,7},{4,8},{5,9},{6,2},{7,3},{8,4},{9,5},{10,... | collective-permute-start | bytes 294920 | tf_op jit(solution)/shard_map/ppermute | solution.py:601
  17.2 8.2 %collective-permute-start.4 = (f32[2,256]{1,0:T(2,128)S(1)}, f32[2,256]{1,0:T(2,128)S(1)}, u32[]{:S(2)}, u32[]{:S(2)}) collective-permute-start(f32[2,256]{1,0:T(2,128)S(1)} %get-tuple-element.65.refs_0_), channel_id=1, source_target_pairs={{0,1},{1,0},{2,3},{3,2},{4,5},{5,4},{6,7},{7,6},{8,9},{9,8},{10,11... | collective-permute-start | bytes 6152 | tf_op jit(solution)/shard_map/ppermute | solution.py:590
  25.4 3.7 %collective-permute-start.7 = (f32[2,256]{1,0:T(2,128)S(1)}, f32[2,256]{1,0:T(2,128)S(1)}, u32[]{:S(2)}, u32[]{:S(2)}) collective-permute-start(f32[2,256]{1,0:T(2,128)S(1)} %shard_map.107.refs_0_), channel_id=1, source_target_pairs={{0,6},{1,7},{2,4},{3,5},{4,2},{5,3},{6,0},{7,1},{8,14},{9,15},{10,... | collective-permute-start | bytes 6152 | tf_op jit(solution)/shard_map/ppermute | solution.py:590
  30.8 3.3 %collective-permute-start.8 = (f32[2,256]{1,0:T(2,128)S(1)}, f32[2,256]{1,0:T(2,128)S(1)}, u32[]{:S(2)}, u32[]{:S(2)}) collective-permute-start(f32[2,256]{1,0:T(2,128)S(1)} %shard_map.108.refs_0_), channel_id=1, source_target_pairs={{0,8},{1,9},{2,10},{3,11},{4,12},{5,13},{6,14},{7,15},{8,0},{9,1},... | collective-permute-start | bytes 6152 | tf_op jit(solution)/shard_map/ppermute | solution.py:590
  38.1 4.7 %collective-permute-start.13 = (bf16[4,288,256]{2,1,0:T(8,128)(2,1)S(1)}, bf16[4,288,256]{2,1,0:T(8,128)(2,1)S(1)}, u32[]{:S(2)}, u32[]{:S(2)}) collective-permute-start(bf16[4,288,256]{2,1,0:T(8,128)(2,1)S(1)} %get-tuple-element.75.refs_2_), channel_id=1, source_target_pairs={{0,1},{1,0},{2,3},{3,2},{4,5},{5,4},{6,7},{7,6},{8,9},{9,8},{10,11... | collective-permute-start | bytes 1769480 | tf_op jit(solution)/shard_map/ppermute | solution.py:590
  43.5 6.0 %collective-permute-start.15 = (bf16[2,288,256]{2,1,0:T(8,128)(2,1)S(1)}, bf16[2,288,256]{2,1,0:T(8,128)(2,1)S(1)}, u32[]{:S(2)}, u32[]{:S(2)}) collective-permute-start(bf16[2,288,256]{2,1,0:T(8,128)(2,1)S(1)} %get-tuple-element.82), channel_id=1, source_target_pairs={{0,16},{1,3},{2,18},{3,1},{4,20},{5,7},{6,22},{7,5},{8,24},{9,11},... | collective-permute-start | bytes 884744 | tf_op jit(solution)/shard_map/ppermute | solution.py:614
  43.6 3.5 %collective-permute-start.12 = (f32[2,256]{1,0:T(2,128)S(1)}, f32[2,256]{1,0:T(2,128)S(1)}, u32[]{:S(2)}, u32[]{:S(2)}) collective-permute-start(f32[2,256]{1,0:T(2,128)S(1)} %shard_map.112.refs_3_.refs_0_), channel_id=1, source_target_pairs={{0,6},{1,7},{2,4},{3,5},{4,2},{5,3},{6,0},{7,1},{8,14},{9,15},{10,... | collective-permute-start | bytes 6152 | tf_op jit(solution)/shard_map/ppermute | solution.py:590
  49.6 4.1 %collective-permute-start.16 = (bf16[288,256]{1,0:T(8,128)(2,1)S(1)}, bf16[288,256]{1,0:T(8,128)(2,1)S(1)}, u32[]{:S(2)}, u32[]{:S(2)}) collective-permute-start(bf16[288,256]{1,0:T(8,128)(2,1)S(1)} %get-tuple-element.84), channel_id=1, source_target_pairs={{0,2},{1,17},{2,0},{3,19},{4,6},{5,21},{6,4},{7,23},{8,10},{9,25},... | collective-permute-start | bytes 442376 | tf_op jit(solution)/shard_map/ppermute | solution.py:614
  56.9 4.3 %collective-permute-start.19 = (bf16[4,144,256]{2,1,0:T(8,128)(2,1)S(1)}, bf16[4,144,256]{2,1,0:T(8,128)(2,1)S(1)}, u32[]{:S(2)}, u32[]{:S(2)}) collective-permute-start(bf16[4,144,256]{2,1,0:T(8,128)(2,1)S(1)} %get-tuple-element.89), channel_id=1, source_target_pairs={{0,1},{1,0},{2,3},{3,2},{4,5},{5,4},{6,7},{7,6},{8,9},{9,8},{10,11... | collective-permute-start | bytes 884744 | tf_op jit(solution)/shard_map/ppermute | solution.py:590
  59.8 5.4 %collective-permute-start.17 = (bf16[288,256]{1,0:T(8,128)(2,1)S(1)}, bf16[288,256]{1,0:T(8,128)(2,1)S(1)}, u32[]{:S(2)}, u32[]{:S(2)}) collective-permute-start(bf16[288,256]{1,0:T(8,128)(2,1)S(1)} %shard_map.117.refs_11_.refs_0_), channel_id=1, source_target_pairs={{0,4},{1,5},{2,6},{3,7},{4,0},{5,1},{6,2},{7,3},{8,12},{9,13},{10,... | collective-permute-start | bytes 442376 | tf_op jit(solution)/shard_map/ppermute | solution.py:590
  61.2 5.4 %collective-permute-start.21 = (bf16[160,256]{1,0:T(8,128)(2,1)S(1)}, bf16[160,256]{1,0:T(8,128)(2,1)S(1)}, u32[]{:S(2)}, u32[]{:S(2)}) collective-permute-start(bf16[160,256]{1,0:T(8,128)(2,1)S(1)} %get-tuple-element.93), channel_id=1, source_target_pairs={{0,16},{1,17},{2,18},{3,19},{4,20},{5,21},{6,22},{7,23},{8,24},{9,... | collective-permute-start | bytes 245768 | tf_op jit(solution)/shard_map/ppermute | solution.py:590
  61.5 4.5 %collective-permute-start.20 = (bf16[144,256]{1,0:T(8,128)(2,1)S(1)}, bf16[144,256]{1,0:T(8,128)(2,1)S(1)}, u32[]{:S(2)}, u32[]{:S(2)}) collective-permute-start(bf16[144,256]{1,0:T(8,128)(2,1)S(1)} %get-tuple-element.92), channel_id=1, source_target_pairs={{0,2},{1,3},{2,0},{3,1},{4,6},{5,7},{6,4},{7,5},{8,10},{9,11},{10,... | collective-permute-start | bytes 221192 | tf_op jit(solution)/shard_map/ppermute | solution.py:590
  62.4 4.2 %collective-permute-start.22 = (bf16[144,256]{1,0:T(8,128)(2,1)S(1)}, bf16[144,256]{1,0:T(8,128)(2,1)S(1)}, u32[]{:S(2)}, u32[]{:S(2)}) collective-permute-start(bf16[144,256]{1,0:T(8,128)(2,1)S(1)} %get-tuple-element.94), channel_id=1, source_target_pairs={{0,18},{1,19},{2,16},{3,17},{4,22},{5,23},{6,20},{7,21},{8,26},{9,... | collective-permute-start | bytes 221192 | tf_op jit(solution)/shard_map/ppermute | solution.py:590
  65.3 12.0 %collective-permute-start.18 = (bf16[288,256]{1,0:T(8,128)(2,1)S(1)}, bf16[288,256]{1,0:T(8,128)(2,1)S(1)}, u32[]{:S(2)}, u32[]{:S(2)}) collective-permute-start(bf16[288,256]{1,0:T(8,128)(2,1)S(1)} %shard_map.120.refs_0_), channel_id=1, source_target_pairs={{0,8},{1,9},{2,10},{3,11},{4,12},{5,13},{6,14},{7,15},{8,0},{9,1},... | collective-permute-start | bytes 442376 | tf_op jit(solution)/shard_map/ppermute | solution.py:590
  67.2 10.1 %collective-permute-start.25 = (bf16[144,256]{1,0:T(8,128)(2,1)S(1)}, bf16[144,256]{1,0:T(8,128)(2,1)S(1)}, u32[]{:S(2)}, u32[]{:S(2)}) collective-permute-start(bf16[144,256]{1,0:T(8,128)(2,1)S(1)} %get-tuple-element.95.refs_2_), channel_id=1, source_target_pairs={{0,12},{1,13},{2,14},{3,15},{4,8},{5,9},{6,10},{7,11},{8,4},{9,5},... | collective-permute-start | bytes 221192 | tf_op jit(solution)/shard_map/ppermute | solution.py:590
  69.4 10.8 %collective-permute-start.24 = (bf16[144,256]{1,0:T(8,128)(2,1)S(1)}, bf16[144,256]{1,0:T(8,128)(2,1)S(1)}, u32[]{:S(2)}, u32[]{:S(2)}) collective-permute-start(bf16[144,256]{1,0:T(8,128)(2,1)S(1)} %get-tuple-element.95.refs_2_), channel_id=1, source_target_pairs={{0,8},{1,9},{2,10},{3,11},{4,12},{5,13},{6,14},{7,15},{8,0},{9,1},... | collective-permute-start | bytes 221192 | tf_op jit(solution)/shard_map/ppermute | solution.py:590
  69.6 10.6 %collective-permute-start.23 = (bf16[144,256]{1,0:T(8,128)(2,1)S(1)}, bf16[144,256]{1,0:T(8,128)(2,1)S(1)}, u32[]{:S(2)}, u32[]{:S(2)}) collective-permute-start(bf16[144,256]{1,0:T(8,128)(2,1)S(1)} %get-tuple-element.95.refs_2_), channel_id=1, source_target_pairs={{0,4},{1,5},{2,6},{3,7},{4,0},{5,1},{6,2},{7,3},{8,12},{9,13},{10,... | collective-permute-start | bytes 221192 | tf_op jit(solution)/shard_map/ppermute | solution.py:590
  80.3 6.1 %collective-permute-start.28 = (bf16[432,256]{1,0:T(8,128)(2,1)S(1)}, bf16[432,256]{1,0:T(8,128)(2,1)S(1)}, u32[]{:S(2)}, u32[]{:S(2)}) collective-permute-start(bf16[432,256]{1,0:T(8,128)(2,1)S(1)} %shard_map.123.refs_1_), channel_id=1, source_target_pairs={{0,18},{1,19},{2,16},{3,17},{4,22},{5,23},{6,20},{7,21},{8,26},{9,... | collective-permute-start | bytes 663560 | tf_op jit(solution)/shard_map/ppermute | solution.py:590
  81.1 10.3 %collective-permute-start.27 = (bf16[432,256]{1,0:T(8,128)(2,1)S(1)}, bf16[432,256]{1,0:T(8,128)(2,1)S(1)}, u32[]{:S(2)}, u32[]{:S(2)}) collective-permute-start(bf16[432,256]{1,0:T(8,128)(2,1)S(1)} %shard_map.123.refs_1_), channel_id=1, source_target_pairs={{0,16},{1,17},{2,18},{3,19},{4,20},{5,21},{6,22},{7,23},{8,24},{9,... | collective-permute-start | bytes 663560 | tf_op jit(solution)/shard_map/ppermute | solution.py:590
  81.9 11.1 %collective-permute-start.26 = (bf16[432,256]{1,0:T(8,128)(2,1)S(1)}, bf16[432,256]{1,0:T(8,128)(2,1)S(1)}, u32[]{:S(2)}, u32[]{:S(2)}) collective-permute-start(bf16[432,256]{1,0:T(8,128)(2,1)S(1)} %shard_map.123.refs_1_), channel_id=1, source_target_pairs={{0,2},{1,3},{2,0},{3,1},{4,6},{5,7},{6,4},{7,5},{8,10},{9,11},{10,... | collective-permute-start | bytes 663560 | tf_op jit(solution)/shard_map/ppermute | solution.py:590
  83.0 10.8 %collective-permute-start.32 = (bf16[432,256]{1,0:T(8,128)(2,1)S(1)}, bf16[432,256]{1,0:T(8,128)(2,1)S(1)}, u32[]{:S(2)}, u32[]{:S(2)}) collective-permute-start(bf16[432,256]{1,0:T(8,128)(2,1)S(1)} %shard_map.123.refs_1_), channel_id=1, source_target_pairs={{0,1},{1,0},{2,3},{3,2},{4,5},{5,4},{6,7},{7,6},{8,9},{9,8},{10,11... | collective-permute-start | bytes 663560 | tf_op jit(solution)/shard_map/ppermute | solution.py:590
  86.3 9.0 %collective-permute-start.31 = (bf16[432,256]{1,0:T(8,128)(2,1)S(1)}, bf16[432,256]{1,0:T(8,128)(2,1)S(1)}, u32[]{:S(2)}, u32[]{:S(2)}) collective-permute-start(bf16[432,256]{1,0:T(8,128)(2,1)S(1)} %collective-permute-done.28.refs_3_), channel_id=1, source_target_pairs={{0,1},{1,0},{2,3},{3,2},{4,5},{5,4},{6,7},{7,6},{8,9},{9,8},{10,11... | collective-permute-start | bytes 663560 | tf_op jit(solution)/shard_map/ppermute | solution.py:590
  91.4 3.9 %collective-permute-start.30 = (bf16[432,256]{1,0:T(8,128)(2,1)S(1)}, bf16[432,256]{1,0:T(8,128)(2,1)S(1)}, u32[]{:S(2)}, u32[]{:S(2)}) collective-permute-start(bf16[432,256]{1,0:T(8,128)(2,1)S(1)} %collective-permute-done.27.refs_2_), channel_id=1, source_target_pairs={{0,1},{1,0},{2,3},{3,2},{4,5},{5,4},{6,7},{7,6},{8,9},{9,8},{10,11... | collective-permute-start | bytes 663560 | tf_op jit(solution)/shard_map/ppermute | solution.py:590
  (13 other events, 42.0 us)

commit v5 on v4

--- a/solution.py
+++ b/solution.py
@@ -80,13 +80,13 @@
         copy.start()
 
     def x_column(ref, index):
-        wide[...] = ref[...].astype(F32).reshape(2 * rows * 16, cin)
+        wide[0 : 2 * rows * 16, :] = ref[...].astype(F32).reshape(2 * rows * 16, cin)
         return wide[pl.ds(index, 2 * rows, stride=16), :]
 
     def g_column(ref, index):
         halves = []
         for half in range(ref.shape[2] // 128):
-            flat[...] = ref[:, :, half * 128 : (half + 1) * 128].astype(F32).reshape(rows * 16, 128)
+            flat[0 : rows * 16, :] = ref[:, :, half * 128 : (half + 1) * 128].astype(F32).reshape(rows * 16, 128)
             halves.append(flat[pl.ds(index, rows, stride=16), :])
         return jnp.concatenate(halves, 0)
 
@@ -171,11 +171,11 @@
     ]
     for copy in copies:
         copy.start()
-    wide[:, 0:8, :] = jnp.zeros((2 * step, 8, cin), F32)
+    wide[0 : 2 * step, 0:8, :] = jnp.zeros((2 * step, 8, cin), F32)
 
     def deinterleave(i):
         copies[i].wait()
-        wide[:, 8 : 8 + 2 * cols, :] = held[i].astype(F32)
+        wide[0 : 2 * step, 8 : 8 + 2 * cols, :] = held[i].astype(F32)
         row = (i * step + 1) * cols
         for parity in range(2):
             for slot, first in enumerate((7, 8, 9)):
@@ -234,13 +234,13 @@
     z = z_ref[...]
     stats_ref[0:1, :] = jnp.sum(z, axis=0, keepdims=True)
     stats_ref[1:2, :] = jnp.sum(z * z, axis=0, keepdims=True)
-    bottom[0] = own_row_ref[0:line, :].astype(F32)
-    bottom[1] = below_ref[0:line, :].astype(F32)
-    bottom[2] = below_ref[line : 2 * line, :].astype(F32)
+    bottom[0, 0:line, :] = own_row_ref[0:line, :].astype(F32)
+    bottom[1, 0:line, :] = below_ref[0:line, :].astype(F32)
+    bottom[2, 0:line, :] = below_ref[line : 2 * line, :].astype(F32)
     over_end = xrow_ref[2 * cols : 2 * cols + 32, :].astype(F32)
     for b, ref in enumerate((own_col_ref, right_ref, right_ref)):
         first = 2 * rows if b == 2 else 0
-        side[b, 8:, :] = ref[first : first + 2 * rows, :].astype(F32)
+        side[b, 8 : 8 + 2 * rows, :] = ref[first : first + 2 * rows, :].astype(F32)
         side[b, 7:8, :] = over_end[15 + b : 16 + b, :]
     parts = []
     for a in range(3):
@@ -494,7 +494,9 @@
                 mixed[pl.ds(parity, step, stride=2), pl.ds(side, cols, stride=2), :] = pair[side].reshape(
                     step, cols, cin
                 )
-        out_ref[pl.ds(pl.multiple_of(i * 2 * step, 2 * step), 2 * step)] = mixed[...].astype(BF16)
+        out_ref[pl.ds(pl.multiple_of(i * 2 * step, 2 * step), 2 * step)] = mixed[
+            0 : 2 * step, 0 : 2 * cols, :
+        ].astype(BF16)
         return carry
 
     lax.fori_loop(0, rows // step, chunk, 0)
@@ -665,7 +667,11 @@
         [place, x, g3],
         [pltpu.VMEM((2 * rows, 16, cin), BF16)] * 2
         + [pltpu.VMEM((rows, 16, depth), BF16)] * 2
-        + [pltpu.VMEM((2 * rows * 16, cin), F32), pltpu.VMEM((rows * 16, 128), F32), pltpu.SemaphoreType.DMA((8,))],
+        + [
+            pltpu.VMEM((2 * rows * 16 + 16, cin), F32),
+            pltpu.VMEM((rows * 16 + 16, 128), F32),
+            pltpu.SemaphoreType.DMA((8,)),
+        ],
         specs=[smem, hbm, hbm],
     )
     one = swapped(one, 0, 1)
@@ -675,7 +681,7 @@
         [shape((cells + cols, 6 * cin), BF16)],
         [x],
         [
-            pltpu.VMEM((2 * CHUNK // cols, 2 * cols + 8, cin), F32),
+            pltpu.VMEM((2 * CHUNK // cols + 2, 2 * cols + 16, cin), F32),
             pltpu.VMEM((cells // CHUNK, 2 * CHUNK // cols, 2 * cols, cin), BF16),
             pltpu.SemaphoreType.DMA((cells // CHUNK,)),
         ],
@@ -701,7 +707,7 @@
         flops=2 * cells * 9 * cin * depth,
         after=[one],
     )
-    pads = [pltpu.VMEM((2 * rows + 8, cin), F32), pltpu.VMEM((2 * cols + 8, cin), F32)]
+    pads = [pltpu.VMEM((2 * rows + 16, cin), F32), pltpu.VMEM((2 * cols + 16, cin), F32)]
     body, w_t, prepared = call(
         functools.partial(prepare_kernel, rows, cols),
         [shape((3, cells, depth), BF16), shape((9 * depth, depth), BF16), shape((8, 128), F32)],
@@ -723,8 +729,8 @@
         pads
         + [
             pltpu.VMEM((rows, depth), F32),
-            pltpu.VMEM((3, 2 * cols + 32, cin), F32),
-            pltpu.VMEM((3, 2 * rows + 8, cin), F32),
+            pltpu.VMEM((3, 2 * cols + 40, cin), F32),
+            pltpu.VMEM((3, 2 * rows + 16, cin), F32),
         ],
         smem=1,
         after=[prepared],
@@ -812,7 +818,7 @@
             pltpu.VMEM((cells + cols, depth), BF16),
             pltpu.VMEM((depth, 9 * cin), BF16),
             pltpu.VMEM(((rows + 1) * (cols + 8), depth), F32),
-            pltpu.VMEM((2 * CHUNK // cols, 2 * cols, cin), F32),
+            pltpu.VMEM((2 * CHUNK // cols + 2, 2 * cols + 8, cin), F32),
         ],
         flops=2 * cells * 9 * cin * depth,
     )

time: 97.8 us -> 97.8 us (level)
  no operation moved by 1% of the time
where the time goes in v5:
time: 97.8 us; the launch traced here: 97.5 us
  starting transfers between devices  49.3 us (50%)
  Pallas kernels  27.8 us (28%)
  waiting for transfers between devices  19.4 us (20%)
    ppermute x27, starting transfers between devices, flip(): return lax.ppermute(value, axes, [(i, i ^ mask) for i in range(devices)])  41.5 us
    pallas_call x25, Pallas kernels, call(): pl.pallas_call(body, out_shape=list(outs), grid=grid, in_specs=list(specs...  27.8 us
    ppermute x27, waiting for transfers between devices, flip(): return lax.ppermute(value, axes, [(i, i ^ mask) for i in range(devices)])  16.9 us
    ppermute x4, starting transfers between devices, swapped(): return lax.ppermute(value, 'space', pairs)  6.41 us
  transfers between devices with their start and end apart: 33, of which 17 were waited for; matrix products, arithmetic and copies ran while one was open for 0% of the time, Pallas kernels for 15%

profile of v5, /device:TPU:1, one launch (start us, length us, event | category | flops | bytes accessed | tf_op | source)
XLA Modules:
  0.0 97.5 jit_solution(17514929373841983)
XLA Ops:
  0.8 2.1 %shard_map.102 = (bf16[384,128]{1,0:T(8,128)(2,1)S(1)}, bf16[384,128]{1,0:T(8,128)(2,1)S(1)}, bf16[192,128]{1,0:T(8,128)(2,1)S(1)}, bf16[3,64,128]{2,1,0:T(8,128)(2,1)S(1)}, bf16[3,32,256]{2,1,0:T(8,128)(2,1)S(1)}) custom-call(s32[6]{0:T(128)S(1)} %stack.35.refs_0_, bf16[96,64,128]{2,1,0:T(8,128)(2,1)} %bitcast.25, bf16[48,32,256]{2,1,0:T(8,128)(2,1)} %bitcast.27), custom_call_target="tpu_custom_call" | custom-call | bytes 2703384 | tf_op jit(solution)/shard_map/pallas_call | solution.py:29
  3.7 1.6 %shard_map.101.refs_5_.refs_0_ = bf16[1568,768]{1,0:T(8,128)(2,1)S(1)} custom-call(bf16[96,64,128]{2,1,0:T(8,128)(2,1)} %bitcast.26), custom_call_target="tpu_custom_call" | custom-call | flops 452984832 | bytes 3981312 | tf_op jit(solution)/shard_map/pallas_call | solution.py:29
  6.0 4.8 %collective-permute-start.3 = (bf16[384,128]{1,0:T(8,128)(2,1)S(1)}, bf16[384,128]{1,0:T(8,128)(2,1)S(1)}, u32[]{:S(2)}, u32[]{:S(2)}) collective-permute-start(bf16[384,128]{1,0:T(8,128)(2,1)S(1)} %get-tuple-element.63), channel_id=1, source_target_pairs={{0,4},{1,5},{2,14},{3,15},{4,0},{5,1},{14,2},{15,3},{16,20},{17,21... | collective-permute-start | bytes 294920 | tf_op jit(solution)/shard_map/ppermute | solution.py:603
  11.7 1.7 %shard_map.105 = (bf16[3,1536,256]{2,1,0:T(8,128)(2,1)S(1)}, bf16[2304,256]{1,0:T(8,128)(2,1)S(1)}, f32[8,128]{1,0:T(8,128)S(1)}) custom-call(bf16[48,32,256]{2,1,0:T(8,128)(2,1)} %bitcast.28, bf16[192,128]{1,0:T(8,128)(2,1)S(1)} %get-tuple-element.59.refs_1_.refs_2_, bf16[384,128]{1,0:T(8,128)(2,1)S(1)} %get-tuple-element.60.refs_2_.refs_3_, ...), custom_call_target="tpu_custom_call" | custom-call | bytes 5656576 | tf_op jit(solution)/shard_map/pallas_call | solution.py:29
  13.4 1.5 %shard_map.104.refs_1_ = f32[1536,256]{1,0:T(8,128)S(1)} custom-call(bf16[1568,768]{1,0:T(8,128)(2,1)S(1)} %shard_map.101.refs_5_.refs_0_, bf16[1152,256]{1,0:T(8,128)(2,1)S(1)} %bitcast.17, bf16[384,128]{1,0:T(8,128)(2,1)S(1)} %get-tuple-element.58.refs_2_.refs_4_), custom_call_target="tpu_custom_call" | custom-call | flops 905969664 | bytes 4571136 | tf_op jit(solution)/shard_map/pallas_call | solution.py:29
  17.2 7.4 %collective-permute-start.4 = (f32[2,256]{1,0:T(2,128)S(1)}, f32[2,256]{1,0:T(2,128)S(1)}, u32[]{:S(2)}, u32[]{:S(2)}) collective-permute-start(f32[2,256]{1,0:T(2,128)S(1)} %get-tuple-element.65.refs_0_), channel_id=1, source_target_pairs={{0,1},{1,0},{2,3},{3,2},{4,5},{5,4},{6,7},{7,6},{8,9},{9,8},{10,11... | collective-permute-start | bytes 6152 | tf_op jit(solution)/shard_map/ppermute | solution.py:592
  25.4 2.8 %collective-permute-start.7 = (f32[2,256]{1,0:T(2,128)S(1)}, f32[2,256]{1,0:T(2,128)S(1)}, u32[]{:S(2)}, u32[]{:S(2)}) collective-permute-start(f32[2,256]{1,0:T(2,128)S(1)} %shard_map.107.refs_0_), channel_id=1, source_target_pairs={{0,6},{1,7},{2,4},{3,5},{4,2},{5,3},{6,0},{7,1},{8,14},{9,15},{10,... | collective-permute-start | bytes 6152 | tf_op jit(solution)/shard_map/ppermute | solution.py:592
  31.4 2.2 %shard_map.109 = (bf16[3,64,256]{2,1,0:T(8,128)(2,1)S(1)}, f32[1536,256]{1,0:T(8,128)S(1)}, f32[88,256]{1,0:T(8,128)S(1)}) custom-call(bf16[3,1536,256]{2,1,0:T(8,128)(2,1)S(1)} %get-tuple-element.67.refs_0_.refs_2_, bf16[2304,256]{1,0:T(8,128)(2,1)S(1)} %get-tuple-element.68.refs_1_, bf16[384,128]{1,0:T(8,128)(2,1)S(1)} %get-tuple-element.60.refs_2_.refs_3_, ...), custom_call_target="tpu_custom_call" | custom-call | flops 1811939328 | bytes 5644288 | tf_op jit(solution)/shard_map/pallas_call | solution.py:29
  35.5 2.6 %shard_map.111 = (f32[4,288,256]{2,1,0:T(8,128)S(1)}, bf16[4,288,256]{2,1,0:T(8,128)(2,1)S(1)}) custom-call(s32[6]{0:T(128)S(1)} %stack.35.refs_0_, bf16[1536,256]{1,0:T(8,128)(2,1)S(1)} %get-tuple-element.73.refs_1_, bf16[3,1536,256]{2,1,0:T(8,128)(2,1)S(1)} %get-tuple-element.67.refs_0_.refs_2_, bf16[3,64,256]{2,1,0:T(8,128)(2,1)S(1)} %get-tuple-element.74.refs_3_), custom_call_target="tpu_custom_call" | custom-call | flops 1811939328 | bytes 5013528 | tf_op jit(solution)/shard_map/pallas_call | solution.py:29
  38.1 3.1 %collective-permute-start.13 = (bf16[4,288,256]{2,1,0:T(8,128)(2,1)S(1)}, bf16[4,288,256]{2,1,0:T(8,128)(2,1)S(1)}, u32[]{:S(2)}, u32[]{:S(2)}) collective-permute-start(bf16[4,288,256]{2,1,0:T(8,128)(2,1)S(1)} %get-tuple-element.75.refs_2_), channel_id=1, source_target_pairs={{0,1},{1,0},{2,3},{3,2},{4,5},{5,4},{6,7},{7,6},{8,9},{9,8},{10,11... | collective-permute-start | bytes 1769480 | tf_op jit(solution)/shard_map/ppermute | solution.py:592
  41.3 1.6 %collective-permute-done.9.refs_1_ = f32[2,256]{1,0:T(2,128)S(1)} collective-permute-done((f32[2,256]{1,0:T(2,128)S(1)}, f32[2,256]{1,0:T(2,128)S(1)}, u32[]{:S(2)}, u32[]{:S(2)}) %collective-permute-start.9) | collective-permute-done | bytes 2080 | tf_op jit(solution)/shard_map/ppermute | solution.py:592
  43.6 2.5 %collective-permute-start.12 = (f32[2,256]{1,0:T(2,128)S(1)}, f32[2,256]{1,0:T(2,128)S(1)}, u32[]{:S(2)}, u32[]{:S(2)}) collective-permute-start(f32[2,256]{1,0:T(2,128)S(1)} %shard_map.112.refs_3_.refs_0_), channel_id=1, source_target_pairs={{0,6},{1,7},{2,4},{3,5},{4,2},{5,3},{6,0},{7,1},{8,14},{9,15},{10,... | collective-permute-start | bytes 6152 | tf_op jit(solution)/shard_map/ppermute | solution.py:592
  47.1 1.7 %collective-permute-done.11.refs_2_ = f32[2,256]{1,0:T(2,128)S(1)} collective-permute-done((f32[2,256]{1,0:T(2,128)S(1)}, f32[2,256]{1,0:T(2,128)S(1)}, u32[]{:S(2)}, u32[]{:S(2)}) %collective-permute-start.11) | collective-permute-done | bytes 2080 | tf_op jit(solution)/shard_map/ppermute | solution.py:592
  54.2 2.6 %shard_map.118 = (bf16[1536,256]{1,0:T(8,128)(2,1)S(1)}, f32[88,256]{1,0:T(8,128)S(1)}, f32[2,256]{1,0:T(2,128)S(1)}, f32[4,144,256]{2,1,0:T(8,128)S(1)}, bf16[4,144,256]{2,1,0:T(8,128)(2,1)S(1)}) custom-call(s32[6]{0:T(128)S(1)} %stack.35.refs_0_, f32[2,256]{1,0:T(2,128)S(1)} %shard_map.114.refs_2_.refs_1_, f32[2,256]{1,0:T(2,128)S(1)} %collective-permute-done.14.refs_2_, ...), custom_call_target="tpu_custom_call" | custom-call | flops 905969664 | bytes 8636440 | tf_op jit(solution)/shard_map/pallas_call | solution.py:29
  56.8 3.0 %collective-permute-start.19 = (bf16[4,144,256]{2,1,0:T(8,128)(2,1)S(1)}, bf16[4,144,256]{2,1,0:T(8,128)(2,1)S(1)}, u32[]{:S(2)}, u32[]{:S(2)}) collective-permute-start(bf16[4,144,256]{2,1,0:T(8,128)(2,1)S(1)} %get-tuple-element.89), channel_id=1, source_target_pairs={{0,1},{1,0},{2,3},{3,2},{4,5},{5,4},{6,7},{7,6},{8,9},{9,8},{10,11... | collective-permute-start | bytes 884744 | tf_op jit(solution)/shard_map/ppermute | solution.py:592
  62.4 1.5 %collective-permute-start.22 = (bf16[144,256]{1,0:T(8,128)(2,1)S(1)}, bf16[144,256]{1,0:T(8,128)(2,1)S(1)}, u32[]{:S(2)}, u32[]{:S(2)}) collective-permute-start(bf16[144,256]{1,0:T(8,128)(2,1)S(1)} %get-tuple-element.94), channel_id=1, source_target_pairs={{0,18},{1,19},{2,16},{3,17},{4,22},{5,23},{6,20},{7,21},{8,26},{9,... | collective-permute-start | bytes 221192 | tf_op jit(solution)/shard_map/ppermute | solution.py:592
  67.2 2.2 %collective-permute-start.25 = (bf16[144,256]{1,0:T(8,128)(2,1)S(1)}, bf16[144,256]{1,0:T(8,128)(2,1)S(1)}, u32[]{:S(2)}, u32[]{:S(2)}) collective-permute-start(bf16[144,256]{1,0:T(8,128)(2,1)S(1)} %get-tuple-element.95.refs_2_), channel_id=1, source_target_pairs={{0,12},{1,13},{2,14},{3,15},{4,8},{5,9},{6,10},{7,11},{8,4},{9,5},... | collective-permute-start | bytes 221192 | tf_op jit(solution)/shard_map/ppermute | solution.py:592
  70.7 4.1 %shard_map.119 = (bf16[96,64,128]{2,1,0:T(8,128)(2,1)}, f32[8,128]{1,0:T(8,128)S(1)}) custom-call(bf16[1536,256]{1,0:T(8,128)(2,1)S(1)} %get-tuple-element.85.refs_0_, f32[88,256]{1,0:T(8,128)S(1)} %get-tuple-element.86.refs_1_, bf16[1152,256]{1,0:T(8,128)(2,1)S(1)} %bitcast.19), custom_call_target="tpu_custom_call" | custom-call | flops 905969664 | bytes 3043328 | tf_op jit(solution)/shard_map/pallas_call | solution.py:29
  74.8 2.5 %collective-permute-done.18.refs_1_ = bf16[288,256]{1,0:T(8,128)(2,1)S(1)} collective-permute-done((bf16[288,256]{1,0:T(8,128)(2,1)S(1)}, bf16[288,256]{1,0:T(8,128)(2,1)S(1)}, u32[]{:S(2)}, u32[]{:S(2)}) %collective-permute-start.18) | collective-permute-done | bytes 147488 | tf_op jit(solution)/shard_map/ppermute | solution.py:592
  77.3 2.9 %collective-permute-done.24.refs_4_ = bf16[144,256]{1,0:T(8,128)(2,1)S(1)} collective-permute-done((bf16[144,256]{1,0:T(8,128)(2,1)S(1)}, bf16[144,256]{1,0:T(8,128)(2,1)S(1)}, u32[]{:S(2)}, u32[]{:S(2)}) %collective-permute-start.24) | collective-permute-done | bytes 73760 | tf_op jit(solution)/shard_map/ppermute | solution.py:592
  83.0 2.7 %collective-permute-start.32 = (bf16[432,256]{1,0:T(8,128)(2,1)S(1)}, bf16[432,256]{1,0:T(8,128)(2,1)S(1)}, u32[]{:S(2)}, u32[]{:S(2)}) collective-permute-start(bf16[432,256]{1,0:T(8,128)(2,1)S(1)} %shard_map.123.refs_1_), channel_id=1, source_target_pairs={{0,1},{1,0},{2,3},{3,2},{4,5},{5,4},{6,7},{7,6},{8,9},{9,8},{10,11... | collective-permute-start | bytes 663560 | tf_op jit(solution)/shard_map/ppermute | solution.py:592
  86.3 5.1 %collective-permute-start.31 = (bf16[432,256]{1,0:T(8,128)(2,1)S(1)}, bf16[432,256]{1,0:T(8,128)(2,1)S(1)}, u32[]{:S(2)}, u32[]{:S(2)}) collective-permute-start(bf16[432,256]{1,0:T(8,128)(2,1)S(1)} %collective-permute-done.28.refs_3_), channel_id=1, source_target_pairs={{0,1},{1,0},{2,3},{3,2},{4,5},{5,4},{6,7},{7,6},{8,9},{9,8},{10,11... | collective-permute-start | bytes 663560 | tf_op jit(solution)/shard_map/ppermute | solution.py:592
  91.4 1.6 %collective-permute-start.30 = (bf16[432,256]{1,0:T(8,128)(2,1)S(1)}, bf16[432,256]{1,0:T(8,128)(2,1)S(1)}, u32[]{:S(2)}, u32[]{:S(2)}) collective-permute-start(bf16[432,256]{1,0:T(8,128)(2,1)S(1)} %collective-permute-done.27.refs_2_), channel_id=1, source_target_pairs={{0,1},{1,0},{2,3},{3,2},{4,5},{5,4},{6,7},{7,6},{8,9},{9,8},{10,11... | collective-permute-start | bytes 663560 | tf_op jit(solution)/shard_map/ppermute | solution.py:592
  95.3 2.2 %shard_map.125 = (f32[9,8,32,256]{3,2,1,0:T(8,128)}, f32[8,144,256]{2,1,0:T(8,128)}) custom-call(s32[6]{0:T(128)S(1)} %stack.35.refs_0_, bf16[432,256]{1,0:T(8,128)(2,1)S(1)} %collective-permute-done.26.refs_1_, bf16[432,256]{1,0:T(8,128)(2,1)S(1)} %collective-permute-done.27.refs_2_, ...), custom_call_target="tpu_custom_call", output_to_operand_aliasing={{0}: (7, {}), {1}: (8, {})} | custom-call | bytes 8405016 | tf_op jit(solution)/shard_map/pallas_call | solution.py:29
  (76 shorter events, 30.8 us)
Async XLA Ops:
  6.0 8.9 %collective-permute-start.3 = (bf16[384,128]{1,0:T(8,128)(2,1)S(1)}, bf16[384,128]{1,0:T(8,128)(2,1)S(1)}, u32[]{:S(2)}, u32[]{:S(2)}) collective-permute-start(bf16[384,128]{1,0:T(8,128)(2,1)S(1)} %get-tuple-element.63), channel_id=1, source_target_pairs={{0,4},{1,5},{2,14},{3,15},{4,0},{5,1},{14,2},{15,3},{16,20},{17,21... | collective-permute-start | bytes 294920 | tf_op jit(solution)/shard_map/ppermute | solution.py:603
  10.8 5.3 %collective-permute-start.2 = (bf16[384,128]{1,0:T(8,128)(2,1)S(1)}, bf16[384,128]{1,0:T(8,128)(2,1)S(1)}, u32[]{:S(2)}, u32[]{:S(2)}) collective-permute-start(bf16[384,128]{1,0:T(8,128)(2,1)S(1)} %get-tuple-element.58.refs_2_.refs_4_), channel_id=1, source_target_pairs={{0,12},{1,13},{2,6},{3,7},{4,8},{5,9},{6,2},{7,3},{8,4},{9,5},{10,... | collective-permute-start | bytes 294920 | tf_op jit(solution)/shard_map/ppermute | solution.py:603
  17.2 8.2 %collective-permute-start.4 = (f32[2,256]{1,0:T(2,128)S(1)}, f32[2,256]{1,0:T(2,128)S(1)}, u32[]{:S(2)}, u32[]{:S(2)}) collective-permute-start(f32[2,256]{1,0:T(2,128)S(1)} %get-tuple-element.65.refs_0_), channel_id=1, source_target_pairs={{0,1},{1,0},{2,3},{3,2},{4,5},{5,4},{6,7},{7,6},{8,9},{9,8},{10,11... | collective-permute-start | bytes 6152 | tf_op jit(solution)/shard_map/ppermute | solution.py:592
  25.4 3.7 %collective-permute-start.7 = (f32[2,256]{1,0:T(2,128)S(1)}, f32[2,256]{1,0:T(2,128)S(1)}, u32[]{:S(2)}, u32[]{:S(2)}) collective-permute-start(f32[2,256]{1,0:T(2,128)S(1)} %shard_map.107.refs_0_), channel_id=1, source_target_pairs={{0,6},{1,7},{2,4},{3,5},{4,2},{5,3},{6,0},{7,1},{8,14},{9,15},{10,... | collective-permute-start | bytes 6152 | tf_op jit(solution)/shard_map/ppermute | solution.py:592
  38.1 4.7 %collective-permute-start.13 = (bf16[4,288,256]{2,1,0:T(8,128)(2,1)S(1)}, bf16[4,288,256]{2,1,0:T(8,128)(2,1)S(1)}, u32[]{:S(2)}, u32[]{:S(2)}) collective-permute-start(bf16[4,288,256]{2,1,0:T(8,128)(2,1)S(1)} %get-tuple-element.75.refs_2_), channel_id=1, source_target_pairs={{0,1},{1,0},{2,3},{3,2},{4,5},{5,4},{6,7},{7,6},{8,9},{9,8},{10,11... | collective-permute-start | bytes 1769480 | tf_op jit(solution)/shard_map/ppermute | solution.py:592
  43.5 6.0 %collective-permute-start.15 = (bf16[2,288,256]{2,1,0:T(8,128)(2,1)S(1)}, bf16[2,288,256]{2,1,0:T(8,128)(2,1)S(1)}, u32[]{:S(2)}, u32[]{:S(2)}) collective-permute-start(bf16[2,288,256]{2,1,0:T(8,128)(2,1)S(1)} %get-tuple-element.82), channel_id=1, source_target_pairs={{0,16},{1,3},{2,18},{3,1},{4,20},{5,7},{6,22},{7,5},{8,24},{9,11},... | collective-permute-start | bytes 884744 | tf_op jit(solution)/shard_map/ppermute | solution.py:616
  43.6 3.5 %collective-permute-start.12 = (f32[2,256]{1,0:T(2,128)S(1)}, f32[2,256]{1,0:T(2,128)S(1)}, u32[]{:S(2)}, u32[]{:S(2)}) collective-permute-start(f32[2,256]{1,0:T(2,128)S(1)} %shard_map.112.refs_3_.refs_0_), channel_id=1, source_target_pairs={{0,6},{1,7},{2,4},{3,5},{4,2},{5,3},{6,0},{7,1},{8,14},{9,15},{10,... | collective-permute-start | bytes 6152 | tf_op jit(solution)/shard_map/ppermute | solution.py:592
  49.6 4.1 %collective-permute-start.16 = (bf16[288,256]{1,0:T(8,128)(2,1)S(1)}, bf16[288,256]{1,0:T(8,128)(2,1)S(1)}, u32[]{:S(2)}, u32[]{:S(2)}) collective-permute-start(bf16[288,256]{1,0:T(8,128)(2,1)S(1)} %get-tuple-element.84), channel_id=1, source_target_pairs={{0,2},{1,17},{2,0},{3,19},{4,6},{5,21},{6,4},{7,23},{8,10},{9,25},... | collective-permute-start | bytes 442376 | tf_op jit(solution)/shard_map/ppermute | solution.py:616
  50.9 3.3 %collective-permute-start.14 = (f32[2,256]{1,0:T(2,128)S(1)}, f32[2,256]{1,0:T(2,128)S(1)}, u32[]{:S(2)}, u32[]{:S(2)}) collective-permute-start(f32[2,256]{1,0:T(2,128)S(1)} %shard_map.114.refs_2_.refs_1_), channel_id=1, source_target_pairs={{0,8},{1,9},{2,10},{3,11},{4,12},{5,13},{6,14},{7,15},{8,0},{9,1},... | collective-permute-start | bytes 6152 | tf_op jit(solution)/shard_map/ppermute | solution.py:592
  56.8 4.3 %collective-permute-start.19 = (bf16[4,144,256]{2,1,0:T(8,128)(2,1)S(1)}, bf16[4,144,256]{2,1,0:T(8,128)(2,1)S(1)}, u32[]{:S(2)}, u32[]{:S(2)}) collective-permute-start(bf16[4,144,256]{2,1,0:T(8,128)(2,1)S(1)} %get-tuple-element.89), channel_id=1, source_target_pairs={{0,1},{1,0},{2,3},{3,2},{4,5},{5,4},{6,7},{7,6},{8,9},{9,8},{10,11... | collective-permute-start | bytes 884744 | tf_op jit(solution)/shard_map/ppermute | solution.py:592
  59.8 5.4 %collective-permute-start.17 = (bf16[288,256]{1,0:T(8,128)(2,1)S(1)}, bf16[288,256]{1,0:T(8,128)(2,1)S(1)}, u32[]{:S(2)}, u32[]{:S(2)}) collective-permute-start(bf16[288,256]{1,0:T(8,128)(2,1)S(1)} %shard_map.117.refs_11_.refs_0_), channel_id=1, source_target_pairs={{0,4},{1,5},{2,6},{3,7},{4,0},{5,1},{6,2},{7,3},{8,12},{9,13},{10,... | collective-permute-start | bytes 442376 | tf_op jit(solution)/shard_map/ppermute | solution.py:592
  61.2 5.4 %collective-permute-start.21 = (bf16[160,256]{1,0:T(8,128)(2,1)S(1)}, bf16[160,256]{1,0:T(8,128)(2,1)S(1)}, u32[]{:S(2)}, u32[]{:S(2)}) collective-permute-start(bf16[160,256]{1,0:T(8,128)(2,1)S(1)} %get-tuple-element.93), channel_id=1, source_target_pairs={{0,16},{1,17},{2,18},{3,19},{4,20},{5,21},{6,22},{7,23},{8,24},{9,... | collective-permute-start | bytes 245768 | tf_op jit(solution)/shard_map/ppermute | solution.py:592
  61.5 4.5 %collective-permute-start.20 = (bf16[144,256]{1,0:T(8,128)(2,1)S(1)}, bf16[144,256]{1,0:T(8,128)(2,1)S(1)}, u32[]{:S(2)}, u32[]{:S(2)}) collective-permute-start(bf16[144,256]{1,0:T(8,128)(2,1)S(1)} %get-tuple-element.92), channel_id=1, source_target_pairs={{0,2},{1,3},{2,0},{3,1},{4,6},{5,7},{6,4},{7,5},{8,10},{9,11},{10,... | collective-permute-start | bytes 221192 | tf_op jit(solution)/shard_map/ppermute | solution.py:592
  62.4 4.2 %collective-permute-start.22 = (bf16[144,256]{1,0:T(8,128)(2,1)S(1)}, bf16[144,256]{1,0:T(8,128)(2,1)S(1)}, u32[]{:S(2)}, u32[]{:S(2)}) collective-permute-start(bf16[144,256]{1,0:T(8,128)(2,1)S(1)} %get-tuple-element.94), channel_id=1, source_target_pairs={{0,18},{1,19},{2,16},{3,17},{4,22},{5,23},{6,20},{7,21},{8,26},{9,... | collective-permute-start | bytes 221192 | tf_op jit(solution)/shard_map/ppermute | solution.py:592
  65.3 12.0 %collective-permute-start.18 = (bf16[288,256]{1,0:T(8,128)(2,1)S(1)}, bf16[288,256]{1,0:T(8,128)(2,1)S(1)}, u32[]{:S(2)}, u32[]{:S(2)}) collective-permute-start(bf16[288,256]{1,0:T(8,128)(2,1)S(1)} %shard_map.120.refs_0_), channel_id=1, source_target_pairs={{0,8},{1,9},{2,10},{3,11},{4,12},{5,13},{6,14},{7,15},{8,0},{9,1},... | collective-permute-start | bytes 442376 | tf_op jit(solution)/shard_map/ppermute | solution.py:592
  67.2 10.1 %collective-permute-start.25 = (bf16[144,256]{1,0:T(8,128)(2,1)S(1)}, bf16[144,256]{1,0:T(8,128)(2,1)S(1)}, u32[]{:S(2)}, u32[]{:S(2)}) collective-permute-start(bf16[144,256]{1,0:T(8,128)(2,1)S(1)} %get-tuple-element.95.refs_2_), channel_id=1, source_target_pairs={{0,12},{1,13},{2,14},{3,15},{4,8},{5,9},{6,10},{7,11},{8,4},{9,5},... | collective-permute-start | bytes 221192 | tf_op jit(solution)/shard_map/ppermute | solution.py:592
  69.4 10.8 %collective-permute-start.24 = (bf16[144,256]{1,0:T(8,128)(2,1)S(1)}, bf16[144,256]{1,0:T(8,128)(2,1)S(1)}, u32[]{:S(2)}, u32[]{:S(2)}) collective-permute-start(bf16[144,256]{1,0:T(8,128)(2,1)S(1)} %get-tuple-element.95.refs_2_), channel_id=1, source_target_pairs={{0,8},{1,9},{2,10},{3,11},{4,12},{5,13},{6,14},{7,15},{8,0},{9,1},... | collective-permute-start | bytes 221192 | tf_op jit(solution)/shard_map/ppermute | solution.py:592
  69.6 10.6 %collective-permute-start.23 = (bf16[144,256]{1,0:T(8,128)(2,1)S(1)}, bf16[144,256]{1,0:T(8,128)(2,1)S(1)}, u32[]{:S(2)}, u32[]{:S(2)}) collective-permute-start(bf16[144,256]{1,0:T(8,128)(2,1)S(1)} %get-tuple-element.95.refs_2_), channel_id=1, source_target_pairs={{0,4},{1,5},{2,6},{3,7},{4,0},{5,1},{6,2},{7,3},{8,12},{9,13},{10,... | collective-permute-start | bytes 221192 | tf_op jit(solution)/shard_map/ppermute | solution.py:592
  80.2 6.1 %collective-permute-start.28 = (bf16[432,256]{1,0:T(8,128)(2,1)S(1)}, bf16[432,256]{1,0:T(8,128)(2,1)S(1)}, u32[]{:S(2)}, u32[]{:S(2)}) collective-permute-start(bf16[432,256]{1,0:T(8,128)(2,1)S(1)} %shard_map.123.refs_1_), channel_id=1, source_target_pairs={{0,18},{1,19},{2,16},{3,17},{4,22},{5,23},{6,20},{7,21},{8,26},{9,... | collective-permute-start | bytes 663560 | tf_op jit(solution)/shard_map/ppermute | solution.py:592
  81.1 10.3 %collective-permute-start.27 = (bf16[432,256]{1,0:T(8,128)(2,1)S(1)}, bf16[432,256]{1,0:T(8,128)(2,1)S(1)}, u32[]{:S(2)}, u32[]{:S(2)}) collective-permute-start(bf16[432,256]{1,0:T(8,128)(2,1)S(1)} %shard_map.123.refs_1_), channel_id=1, source_target_pairs={{0,16},{1,17},{2,18},{3,19},{4,20},{5,21},{6,22},{7,23},{8,24},{9,... | collective-permute-start | bytes 663560 | tf_op jit(solution)/shard_map/ppermute | solution.py:592
  81.9 11.1 %collective-permute-start.26 = (bf16[432,256]{1,0:T(8,128)(2,1)S(1)}, bf16[432,256]{1,0:T(8,128)(2,1)S(1)}, u32[]{:S(2)}, u32[]{:S(2)}) collective-permute-start(bf16[432,256]{1,0:T(8,128)(2,1)S(1)} %shard_map.123.refs_1_), channel_id=1, source_target_pairs={{0,2},{1,3},{2,0},{3,1},{4,6},{5,7},{6,4},{7,5},{8,10},{9,11},{10,... | collective-permute-start | bytes 663560 | tf_op jit(solution)/shard_map/ppermute | solution.py:592
  83.0 10.8 %collective-permute-start.32 = (bf16[432,256]{1,0:T(8,128)(2,1)S(1)}, bf16[432,256]{1,0:T(8,128)(2,1)S(1)}, u32[]{:S(2)}, u32[]{:S(2)}) collective-permute-start(bf16[432,256]{1,0:T(8,128)(2,1)S(1)} %shard_map.123.refs_1_), channel_id=1, source_target_pairs={{0,1},{1,0},{2,3},{3,2},{4,5},{5,4},{6,7},{7,6},{8,9},{9,8},{10,11... | collective-permute-start | bytes 663560 | tf_op jit(solution)/shard_map/ppermute | solution.py:592
  86.3 9.0 %collective-permute-start.31 = (bf16[432,256]{1,0:T(8,128)(2,1)S(1)}, bf16[432,256]{1,0:T(8,128)(2,1)S(1)}, u32[]{:S(2)}, u32[]{:S(2)}) collective-permute-start(bf16[432,256]{1,0:T(8,128)(2,1)S(1)} %collective-permute-done.28.refs_3_), channel_id=1, source_target_pairs={{0,1},{1,0},{2,3},{3,2},{4,5},{5,4},{6,7},{7,6},{8,9},{9,8},{10,11... | collective-permute-start | bytes 663560 | tf_op jit(solution)/shard_map/ppermute | solution.py:592
  91.4 3.9 %collective-permute-start.30 = (bf16[432,256]{1,0:T(8,128)(2,1)S(1)}, bf16[432,256]{1,0:T(8,128)(2,1)S(1)}, u32[]{:S(2)}, u32[]{:S(2)}) collective-permute-start(bf16[432,256]{1,0:T(8,128)(2,1)S(1)} %collective-permute-done.27.refs_2_), channel_id=1, source_target_pairs={{0,1},{1,0},{2,3},{3,2},{4,5},{5,4},{6,7},{7,6},{8,9},{9,8},{10,11... | collective-permute-start | bytes 663560 | tf_op jit(solution)/shard_map/ppermute | solution.py:592
  (13 other events, 42.0 us)
